TPU v7x, 32 devices: a whole 2x2x4 slice. The times are simulated.
32 devices in a mesh: seq: 8 (over z, y), batch: 4 (over x, core).
Axes of the slice: x: 2, y: 2, z: 4, core: 2. Of those that a mesh axis runs over, the one named last changes fastest.
Arguments:
- inputs: bfloat16 [4, 2048, 1024], P('batch', 'seq'), may hold values from -6 to 6
- domain_ids: int32 [4], P('batch'), may hold values from 0 to 3
- norm1_gain: bfloat16 [1024], P(('seq', 'batch')), may hold values from 0.099609375 to 1.8984375
- w_qkv: bfloat16 [1024, 3072], P(('seq', 'batch')), may hold values from -0.1875 to 0.1875
- w_beta: bfloat16 [1024, 8], P(('seq', 'batch')), may hold values from -0.1875 to 0.1875
- conv_weight: bfloat16 [3072, 4], P(('seq', 'batch')), may hold values from -3 to 3
- domain_bias: bfloat16 [4, 8], replicated, may hold values from -7 to 3
- head_gain: bfloat16 [128], replicated, may hold values from 0.099609375 to 1.8984375
- w_out: bfloat16 [1024, 1024], P(('seq', 'batch')), may hold values from -0.1875 to 0.1875
- norm2_gain: bfloat16 [1024], P(('seq', 'batch')), may hold values from 0.099609375 to 1.8984375
- w_gate_up: bfloat16 [1024, 5632], P(('seq', 'batch')), may hold values from -0.1875 to 0.1875
- w_down: bfloat16 [2816, 1024], P(('seq', 'batch')), may hold values from -0.15625 to 0.15625
- cotangent: bfloat16 [4, 2048, 1024], P('batch', 'seq'), may hold values from -6 to 6
Outputs:
- output: bfloat16 [4, 2048, 1024], P('batch', 'seq')
- grad_input: float32 [4, 2048, 1024], P('batch', 'seq')
- grad_norm1: float32 [1024], P(('seq', 'batch'))
- grad_qkv: float32 [1024, 3072], P(('seq', 'batch'))
- grad_beta: float32 [1024, 8], P(('seq', 'batch'))
- grad_conv: float32 [3072, 4], P(('seq', 'batch'))
- grad_domain_bias: float32 [4, 8], replicated
- grad_head_gain: float32 [128], replicated
- grad_out_proj: float32 [1024, 1024], P(('seq', 'batch'))
- grad_norm2: float32 [1024], P(('seq', 'batch'))
- grad_gate_up: float32 [1024, 5632], P(('seq', 'batch'))
- grad_down: float32 [2816, 1024], P(('seq', 'batch'))
All inputs are finite; a program needn't handle non-finite values.
Results may differ from a plain program's by a relative error of at most 0.02.
Values may be sent and summed in bfloat16 or wider, within the bound.
No kernel may reach another device: no remote copies, remote signals or barrier semaphores. Data moves between devices by JAX's collectives and lax.ppermute only.
A program may use at most 256 MiB of HBM per device.

v0:
```python
import jax
import jax.numpy as jnp
from jax import lax
from jax.sharding import PartitionSpec as P

D = 1024
H = 8
DK = 128
FF = 2816
BLOCK = 64
CONV = 4
NDOM = 4


PRECISE = lax.Precision.HIGHEST
EPS = 1e-06


def shifted(x, axis, by):
    devices = lax.axis_size(axis)
    pairs = [(i, i + by) for i in range(devices) if 0 <= i + by < devices]
    return lax.ppermute(x, axis, pairs)


def prefix_2(x, axis, join, neutral):
    place = lax.axis_index(axis)
    gathered = jax.tree.map(
        lambda a, kind: lax.all_gather(a.astype(kind), axis), x, (jnp.bfloat16, jnp.bfloat16)
    )
    state = jax.tree.map(lambda a, e: jnp.zeros_like(a) + jnp.asarray(e, a.dtype), x, neutral)

    def one(turn, state):
        return join(
            state,
            jax.tree.map(
                lambda a, own: lax.dynamic_index_in_dim(a, turn, 0, False).astype(own.dtype),
                gathered,
                x,
            ),
        )

    return lax.fori_loop(0, place, one, state)


def carried_in(x, axis, combine, identity):
    devices, mine = (lax.axis_size(axis), lax.axis_index(axis))
    everything = jax.tree.map(
        lambda part, kind: lax.all_gather(part.astype(kind), axis),
        x,
        jax.tree.map(lambda a: jnp.bfloat16 if a.dtype == jnp.float32 else a.dtype, x),
    )
    start = jax.tree.map(
        lambda part, zero: jnp.broadcast_to(jnp.asarray(zero, part.dtype), part.shape), x, identity
    )

    def turn(k, before):
        at = devices - 1 - k
        reached = at > mine
        new = combine(
            before, jax.tree.map(lambda part, own: part[at].astype(own.dtype), everything, x)
        )
        return jax.tree.map(lambda a, b: jnp.where(reached, a, b), new, before)

    return lax.fori_loop(0, devices, turn, start)


def rms_scale(values, gain):
    return values * lax.rsqrt(jnp.mean(values * values, axis=-1, keepdims=True) + EPS) * gain


def unit_rows(values):
    return values * lax.rsqrt(jnp.sum(values * values, axis=-1, keepdims=True) + EPS)


def to_low(values):
    return lax.optimization_barrier(values.astype(jnp.bfloat16)).astype(jnp.float32)


def conv_piece(extended, conv_taps):
    out_len = extended.shape[-2] - CONV + 1
    mixed_sum = conv_taps[:, 0] * extended[..., 0:out_len, :]
    for position in range(1, CONV):
        mixed_sum = (
            mixed_sum + conv_taps[:, position] * extended[..., position : position + out_len, :]
        )
    activated = jax.nn.silu(mixed_sum)
    shape_out = activated.shape[:-1] + (H, DK)
    query_part = unit_rows(activated[..., :D].reshape(shape_out)) * DK ** (-0.5)
    key_part = unit_rows(activated[..., D : 2 * D].reshape(shape_out))
    value_part = activated[..., 2 * D :].reshape(shape_out)
    return (query_part, key_part, value_part)


def block_weights(key_rows, value_rows, beta_rates):
    key_inner = jnp.einsum("...cd,...ed->...ce", key_rows, key_rows, precision=PRECISE)
    lower_part = jnp.tril(key_inner * beta_rates[..., :, None], -1)
    system = lower_part + jnp.eye(BLOCK, dtype=jnp.float32)
    right_side = jnp.concatenate([key_rows, value_rows], axis=-1) * beta_rates[..., :, None]
    solved = lax.linalg.triangular_solve(
        system, right_side, left_side=True, lower=True, unit_diagonal=True
    )
    return (solved[..., :DK], solved[..., DK:])


def to_blocks(values):
    seq_count, tokens = (values.shape[0], values.shape[1])
    return values.reshape(seq_count, tokens // BLOCK, BLOCK, H, DK).transpose(0, 3, 1, 2, 4)


def from_blocks(values):
    seq_count, blocks = (values.shape[0], values.shape[2])
    return values.transpose(0, 2, 3, 1, 4).reshape(seq_count, blocks * BLOCK, H, DK)


def first_section(key_rows, value_rows, beta_rates):
    w_factor, u_factor = block_weights(key_rows, value_rows, beta_rates)
    carry_map = jnp.eye(DK, dtype=jnp.float32) - jnp.einsum(
        "...cd,...ce->...de", key_rows, w_factor, precision=PRECISE
    )
    drive = jnp.einsum("...cd,...ce->...de", key_rows, u_factor, precision=PRECISE)
    total_map = carry_map[:, :, 0]
    total_drive = drive[:, :, 0]
    for position in range(1, key_rows.shape[2]):
        total_map = jnp.einsum(
            "...ij,...jk->...ik", carry_map[:, :, position], total_map, precision=PRECISE
        )
        total_drive = (
            jnp.einsum(
                "...ij,...jk->...ik", carry_map[:, :, position], total_drive, precision=PRECISE
            )
            + drive[:, :, position]
        )
    return (w_factor, u_factor, total_map, total_drive)


def second_section(queries, key_rows, w_factor, u_factor, start_state):
    scores = jnp.tril(jnp.einsum("...cd,...ed->...ce", queries, key_rows, precision=PRECISE))
    state_now = start_state
    pieces = []
    count = queries.shape[2]
    for position in range(count):
        fresh_values = u_factor[:, :, position] - jnp.einsum(
            "shcd,shde->shce", w_factor[:, :, position], state_now, precision=PRECISE
        )
        piece_out = jnp.einsum(
            "shcd,shde->shce", queries[:, :, position], state_now, precision=PRECISE
        )
        piece_out = piece_out + jnp.einsum(
            "shce,shef->shcf", scores[:, :, position], fresh_values, precision=PRECISE
        )
        pieces.append(piece_out)
        if position + 1 < count:
            state_now = state_now + jnp.einsum(
                "shcd,shce->shde", key_rows[:, :, position], fresh_values, precision=PRECISE
            )
    return jnp.stack(pieces, axis=2)


def head_piece(block_outs, gain):
    return rms_scale(block_outs, gain).transpose(0, 2, 3, 1, 4).reshape(-1, D)


def swiglu(gate_up):
    return jax.nn.silu(gate_up[:, :FF]) * gate_up[:, FF:]


def compose(early_pair, late_pair):
    early_map, early_drive = early_pair
    late_map, late_drive = late_pair
    joined_map = jnp.einsum("...ij,...jk->...ik", late_map, early_map, precision=PRECISE)
    joined_drive = (
        jnp.einsum("...ij,...jk->...ik", late_map, early_drive, precision=PRECISE) + late_drive
    )
    return (joined_map, joined_drive)


def shards(
    inputs,
    domain_ids,
    norm1_gain,
    w_qkv,
    w_beta,
    conv_weight,
    domain_bias,
    head_gain,
    w_out,
    norm2_gain,
    w_gate_up,
    w_down,
    cotangent,
):
    part_g1, part_qkv, part_beta, part_conv, part_out, part_g2, part_gu, part_down = (
        lax.all_gather(norm1_gain, "batch", axis=0, tiled=True),
        lax.all_gather(w_qkv, "batch", axis=0, tiled=True),
        lax.all_gather(w_beta, "batch", axis=0, tiled=True),
        lax.all_gather(conv_weight, "batch", axis=0, tiled=True),
        lax.all_gather(w_out, "batch", axis=0, tiled=True),
        lax.all_gather(norm2_gain, "batch", axis=0, tiled=True),
        lax.all_gather(w_gate_up, "batch", axis=0, tiled=True),
        lax.all_gather(w_down, "batch", axis=0, tiled=True),
    )
    full_g1, full_qkv, full_beta, full_conv, full_out, full_g2, full_gu, full_down = (
        lax.all_gather(part_g1, "seq", axis=0, tiled=True),
        lax.all_gather(part_qkv, "seq", axis=0, tiled=True),
        lax.all_gather(part_beta, "seq", axis=0, tiled=True),
        lax.all_gather(part_conv, "seq", axis=0, tiled=True),
        lax.all_gather(part_out, "seq", axis=0, tiled=True),
        lax.all_gather(part_g2, "seq", axis=0, tiled=True),
        lax.all_gather(part_gu, "seq", axis=0, tiled=True),
        lax.all_gather(part_down, "seq", axis=0, tiled=True),
    )
    seq_count, tokens = (inputs.shape[0], inputs.shape[1])
    row_count = seq_count * tokens
    gain_one = full_g1.astype(jnp.float32)
    gain_two = full_g2.astype(jnp.float32)
    conv_taps = full_conv.astype(jnp.float32)
    bias_table = domain_bias.astype(jnp.float32)
    head_scale = head_gain.astype(jnp.float32)
    choose = (domain_ids[:, None] == jnp.arange(NDOM, dtype=jnp.int32)[None, :]).astype(jnp.float32)
    input_rows = inputs.astype(jnp.float32)
    normed, norm1_pull = jax.vjp(rms_scale, input_rows, gain_one)
    rows_in = normed.astype(jnp.bfloat16).reshape(row_count, D)
    pre_conv = (
        jnp.dot(rows_in, full_qkv, preferred_element_type=jnp.float32)
        .astype(jnp.bfloat16)
        .reshape(seq_count, tokens, 3 * D)
    )
    tail_rows = shifted(pre_conv[:, tokens - CONV + 1 :, :], "seq", 1)
    extended = jnp.concatenate([tail_rows, pre_conv], axis=1).astype(jnp.float32)
    (query_raw, key_raw, value_raw), conv_pull = jax.vjp(conv_piece, extended, conv_taps)

    def rate_piece(linear, table):
        bias_rows = jnp.dot(choose, table, precision=PRECISE, preferred_element_type=jnp.float32)
        return jax.nn.sigmoid(linear + bias_rows[:, None, :])

    linear_beta = jnp.dot(rows_in, full_beta, preferred_element_type=jnp.float32).reshape(
        seq_count, tokens, H
    )
    beta_rates, rate_pull = jax.vjp(rate_piece, linear_beta, bias_table)
    query_blocks = to_blocks(to_low(query_raw))
    key_blocks = to_blocks(to_low(key_raw))
    value_blocks = to_blocks(to_low(value_raw))
    rate_blocks = beta_rates.reshape(seq_count, tokens // BLOCK, BLOCK, H).transpose(0, 3, 1, 2)
    (w_factor, u_factor, total_map, total_drive), first_pull = jax.vjp(
        first_section, key_blocks, value_blocks, rate_blocks
    )
    identity_pair = (
        jnp.broadcast_to(jnp.eye(DK, dtype=jnp.float32), total_map.shape),
        jnp.zeros_like(total_drive),
    )
    prefix = prefix_2((total_map, total_drive), "seq", compose, identity_pair)
    start_state = prefix[1]
    mixed_out, second_pull = jax.vjp(
        second_section, query_blocks, key_blocks, w_factor, u_factor, start_state
    )
    heads_f, head_pull = jax.vjp(head_piece, mixed_out, head_scale)
    heads_rows = heads_f.astype(jnp.bfloat16)
    middle = input_rows.reshape(row_count, D) + jnp.dot(
        heads_rows, full_out, preferred_element_type=jnp.float32
    )
    normed_two, norm2_pull = jax.vjp(rms_scale, middle, gain_two)
    rows_two = normed_two.astype(jnp.bfloat16)
    gate_up = jnp.dot(rows_two, full_gu, preferred_element_type=jnp.float32)
    hidden_f, ffn_pull = jax.vjp(swiglu, gate_up)
    hidden = hidden_f.astype(jnp.bfloat16)
    result_rows = middle + jnp.dot(hidden, full_down, preferred_element_type=jnp.float32)
    output = result_rows.astype(jnp.bfloat16).reshape(seq_count, tokens, D)
    grad_rows = cotangent.reshape(row_count, D)
    grad_down = jnp.einsum("nf,nd->fd", hidden, grad_rows, preferred_element_type=jnp.float32)
    hidden_grad = jnp.einsum("nd,fd->nf", grad_rows, full_down, preferred_element_type=jnp.float32)
    (gate_up_grad,) = ffn_pull(hidden_grad)
    gate_up_low = gate_up_grad.astype(jnp.bfloat16)
    grad_gate_up = jnp.einsum(
        "nd,nf->df", rows_two, gate_up_low, preferred_element_type=jnp.float32
    )
    normed_two_grad = jnp.einsum(
        "nf,df->nd", gate_up_low, full_gu, preferred_element_type=jnp.float32
    )
    middle_part, grad_norm2 = norm2_pull(normed_two_grad)
    middle_grad = grad_rows.astype(jnp.float32) + middle_part
    middle_low = middle_grad.astype(jnp.bfloat16)
    grad_out_proj = jnp.einsum(
        "nd,ne->de", heads_rows, middle_low, preferred_element_type=jnp.float32
    )
    heads_grad = jnp.einsum("ne,de->nd", middle_low, full_out, preferred_element_type=jnp.float32)
    mixed_grad, grad_head_gain = head_pull(heads_grad)
    query_grad, key_grad_two, w_grad, u_grad, start_grad = second_pull(mixed_grad)
    adjoint = carried_in(
        (jnp.swapaxes(total_map, -1, -2), start_grad), "seq", compose, identity_pair
    )
    adjoint_next = adjoint[1]
    map_grad = jnp.einsum("...de,...fe->...df", adjoint_next, start_state, precision=PRECISE)
    key_grad_one, value_grad, rate_grad = first_pull((w_grad, u_grad, map_grad, adjoint_next))
    key_grad = key_grad_one + key_grad_two
    rate_tokens = rate_grad.transpose(0, 2, 3, 1).reshape(seq_count, tokens, H)
    extended_grad, grad_conv = conv_pull(
        (from_blocks(query_grad), from_blocks(key_grad), from_blocks(value_grad))
    )
    sent_back = shifted(extended_grad[:, : CONV - 1, :].astype(jnp.bfloat16), "seq", -1).astype(
        jnp.float32
    )
    pre_grad = extended_grad[:, CONV - 1 :, :] + jnp.pad(
        sent_back, ((0, 0), (tokens - CONV + 1, 0), (0, 0))
    )
    pre_low = pre_grad.astype(jnp.bfloat16).reshape(row_count, 3 * D)
    linear_grad, grad_domain_bias = rate_pull(rate_tokens)
    linear_low = linear_grad.astype(jnp.bfloat16).reshape(row_count, H)
    grad_qkv = jnp.einsum("nd,nf->df", rows_in, pre_low, preferred_element_type=jnp.float32)
    grad_beta = jnp.einsum("nd,nh->dh", rows_in, linear_low, preferred_element_type=jnp.float32)
    normed_grad = jnp.einsum("nf,df->nd", pre_low, full_qkv, preferred_element_type=jnp.float32)
    normed_grad = normed_grad + jnp.einsum(
        "nh,dh->nd", linear_low, full_beta, preferred_element_type=jnp.float32
    )
    input_part, grad_norm1 = norm1_pull(normed_grad.reshape(seq_count, tokens, D))
    grad_input = middle_grad.reshape(seq_count, tokens, D) + input_part
    sum_g1, sum_qkv, sum_beta, sum_conv, sum_out, sum_g2, sum_gu, sum_down = (
        lax.psum_scatter(
            grad_norm1.astype(jnp.bfloat16), "seq", scatter_dimension=0, tiled=True
        ).astype(jnp.float32),
        lax.psum_scatter(
            grad_qkv.astype(jnp.bfloat16), "seq", scatter_dimension=0, tiled=True
        ).astype(jnp.float32),
        lax.psum_scatter(
            grad_beta.astype(jnp.bfloat16), "seq", scatter_dimension=0, tiled=True
        ).astype(jnp.float32),
        lax.psum_scatter(
            grad_conv.astype(jnp.bfloat16), "seq", scatter_dimension=0, tiled=True
        ).astype(jnp.float32),
        lax.psum_scatter(
            grad_out_proj.astype(jnp.bfloat16), "seq", scatter_dimension=0, tiled=True
        ).astype(jnp.float32),
        lax.psum_scatter(
            grad_norm2.astype(jnp.bfloat16), "seq", scatter_dimension=0, tiled=True
        ).astype(jnp.float32),
        lax.psum_scatter(
            grad_gate_up.astype(jnp.bfloat16), "seq", scatter_dimension=0, tiled=True
        ).astype(jnp.float32),
        lax.psum_scatter(
            grad_down.astype(jnp.bfloat16), "seq", scatter_dimension=0, tiled=True
        ).astype(jnp.float32),
    )
    own_g1, own_qkv, own_beta, own_conv, own_out, own_g2, own_gu, own_down = (
        lax.psum_scatter(
            sum_g1.astype(jnp.bfloat16), "batch", scatter_dimension=0, tiled=True
        ).astype(jnp.float32),
        lax.psum_scatter(
            sum_qkv.astype(jnp.bfloat16), "batch", scatter_dimension=0, tiled=True
        ).astype(jnp.float32),
        lax.psum_scatter(
            sum_beta.astype(jnp.bfloat16), "batch", scatter_dimension=0, tiled=True
        ).astype(jnp.float32),
        lax.psum_scatter(
            sum_conv.astype(jnp.bfloat16), "batch", scatter_dimension=0, tiled=True
        ).astype(jnp.float32),
        lax.psum_scatter(
            sum_out.astype(jnp.bfloat16), "batch", scatter_dimension=0, tiled=True
        ).astype(jnp.float32),
        lax.psum_scatter(
            sum_g2.astype(jnp.bfloat16), "batch", scatter_dimension=0, tiled=True
        ).astype(jnp.float32),
        lax.psum_scatter(
            sum_gu.astype(jnp.bfloat16), "batch", scatter_dimension=0, tiled=True
        ).astype(jnp.float32),
        lax.psum_scatter(
            sum_down.astype(jnp.bfloat16), "batch", scatter_dimension=0, tiled=True
        ).astype(jnp.float32),
    )
    bias_total, gain_total = lax.psum((grad_domain_bias, grad_head_gain), ("seq", "batch"))
    return (
        output,
        grad_input,
        own_g1,
        own_qkv,
        own_beta,
        own_conv,
        bias_total,
        gain_total,
        own_out,
        own_g2,
        own_gu,
        own_down,
    )


def solution(mesh):
    placed = (
        P("batch", "seq", None),
        P("batch"),
        P(("seq", "batch")),
        P(("seq", "batch"), None),
        P(("seq", "batch"), None),
        P(("seq", "batch"), None),
        P(),
        P(),
        P(("seq", "batch"), None),
        P(("seq", "batch")),
        P(("seq", "batch"), None),
        P(("seq", "batch"), None),
        P("batch", "seq", None),
    )
    return jax.shard_map(
        shards,
        mesh=mesh,
        in_specs=placed,
        out_specs=(
            P("batch", "seq", None),
            P("batch", "seq", None),
            P(("seq", "batch")),
            P(("seq", "batch"), None),
            P(("seq", "batch"), None),
            P(("seq", "batch"), None),
            P(),
            P(),
            P(("seq", "batch"), None),
            P(("seq", "batch")),
            P(("seq", "batch"), None),
            P(("seq", "batch"), None),
        ),
        check_vma=False,
    )
```

profile of v0, /device:TPU:0, one launch (start us, length us, event | category | flops | bytes accessed | tf_op | source)
XLA Modules:
  0.0 1704.8 jit_solution(12974857980447764156)
XLA Ops:
  7.3 11.8 all_gather.76
  27.7 21.2 %all-gather.5 = bf16[8,1,128]{2,1,0:T(2,128)(2,1)S(1)} all-gather(bf16[1,1,128]{2,1,0:T(2,128)(2,1)S(1)} %bitcast.904), channel_id=1, replica_groups=mesh['seq'=8,'batch'=4] {'seq'}, dimensions={0}, use_global_device_ids=true | all-gather | bytes 2304 | tf_op jit(solution)/shard_map/all_gather | solution.py:203
  54.8 30.9 %all_gather.73 = bf16[3072,4]{0,1:T(4,128)(2,1)S(1)} all-gather(bf16[384,4]{0,1:T(4,128)(2,1)S(1)} %reshape.1466), channel_id=1, replica_groups=mesh['seq'=8,'batch'=4] {'seq'}, dimensions={0}, use_global_device_ids=true | all-gather | bytes 27648 | tf_op jit(solution)/shard_map/all_gather | solution.py:206
  91.2 26.2 %all_gather.79 = bf16[1024,8]{0,1:T(8,128)(2,1)S(1)} all-gather(bf16[128,8]{0,1:T(8,128)(2,1)S(1)} %reshape.1470), channel_id=1, replica_groups=mesh['seq'=8,'batch'=4] {'seq'}, dimensions={0}, use_global_device_ids=true | all-gather | bytes 18432 | tf_op jit(solution)/shard_map/all_gather | solution.py:205
  140.6 158.7 %custom-call.7 = f32[1,8,4,1,64,64]{4,5,3,2,1,0:T(8,128)} custom-call(f32[1,8,4,1,64,64]{5,4,3,2,1,0:T(8,128)} %add_bitcast_fusion.1), custom_call_target="InvertDiagBlocksLowerTriangular" | custom-call | tf_op jit(solution)/shard_map/jvp()/triangular_solve | solution.py:99
  332.7 19.4 %all-gather.7 = bf16[8,1,128]{2,1,0:T(2,128)(2,1)S(1)} all-gather(bf16[1,1,128]{2,1,0:T(2,128)(2,1)S(1)} %bitcast.903), channel_id=1, replica_groups=mesh['seq'=8,'batch'=4] {'seq'}, dimensions={0}, use_global_device_ids=true | all-gather | bytes 2304 | tf_op jit(solution)/shard_map/all_gather | solution.py:208
  360.1 49.3 %all-gather.30.cloned.1.call-done = bf16[64,128,128]{2,1,0:T(8,128)(2,1)} async-done(((bf16[8,128,128]{2,1,0:T(8,128)(2,1)}), bf16[64,128,128]{2,1,0:T(8,128)(2,1)}) %all-gather.30.cloned.1.call-update) | async-done | bytes 2097168 | tf_op jit(solution)/shard_map/all_gather | solution.py:28
  426.1 33.1 %all-gather.20.cloned.1.call-done = bf16[1024,1024]{1,0:T(8,128)(2,1)} async-done(((bf16[128,1024]{1,0:T(8,128)(2,1)}), bf16[1024,1024]{1,0:T(8,128)(2,1)}) %all-gather.20.cloned.1.call-update) | async-done | bytes 2097168 | tf_op jit(solution)/shard_map/all_gather | solution.py:207
  463.9 159.5 %all-gather.24.cloned.1.call-done = bf16[1024,5632]{1,0:T(8,128)(2,1)} async-done(((bf16[128,5632]{1,0:T(8,128)(2,1)}), bf16[1024,5632]{1,0:T(8,128)(2,1)}) %all-gather.24.cloned.1.call-update) | async-done | bytes 11534352 | tf_op jit(solution)/shard_map/all_gather | solution.py:209
  623.4 10.3 fusion.216
  633.7 82.7 %all-gather.26.cloned.1.call-done = bf16[2816,1024]{1,0:T(8,128)(2,1)} async-done(((bf16[352,1024]{1,0:T(8,128)(2,1)}), bf16[2816,1024]{1,0:T(8,128)(2,1)}) %all-gather.26.cloned.1.call-update) | async-done | bytes 5767184 | tf_op jit(solution)/shard_map/all_gather | solution.py:210
  726.1 11.0 multiply_reduce_fusion.4
  805.0 11.0 all-gather.34.cloned.1.call-done
  816.1 36.7 %while.29 = (s32[]{:T(128)}, f32[1,8,128,128]{3,2,1,0:T(8,128)}, s32[]{:T(128)}, bf16[8,1,8,128,128]{4,3,2,1,0:T(8,128)(2,1)}, bf16[8,1,8,128,128]{4,3,2,1,0:T(8...) while((s32[]{:T(128)}, f32[1,8,128,128]{3,2,1,0:T(8,128)}, s32[]{:T(128)}, ...), condition=%wide.region_10.11_spmd.clone, body=%wide.region_9.10_spmd.clone.sunk | while | flops 201981952 | bytes 3148453 | solution.py:64
  967.1 15.8 reduce-scatter.37.cloned.1.call-done
  982.9 65.3 %reduce-scatter.41.cloned.1.call-done = bf16[384,4]{1,0:T(8,128)(2,1)} async-done(((bf16[3072,4]{1,0:T(8,128)(2,1)}), bf16[384,4]{1,0:T(8,128)(2,1)}) %reduce-scatter.41.cloned.1.call-update) | async-done | bytes 3088
  1048.3 70.5 %reduce-scatter.25.cloned.1.call-done = bf16[128,1024]{1,0:T(8,128)(2,1)} async-done(((bf16[1024,1024]{1,0:T(8,128)(2,1)}), bf16[128,1024]{1,0:T(8,128)(2,1)}) %reduce-scatter.25.cloned.1.call-update) | async-done | bytes 262160 | tf_op jit(solution)/shard_map/reduce_scatter | solution.py:329
  1118.9 113.0 %reduce-scatter.33.cloned.1.call-done = bf16[352,1024]{1,0:T(8,128)(2,1)} async-done(((bf16[2816,1024]{1,0:T(8,128)(2,1)}), bf16[352,1024]{1,0:T(8,128)(2,1)}) %reduce-scatter.33.cloned.1.call-update) | async-done | bytes 720912 | tf_op jit(solution)/shard_map/reduce_scatter | solution.py:338
  1232.0 121.6 %reduce-scatter.21.cloned.1.call-done = bf16[128,3072]{1,0:T(8,128)(2,1)} async-done(((bf16[1024,3072]{1,0:T(8,128)(2,1)}), bf16[128,3072]{1,0:T(8,128)(2,1)}) %reduce-scatter.21.cloned.1.call-update) | async-done | bytes 786448 | tf_op jit(solution)/shard_map/reduce_scatter | solution.py:320
  1353.7 195.7 %reduce-scatter.29.cloned.1.call-done = bf16[128,5632]{1,0:T(8,128)(2,1)} async-done(((bf16[1024,5632]{1,0:T(8,128)(2,1)}), bf16[128,5632]{1,0:T(8,128)(2,1)}) %reduce-scatter.29.cloned.1.call-update) | async-done | bytes 1441808 | tf_op jit(solution)/shard_map/reduce_scatter | solution.py:335
  1556.9 39.3 %all-reduce.52 = (f32[4,8]{1,0:T(4,128)}, f32[128]{0:T(128)}) all-reduce(f32[4,8]{1,0:T(4,128)S(1)} %broadcast_multiply_fusion.7, f32[128]{0:T(128)S(1)} %copy-done.170), channel_id=1, replica_groups=mesh['seq'=8,'batch'=4] {'seq','batch'}, use_global_device_ids=true, to_apply=%region_30.31 | all-reduce | flops 160 | bytes 1280 | tf_op jit(solution)/shard_map/psum | solution.py:368
  1603.4 21.3 %all-reduce.53 = (bf16[1024]{0:T(1024)(128)(2,1)S(1)}, bf16[1024]{0:T(1024)(128)(2,1)S(1)}) all-reduce(bf16[1024]{0:T(1024)(128)(2,1)S(1)} %get-tuple-element.256, bf16[1024]{0:T(1024)(128)(2,1)S(1)} %copy-done.169), channel_id=6, replica_groups=mesh['seq'=8,'batch'=4] {'seq'}, use_global_device_ids=true, to_apply=%region_17.18.clone | all-reduce | flops 2048 | bytes 8192
  1641.8 24.0 %reduce-scatter.23.cloned.1.call-done = bf16[32,3072]{1,0:T(8,128)(2,1)} async-done(((bf16[128,3072]{1,0:T(8,128)(2,1)}), bf16[32,3072]{1,0:T(8,128)(2,1)}) %reduce-scatter.23.cloned.1.call-update) | async-done | bytes 196624 | tf_op jit(solution)/shard_map/reduce_scatter | solution.py:346
  1667.5 28.4 %reduce-scatter.31.cloned.1.call-done = bf16[32,5632]{1,0:T(8,128)(2,1)} async-done(((bf16[128,5632]{1,0:T(8,128)(2,1)}), bf16[32,5632]{1,0:T(8,128)(2,1)}) %reduce-scatter.31.cloned.1.call-update) | async-done | bytes 360464 | tf_op jit(solution)/shard_map/reduce_scatter | solution.py:361
  (629 shorter events, 365.1 us)
Async XLA Ops:
  7.3 111.8 %all-gather.18.cloned.1.call-start = ((), (), s32[]{:S(2)}) async-start(), calls=%async_computation.12 | async-start | bytes 7077888 | tf_op jit(solution)/shard_map/all_gather | solution.py:204
  19.1 303.6 %all-gather.22.cloned.1.call-start = ((), (), s32[]{:S(2)}) async-start(), calls=%async_computation.14 | async-start | bytes 1802240 | tf_op jit(solution)/shard_map/all_gather | solution.py:199
  19.9 340.3 %all-gather.28.cloned.1.call-start = ((), (), s32[]{:S(2)}) async-start(), calls=%async_computation.25 | async-start | bytes 2359296 | tf_op jit(solution)/shard_map/all_gather | solution.py:28
  123.8 4.3 collective-permute-start
  309.0 100.4 %all-gather.30.cloned.1.call-start = ((), (), s32[]{:S(2)}) async-start(), calls=%async_computation.26 | async-start | bytes 2359296 | tf_op jit(solution)/shard_map/all_gather | solution.py:28
  316.3 142.9 %all-gather.20.cloned.1.call-start = ((), (), s32[]{:S(2)}) async-start(), calls=%async_computation.13 | async-start | bytes 2359296 | tf_op jit(solution)/shard_map/all_gather | solution.py:207
  322.6 300.8 %all-gather.24.cloned.1.call-start = ((), (), s32[]{:S(2)}) async-start(), calls=%async_computation.15 | async-start | bytes 12976128 | tf_op jit(solution)/shard_map/all_gather | solution.py:209
  323.2 393.2 %all-gather.26.cloned.1.call-start = ((), (), s32[]{:S(2)}) async-start(), calls=%async_computation.16 | async-start | bytes 6488064 | tf_op jit(solution)/shard_map/all_gather | solution.py:210
  332.1 472.9 %all-gather.32.cloned.1.call-start = ((), (), s32[]{:S(2)}) async-start(), calls=%async_computation.27 | async-start | bytes 2359296 | tf_op jit(solution)/shard_map/all_gather | solution.py:48
  360.1 456.0 %all-gather.34.cloned.1.call-start = ((), (), s32[]{:S(2)}) async-start(), calls=%async_computation.28 | async-start | bytes 2359296 | tf_op jit(solution)/shard_map/all_gather | solution.py:48
  757.1 225.7 %reduce-scatter.37.cloned.1.call-start = ((), (), s32[]{:S(2)}) async-start(), calls=%async_computation.29 | async-start | bytes 294912
  923.0 125.3 %reduce-scatter.41.cloned.1.call-start = ((), (), s32[]{:S(2)}) async-start(), calls=%async_computation.31 | async-start | bytes 884736
  932.7 186.1 %reduce-scatter.25.cloned.1.call-start = ((), (), s32[]{:S(2)}) async-start(), calls=%async_computation.19 | async-start | bytes 2359296 | tf_op jit(solution)/shard_map/reduce_scatter | solution.py:329
  936.1 295.9 %reduce-scatter.33.cloned.1.call-start = ((), (), s32[]{:S(2)}) async-start(), calls=%async_computation.23 | async-start | bytes 6488064 | tf_op jit(solution)/shard_map/reduce_scatter | solution.py:338
  940.4 413.2 %reduce-scatter.21.cloned.1.call-start = ((), (), s32[]{:S(2)}) async-start(), calls=%async_computation.17 | async-start | bytes 7077888 | tf_op jit(solution)/shard_map/reduce_scatter | solution.py:320
  946.3 5.7 collective-permute-start.1
  956.7 592.7 %reduce-scatter.29.cloned.1.call-start = ((), (), s32[]{:S(2)}) async-start(), calls=%async_computation.21 | async-start | bytes 12976128 | tf_op jit(solution)/shard_map/reduce_scatter | solution.py:335
  967.0 582.4 %copy-start.175 = (u32[32]{0:T(128)S(1)}, u32[32]{0:T(128)}, u32[]{:S(2)}) copy-start(u32[32]{0:T(128)} %constant.233) | copy-start | bytes 388
  967.0 667.5 %reduce-scatter.39.cloned.1.call-start = ((), (), s32[]{:S(2)}) async-start(), calls=%async_computation.30 | async-start | bytes 40960
  982.9 653.0 %reduce-scatter.43.cloned.1.call-start = ((), (), s32[]{:S(2)}) async-start(), calls=%async_computation.32 | async-start | bytes 122880
  1048.3 589.0 %reduce-scatter.27.cloned.1.call-start = ((), (), s32[]{:S(2)}) async-start(), calls=%async_computation.20 | async-start | bytes 327680 | tf_op jit(solution)/shard_map/reduce_scatter | solution.py:355
  1118.9 521.2 %reduce-scatter.35.cloned.1.call-start = ((), (), s32[]{:S(2)}) async-start(), calls=%async_computation.24 | async-start | bytes 901120 | tf_op jit(solution)/shard_map/reduce_scatter | solution.py:364
  1232.0 433.8 %reduce-scatter.23.cloned.1.call-start = ((), (), s32[]{:S(2)}) async-start(), calls=%async_computation.18 | async-start | bytes 983040 | tf_op jit(solution)/shard_map/reduce_scatter | solution.py:346
  1353.6 342.2 %reduce-scatter.31.cloned.1.call-start = ((), (), s32[]{:S(2)}) async-start(), calls=%async_computation.22 | async-start | bytes 1802240 | tf_op jit(solution)/shard_map/reduce_scatter | solution.py:361
  (175 other events, 1494.2 us)
Sparse Core Ops, SparseCore 0:
  19.2 99.7 all-gather.17
  120.6 17.4 all-gather.21
  309.1 49.8 all-gather.27
  361.6 47.7 all-gather.29
  411.4 47.7 all-gather.19
  461.2 162.1 all-gather.23
  625.6 90.8 all-gather.25
  718.6 47.5 all-gather.31
  768.2 47.7 all-gather.33
  923.1 59.6 reduce-scatter.36
  986.7 61.4 reduce-scatter.40
  1052.0 66.7 reduce-scatter.24
  1122.9 108.9 reduce-scatter.32
  1235.8 117.7 reduce-scatter.20
  1357.5 191.8 reduce-scatter.28
  1551.8 18.4 reduce-scatter.38
  1572.5 19.5 reduce-scatter.42
  1594.4 20.0 reduce-scatter.26
  1617.2 22.8 reduce-scatter.34
  1642.5 23.2 reduce-scatter.22
  1668.5 27.3 reduce-scatter.30
where the time goes:
time: 1710 us; the launch traced here: 1700 us
  waiting for transfers between devices  979 us (57%)
  blocking collectives  207 us (12%)
  matrix products  207 us (12%)
  other arithmetic  200 us (12%)
  local copies, waits for them, and re-layouts  85.2 us (5%)
  between operations  19.7 us (1%)
    reduce_scatter x1, waiting for transfers between devices, shards(): lax.psum_scatter(grad_gate_up.astype(jnp.bfloat16), 'seq', scatter_dimens...  196 us
    another operation x5, other arithmetic, block_weights(): lax.linalg.triangular_solve(system, right_side, left_side=True, lower=Tru...  160 us
    all_gather x1, waiting for transfers between devices, shards(): lax.all_gather(part_gu, 'seq', axis=0, tiled=True)  159 us
    reduce_scatter x1, waiting for transfers between devices, shards(): lax.psum_scatter(grad_qkv.astype(jnp.bfloat16), 'seq', scatter_dimension=...  122 us
    reduce_scatter x1, waiting for transfers between devices, shards(): lax.psum_scatter(grad_down.astype(jnp.bfloat16), 'seq', scatter_dimension...  113 us
    all_gather x1, waiting for transfers between devices, shards(): lax.all_gather(part_down, 'seq', axis=0, tiled=True)  82.7 us
    unnamed x25, waiting for transfers between devices  82.6 us
    reduce_scatter x1, waiting for transfers between devices, shards(): lax.psum_scatter(grad_out_proj.astype(jnp.bfloat16), 'seq', scatter_dimen...  70.5 us
  transfers between devices with their start and end apart: 23, of which 17 were waited for; matrix products, arithmetic and copies ran while one was open for 22% of the time, Pallas kernels for 0%

commit v1 on v0

v1 whole, which is shorter than its diff:
```python
import functools

import jax
import jax.numpy as jnp
from jax import lax
from jax.experimental import pallas as pl
from jax.experimental.pallas import tpu as pltpu
from jax.sharding import Mesh
from jax.sharding import PartitionSpec as P

D = 1024
H = 8
DK = 128
FF = 2816
CONV = 4
NDOM = 4
EPS = 1e-06
HALO = 16
F32 = jnp.float32
BF16 = jnp.bfloat16
SEQ = ("z", "y")
ALL = ("z", "y", "x", "core")
VMEM_LIMIT = 48 * 1024 * 1024


def swap(a):
    return lax.ppermute(a, "core", [(0, 1), (1, 0)])


def turned(a, axis, by):
    n = lax.axis_size(axis)
    return lax.ppermute(a, axis, [(i, (i + by) % n) for i in range(n)])


def gather_axis(a, axis, dim):
    n, me = lax.axis_size(axis), lax.axis_index(axis)
    if n == 1:
        return jnp.expand_dims(a, dim)
    got = [turned(a, axis, k) for k in range(1, n)]
    if n == 2:
        first = me == 0
        return jnp.stack([jnp.where(first, a, got[0]), jnp.where(first, got[0], a)], axis=dim)
    back = got[::-1] + [a]
    return lax.dynamic_slice_in_dim(jnp.stack(back + back, axis=dim), n - 1 - me, n, axis=dim)


def scatter_axis(a, axis, dim):
    n, me = lax.axis_size(axis), lax.axis_index(axis)
    total = lax.dynamic_index_in_dim(a, me, dim, False).astype(F32)
    sent = []
    for k in range(1, n):
        part = lax.dynamic_index_in_dim(a, (me + k) % n, dim, False).astype(BF16)
        sent.append(turned(part, axis, k))
    for part in sent:
        total = total + part.astype(F32)
    return total


def gather_chips(pair):
    flat = gather_axis(pair, "z", 0)
    one = gather_axis(gather_axis(flat[:, 0], "x", 1), "y", 1)
    two = gather_axis(gather_axis(flat[:, 1], "y", 1), "x", 2)
    n = pair.shape[-1]
    return one.reshape(-1, n), two.reshape(-1, n)


def scatter_chips(one, two):
    nz, ny, nx = (lax.axis_size(a) for a in ("z", "y", "x"))
    n = one.shape[-1]
    one = one.reshape(nz, ny, nx, -1, n)
    two = two.reshape(nz, ny, nx, -1, n)
    one = scatter_axis(one, "y", 1).astype(BF16)
    two = scatter_axis(two, "x", 2).astype(BF16)
    one = scatter_axis(one, "x", 1).astype(BF16)
    two = scatter_axis(two, "y", 1).astype(BF16)
    return scatter_axis(jnp.stack([one, two], axis=1), "z", 0)


def core_pick(a, core):
    return (
        lax.dynamic_index_in_dim(a, core, 0, False),
        lax.dynamic_index_in_dim(a, 1 - core, 0, False),
    )


def chip_rows(by_core, core):
    mine, other = core_pick(by_core, core)
    got = swap(other)
    first = core == 0
    return jnp.concatenate(
        [jnp.where(first, mine, got), jnp.where(first, got, mine)], axis=-2
    )


def own_rows(total, core):
    k, both, n = total.shape
    parts = total.reshape(k, 2, both // 2, n).transpose(1, 0, 2, 3)
    mine, other = core_pick(parts, core)
    got = swap(other)
    first = core == 0
    return jnp.stack([jnp.where(first, mine, got), jnp.where(first, got, mine)], axis=0)


def reduce_small(a):
    a = a + swap(a)
    for axis in ("x", "y", "z"):
        every = gather_axis(a, axis, 0)
        total = every[0]
        for k in range(1, every.shape[0]):
            total = total + every[k]
        a = total
    return a


def dot1(a, b, dims=((1,), (0,))):
    return lax.dot_general(
        a.astype(BF16), b.astype(BF16), (dims, ((), ())), preferred_element_type=F32
    )


TN = ((0,), (0,))
NT = ((1,), (1,))


def split(a):
    high = a.astype(BF16)
    return high, (a - high.astype(F32)).astype(BF16)


def dot3(a, b):
    ah, al = split(a)
    bh, bl = split(b)
    return dot1(ah, bh) + (dot1(ah, bl) + dot1(al, bh))


def sigmoid(v):
    return 1.0 / (1.0 + jnp.exp(-v))


def grid_masks(n):
    i = lax.broadcasted_iota(jnp.int32, (n, n), 0)
    j = lax.broadcasted_iota(jnp.int32, (n, n), 1)
    return i, j


def unit_inverse(lower, i, j):
    n = lower.shape[0]
    level = jnp.where(i > j, i ^ j, 0)
    eye = jnp.where(i == j, 1.0, 0.0).astype(F32)
    inverse = eye - jnp.where(level == 1, lower, 0.0)
    size = 2
    while size < n:
        corner = jnp.where((level >= size) & (level < 2 * size), lower, 0.0).astype(BF16)
        low = inverse.astype(BF16)
        inverse = inverse - dot1(low, dot1(corner, low))
        size *= 2
    rest = eye - inverse - dot3(lower, inverse)
    return inverse + dot1(inverse, rest)


def conv_of(ext, taps, rows):
    total = taps[0:1, :] * ext[HALO - 3 : HALO - 3 + rows]
    for i in range(1, CONV):
        total = total + taps[i : i + 1, :] * ext[HALO - 3 + i : HALO - 3 + i + rows]
    return total


def first_kernel(x_ref, g_ref, w_ref, wb_ref, cv_ref, bias_ref, n_ref, pre_ref, qkv_ref, t_ref, wu_ref, pd_ref, b_ref):
    rows = qkv_ref.shape[1] // 2
    frame = rows + HALO

    @pl.when(pl.program_id(0) == 0)
    def _():
        x = x_ref[...].astype(F32)
        scale = lax.rsqrt(jnp.mean(x * x, axis=-1, keepdims=True) + EPS)
        n_ref[...] = (x * scale * g_ref[...]).astype(BF16)

    normed = n_ref[...]
    pre = dot1(normed, w_ref[0]).astype(BF16)
    pre_ref[0] = pre
    linear = dot1(normed, wb_ref[0])
    i, j = grid_masks(rows)
    for q in range(2):
        rate = sigmoid(linear[q * frame + HALO : (q + 1) * frame] + bias_ref[0, q : q + 1, :])
        b_ref[0, q * rows : (q + 1) * rows, :] = rate
        ext = pre[q * frame : (q + 1) * frame].astype(F32)
        conv = conv_of(ext, cv_ref[0], rows)
        act = conv * sigmoid(conv)
        for h in range(2):
            place = pl.ds(q * rows, rows)
            parts = []
            for kind in range(3):
                lane = (kind * 2 + h) * DK
                one = act[:, lane : lane + DK]
                if kind < 2:
                    one = one * lax.rsqrt(jnp.sum(one * one, axis=-1, keepdims=True) + EPS)
                if kind == 0:
                    one = one * DK ** (-0.5)
                one = one.astype(BF16)
                qkv_ref[0, place, lane : lane + DK] = one
                parts.append(one)
            key, value = parts[1], parts[2]
            col = rate[:, h : h + 1]
            lower = jnp.where(i > j, dot1(key, key, NT) * col, 0.0)
            inverse = unit_inverse(lower, i, j)
            right = jnp.concatenate([key, value], axis=1).astype(F32) * col
            both = dot3(inverse, right)
            p = q * 2 + h
            t_ref[0, p] = inverse.astype(BF16)
            wu_ref[0, p] = both.astype(BF16)
            pd_ref[0, p] = dot1(key, both, TN).astype(BF16)


def state_kernel(pd_ref, s_ref):
    count = pd_ref.shape[0]
    state = jnp.zeros((DK, DK), F32)
    for s in range(count):
        s_ref[s] = state.astype(BF16)
        if s + 1 < count:
            high, low = split(state)
            move = pd_ref[s, :, :DK]
            state = state - (dot1(move, high) + dot1(move, low)) + pd_ref[s, :, DK:].astype(F32)


def adjoint_kernel(pd_ref, g_ref, l_ref):
    count = pd_ref.shape[0]
    adjoint = jnp.zeros((DK, DK), F32)
    for s in range(count - 1, -1, -1):
        l_ref[s] = adjoint.astype(BF16)
        if s > 0:
            high, low = split(adjoint)
            move = pd_ref[s, :, :DK]
            adjoint = (
                adjoint - (dot1(move, high, TN) + dot1(move, low, TN)) + g_ref[s].astype(F32)
            )


def second_kernel(qkv_ref, wu_ref, s_ref, hg_ref, f_ref, m_ref, h_ref):
    rows = qkv_ref.shape[1] // 2
    i, j = grid_masks(rows)
    for q in range(2):
        place = pl.ds(q * rows, rows)
        for h in range(2):
            p = q * 2 + h
            lanes = pl.ds(h * DK, DK)
            query = qkv_ref[0, place, pl.ds(h * DK, DK)]
            key = qkv_ref[0, place, pl.ds((2 + h) * DK, DK)]
            state = s_ref[p]
            fresh = wu_ref[0, p, :, DK:].astype(F32) - dot1(wu_ref[0, p, :, :DK], state)
            scores = jnp.where(i >= j, dot1(query, key, NT), 0.0)
            mixed = dot1(query, state) + dot1(scores, fresh)
            scale = lax.rsqrt(jnp.mean(mixed * mixed, axis=-1, keepdims=True) + EPS)
            f_ref[place, lanes] = fresh.astype(BF16)
            m_ref[place, lanes] = mixed
            h_ref[place, lanes] = (mixed * scale * hg_ref[...]).astype(BF16)


def third_kernel(qkv_ref, wu_ref, s_ref, f_ref, m_ref, dh_ref, hg_ref, sg_ref, gf_ref, gq_ref, gk_ref, ghg_ref):
    rows = qkv_ref.shape[1] // 2
    i, j = grid_masks(rows)
    gain = hg_ref[...]
    gain_grad = jnp.zeros((1, DK), F32)
    for q in range(2):
        place = pl.ds(q * rows, rows)
        for h in range(2):
            p = q * 2 + h
            lanes = pl.ds(h * DK, DK)
            query = qkv_ref[0, place, pl.ds(h * DK, DK)]
            key = qkv_ref[0, place, pl.ds((2 + h) * DK, DK)]
            mixed = m_ref[place, lanes]
            up = dh_ref[place, lanes].astype(F32)
            scale = lax.rsqrt(jnp.mean(mixed * mixed, axis=-1, keepdims=True) + EPS)
            unit = mixed * scale
            gain_grad = gain_grad + jnp.sum(up * unit, axis=0, keepdims=True)
            inner = up * gain
            grad = scale * (inner - unit * jnp.mean(inner * unit, axis=-1, keepdims=True))
            grad = grad.astype(BF16)
            state = s_ref[p]
            fresh = f_ref[place, lanes]
            scores = jnp.where(i >= j, dot1(query, key, NT), 0.0)
            fresh_grad = dot1(scores, grad, TN)
            gf_ref[place, lanes] = fresh_grad
            sg_ref[0, p] = (
                dot1(query, grad, TN) - dot1(wu_ref[0, p, :, :DK], fresh_grad, TN)
            ).astype(BF16)
            score_grad = jnp.where(i >= j, dot1(grad, fresh, NT), 0.0).astype(BF16)
            gq_ref[place, lanes] = dot1(grad, state, NT) + dot1(score_grad, key)
            gk_ref[place, lanes] = dot1(score_grad, query, TN)
    ghg_ref[0] = jnp.broadcast_to(gain_grad, ghg_ref.shape[1:])


def fourth_kernel(qkv_ref, pre_ref, cv_ref, b_ref, t_ref, wu_ref, s_ref, l_ref, f_ref, gf_ref, gq_ref, gk_ref, eg_ref, gc_ref, lg_ref, gb_ref):
    rows = qkv_ref.shape[1] // 2
    frame = rows + HALO
    i, j = grid_masks(rows)
    taps = cv_ref[0]
    lane = lax.broadcasted_iota(jnp.int32, (rows, DK), 1)
    conv_grad = [[jnp.zeros((1, DK), F32) for _ in range(CONV)] for _ in range(6)]
    for q in range(2):
        place = pl.ds(q * rows, rows)
        rate_grads = []
        for h in range(2):
            p = q * 2 + h
            lanes = pl.ds(h * DK, DK)
            query = qkv_ref[0, place, pl.ds(h * DK, DK)]
            key = qkv_ref[0, place, pl.ds((2 + h) * DK, DK)]
            value = qkv_ref[0, place, pl.ds((4 + h) * DK, DK)]
            col = b_ref[0, place, h : h + 1]
            state, adjoint = s_ref[p], l_ref[p]
            both = wu_ref[0, p]
            fresh_grad = gf_ref[place, lanes] + dot1(key, adjoint)
            key_grad = gk_ref[place, lanes] + dot1(f_ref[place, lanes], adjoint, NT)
            factor_grad = jnp.concatenate([-dot1(fresh_grad, state, NT), fresh_grad], axis=1)
            solved = dot1(t_ref[0, p], factor_grad, TN)
            key32, value32 = key.astype(F32), value.astype(F32)
            rate_grad = jnp.sum(
                solved[:, :DK] * key32 + solved[:, DK:] * value32, axis=-1, keepdims=True
            )
            key_grad = key_grad + col * solved[:, :DK]
            value_grad = col * solved[:, DK:]
            system_grad = jnp.where(i > j, -dot1(solved, both, NT), 0.0)
            inner = dot1(key, key, NT)
            rate_grad = rate_grad + jnp.sum(system_grad * inner, axis=-1, keepdims=True)
            inner_grad = (system_grad * col).astype(BF16)
            key_grad = key_grad + dot1(inner_grad, key) + dot1(inner_grad, key, TN)
            rate_grads.append(rate_grad * col * (1.0 - col))
            grads = (gq_ref[place, lanes], key_grad, value_grad)
            for kind in range(3):
                at = kind * 2 + h
                cols = pl.ds(at * DK, DK)
                ext = pre_ref[0, q * frame : (q + 1) * frame, cols].astype(F32)
                tap = cv_ref[0, :, cols]
                conv = conv_of(ext, tap, rows)
                sig = sigmoid(conv)
                act = conv * sig
                grad = grads[kind]
                if kind < 2:
                    scale = lax.rsqrt(jnp.sum(act * act, axis=-1, keepdims=True) + EPS)
                    unit = act * scale
                    grad = grad * DK ** (-0.5) if kind == 0 else grad
                    grad = scale * (grad - unit * jnp.sum(grad * unit, axis=-1, keepdims=True))
                grad = grad * (sig * (1.0 + conv * (1.0 - sig)))
                zero = jnp.zeros((HALO, DK), F32)
                wide = jnp.concatenate([zero, grad, zero], axis=0)
                total = tap[0:1, :] * wide[3 : 3 + frame]
                for t in range(1, CONV):
                    total = total + tap[t : t + 1, :] * wide[3 - t : 3 - t + frame]
                eg_ref[0, q * frame : (q + 1) * frame, cols] = total.astype(BF16)
                for t in range(CONV):
                    conv_grad[at][t] = conv_grad[at][t] + jnp.sum(
                        grad * ext[HALO - 3 + t : HALO - 3 + t + rows], axis=0, keepdims=True
                    )
        logit = jnp.where(lane == 0, rate_grads[0], jnp.where(lane == 1, rate_grads[1], 0.0))
        lg_ref[0, place, :] = logit.astype(BF16)
        gb_ref[0, q : q + 1, :] = jnp.sum(logit, axis=0, keepdims=True)
    for at in range(6):
        for t in range(CONV):
            gc_ref[0, t : t + 1, at * DK : (at + 1) * DK] = conv_grad[at][t]


def lead(*shape):
    return pl.BlockSpec((1,) + shape, lambda p: (p,) + (0,) * len(shape))


def whole(*shape):
    return pl.BlockSpec(shape, lambda p: (0,) * len(shape))


def columns(rows, cols):
    return pl.BlockSpec((rows, cols), lambda p: (0, p))


def quarter():
    return pl.BlockSpec((4, DK, DK), lambda p: (p, 0, 0))


def on_core(kernel, outs, in_specs, out_specs, flops, name):
    return pl.pallas_call(
        kernel,
        out_shape=outs,
        grid=(2,),
        in_specs=in_specs,
        out_specs=out_specs,
        compiler_params=pltpu.CompilerParams(
            vmem_limit_bytes=VMEM_LIMIT, dimension_semantics=("arbitrary",)
        ),
        cost_estimate=pl.CostEstimate(flops=flops, bytes_accessed=8_000_000, transcendentals=0),
        name=name,
    )


def sds(shape, kind):
    return jax.ShapeDtypeStruct(shape, kind)


def scan_states(pd):
    count = lax.axis_size("z") * lax.axis_size("y")
    if count == pd.shape[0]:
        every = lax.all_to_all(pd, SEQ, 0, 0, tiled=True)
        states = pl.pallas_call(
            state_kernel, out_shape=sds((count, DK, DK), BF16), name="state_scan"
        )(every)
        return lax.all_to_all(states, SEQ, 0, 0, tiled=True), every
    every = lax.all_gather(pd, SEQ)
    me = lax.axis_index(SEQ)

    def step(s, state):
        one = lax.dynamic_index_in_dim(every, s, 0, False).astype(F32)
        moved = jnp.einsum(
            "pij,pjk->pik", one[:, :, :DK], state, precision=lax.Precision.HIGHEST
        )
        return state - moved + one[:, :, DK:]

    state = lax.fori_loop(0, me, step, jnp.zeros((pd.shape[0], DK, DK), F32))
    return state.astype(BF16), every


def scan_adjoints(every, start):
    count = lax.axis_size("z") * lax.axis_size("y")
    if count == start.shape[0]:
        grads = lax.all_to_all(start, SEQ, 0, 0, tiled=True)
        adjoints = pl.pallas_call(
            adjoint_kernel, out_shape=sds((count, DK, DK), BF16), name="adjoint_scan"
        )(every, grads)
        return lax.all_to_all(adjoints, SEQ, 0, 0, tiled=True)
    grads = lax.all_gather(start, SEQ)
    me = lax.axis_index(SEQ)

    def step(k, adjoint):
        s = count - 1 - k
        one = lax.dynamic_index_in_dim(every, s, 0, False).astype(F32)
        moved = jnp.einsum(
            "pji,pjk->pik", one[:, :, :DK], adjoint, precision=lax.Precision.HIGHEST
        )
        return adjoint - moved + lax.dynamic_index_in_dim(grads, s, 0, False).astype(F32)

    adjoint = lax.fori_loop(0, count - 1 - me, step, jnp.zeros((start.shape[0], DK, DK), F32))
    return adjoint.astype(BF16)


def shards(
    inputs,
    domain_ids,
    norm1_gain,
    w_qkv,
    w_beta,
    conv_weight,
    domain_bias,
    head_gain,
    w_out,
    norm2_gain,
    w_gate_up,
    w_down,
    cotangent,
):
    core = lax.axis_index("core")
    nz, ny, nx = (lax.axis_size(a) for a in ("z", "y", "x"))
    chips = nz * ny * nx
    seq_devices = nz * ny
    rows = inputs.shape[1]
    frame = rows + HALO
    drows = w_qkv.shape[0]
    frows = w_down.shape[0]
    first = core == 0
    half = H // 2

    qkv_part = chip_rows(
        w_qkv.reshape(drows, 3, 2, 2, 256).transpose(2, 3, 0, 1, 4).reshape(2, 2, drows, 768), core
    )
    w_q_one, w_q_two = gather_chips(qkv_part)

    grows = conv_weight.shape[0]
    small = jnp.concatenate(
        [norm1_gain, norm2_gain, w_beta.reshape(-1), conv_weight.reshape(-1)]
    ).reshape(1, -1)
    smalls = gather_axis(small, "core", 0)
    for axis in ("x", "y", "z"):
        smalls = gather_axis(smalls, axis, 0)
    smalls = smalls.reshape(2 * chips, -1)
    gain_one = smalls[:, :drows].reshape(1, D).astype(F32)
    gain_two = smalls[:, drows : 2 * drows].reshape(1, D).astype(F32)
    full_beta = smalls[:, 2 * drows : 2 * drows + drows * H].reshape(D, 2, half)
    full_conv = smalls[:, 2 * drows + drows * H :].reshape(3, 2, 2, 256, CONV)
    beta_mine = lax.dynamic_index_in_dim(full_beta, core, 1, False)
    conv_mine = (
        lax.dynamic_index_in_dim(full_conv, core, 1, False)
        .transpose(1, 3, 0, 2)
        .reshape(2, CONV, 768)
        .astype(F32)
    )
    beta_pairs = jnp.pad(
        beta_mine.reshape(D, 2, 2).transpose(1, 0, 2), ((0, 0), (0, 0), (0, DK - 2))
    )

    x_own = inputs.reshape(rows, D)
    halo = lax.ppermute(
        x_own[rows - HALO :], SEQ, [(i, i + 1) for i in range(seq_devices - 1)]
    )
    choose = (domain_ids[0] == jnp.arange(NDOM, dtype=jnp.int32)).astype(BF16)
    bias_own = jnp.sum(domain_bias.astype(F32) * choose.astype(F32)[:, None], axis=0)
    extra = jnp.pad(jnp.concatenate([bias_own.astype(BF16), choose]), (0, D - H - NDOM))
    extra = jnp.pad(extra.reshape(1, D), ((0, HALO - 1), (0, 0)))
    frame_own = jnp.concatenate([halo, x_own, extra], axis=0)
    frame_other = swap(frame_own)
    x_frames = jnp.concatenate([frame_own[:frame], frame_other[:frame]], axis=0)
    x_both = jnp.concatenate([x_own, frame_other[HALO:frame]], axis=0).astype(F32)
    bias_both = jnp.stack([extra[0, :H], frame_other[frame, :H]]).astype(F32)
    choose_both = jnp.stack(
        [extra[0, H : H + NDOM], frame_other[frame, H : H + NDOM]]
    ).astype(F32)
    bias_mine = lax.dynamic_index_in_dim(bias_both.reshape(2, 2, half), core, 1, False)
    bias_pairs = jnp.pad(
        bias_mine.reshape(2, 2, 2).transpose(1, 0, 2), ((0, 0), (0, 0), (0, DK - 2))
    )
    g_own = cotangent.reshape(rows, D)
    g_both = jnp.concatenate([g_own, swap(g_own)], axis=0)

    out_cols = w_out.reshape(drows, 2, 2, 256).transpose(1, 2, 0, 3)
    gu_cols = (
        w_gate_up.reshape(drows, 2, chips, 2, frows)
        .transpose(3, 1, 0, 2, 4)
        .reshape(2, 2, drows, FF // 2)
    )
    gu_one, gu_two = gather_chips(
        chip_rows(jnp.concatenate([gu_cols, out_cols], axis=-1), core)
    )
    w_gate, w_up = gu_one[:, : FF // 2], gu_two[:, : FF // 2]
    out_mine = jnp.concatenate([gu_one[:, FF // 2 :], gu_two[:, FF // 2 :]], axis=1)
    out_got = swap(out_mine)
    full_out = jnp.concatenate(
        [jnp.where(first, out_mine, out_got), jnp.where(first, out_got, out_mine)], axis=1
    )
    down_one, down_two = gather_chips(w_down.reshape(frows, 2, D // 2).transpose(1, 0, 2))
    w_down_mine = jnp.concatenate([down_one, down_two], axis=1)

    w_q = jnp.stack([w_q_one, w_q_two])
    tall = 2 * rows
    normed, pre, qkv, inverse, factors, pd, rates = on_core(
        first_kernel,
        (
            sds((2 * frame, D), BF16),
            sds((2, 2 * frame, 768), BF16),
            sds((2, tall, 768), BF16),
            sds((2, 4, rows, rows), BF16),
            sds((2, 4, rows, 2 * DK), BF16),
            sds((2, 4, DK, 2 * DK), BF16),
            sds((2, tall, DK), F32),
        ),
        [
            whole(2 * frame, D),
            whole(1, D),
            lead(D, 768),
            lead(D, DK),
            lead(CONV, 768),
            lead(2, DK),
        ],
        (
            whole(2 * frame, D),
            lead(2 * frame, 768),
            lead(tall, 768),
            lead(4, rows, rows),
            lead(4, rows, 2 * DK),
            lead(4, DK, 2 * DK),
            lead(tall, DK),
        ),
        10_000_000_000,
        "delta_local",
    )(x_frames, gain_one, w_q, beta_pairs, conv_mine, bias_pairs)

    states, every = scan_states(pd.reshape(H, DK, 2 * DK))
    gain_head = head_gain.astype(F32).reshape(1, DK)
    fresh, mixed, heads_mine = on_core(
        second_kernel,
        (sds((tall, 512), BF16), sds((tall, 512), F32), sds((tall, 512), BF16)),
        [lead(tall, 768), lead(4, rows, 2 * DK), quarter(), whole(1, DK)],
        (columns(tall, 256), columns(tall, 256), columns(tall, 256)),
        2_000_000_000,
        "delta_mix",
    )(qkv, factors, states, gain_head)

    heads_got = swap(heads_mine)
    heads_got = jnp.concatenate([heads_got[rows:], heads_got[:rows]], axis=0)
    heads = jnp.concatenate(
        [jnp.where(first, heads_mine, heads_got), jnp.where(first, heads_got, heads_mine)], axis=1
    )
    middle = x_both + jnp.dot(heads, full_out, preferred_element_type=F32)
    scale_two = lax.rsqrt(jnp.mean(middle * middle, axis=-1, keepdims=True) + EPS)
    unit_two = middle * scale_two
    normed_two = (unit_two * gain_two).astype(BF16)
    gate = jnp.dot(normed_two, w_gate, preferred_element_type=F32)
    up = jnp.dot(normed_two, w_up, preferred_element_type=F32)
    sig = jax.nn.sigmoid(gate)
    hidden = (gate * sig * up).astype(BF16)
    hidden_grad = jnp.einsum("nd,fd->nf", g_both, w_down_mine, preferred_element_type=F32)
    up_grad = (hidden_grad * gate * sig).astype(BF16)
    gate_grad = (hidden_grad * up * sig * (1.0 + gate * (1.0 - sig))).astype(BF16)
    normed_two_part = jnp.einsum(
        "nf,df->nd", gate_grad, w_gate, preferred_element_type=F32
    ) + jnp.einsum("nf,df->nd", up_grad, w_up, preferred_element_type=F32)
    part_got = swap(normed_two_part.astype(BF16))
    part_got = jnp.concatenate([part_got[rows:], part_got[:rows]], axis=0)
    normed_two_grad = normed_two_part + part_got.astype(F32)
    grad_norm2 = jnp.sum(normed_two_grad[:rows] * unit_two[:rows], axis=0)
    inner = normed_two_grad * gain_two
    middle_grad = g_both.astype(F32) + scale_two * (
        inner - unit_two * jnp.mean(inner * unit_two, axis=-1, keepdims=True)
    )
    middle_low = middle_grad.astype(BF16)
    out_rows = lax.dynamic_slice_in_dim(full_out, core * 512, 512, 0)
    heads_grad = jnp.einsum("ne,de->nd", middle_low, out_rows, preferred_element_type=F32)

    start_grad, fresh_grad, query_grad, key_grad, gain_part = on_core(
        third_kernel,
        (
            sds((2, 4, DK, DK), BF16),
            sds((tall, 512), F32),
            sds((tall, 512), F32),
            sds((tall, 512), F32),
            sds((2, 8, DK), F32),
        ),
        [
            lead(tall, 768),
            lead(4, rows, 2 * DK),
            quarter(),
            columns(tall, 256),
            columns(tall, 256),
            columns(tall, 256),
            whole(1, DK),
        ],
        (
            lead(4, DK, DK),
            columns(tall, 256),
            columns(tall, 256),
            columns(tall, 256),
            lead(8, DK),
        ),
        4_000_000_000,
        "delta_back_local",
    )(qkv, factors, states, fresh, mixed, heads_grad, gain_head)
    adjoints = scan_adjoints(every, start_grad.reshape(H, DK, DK))

    grad_down = jnp.einsum("nf,nd->fd", hidden, g_both, preferred_element_type=F32).astype(BF16)
    down_sum = scatter_chips(grad_down[:, : D // 2], grad_down[:, D // 2 :])
    own_down = down_sum.transpose(1, 0, 2).reshape(frows, D)
    grad_gate = jnp.einsum("nd,nf->df", normed_two, gate_grad, preferred_element_type=F32)
    grad_up = jnp.einsum("nd,nf->df", normed_two, up_grad, preferred_element_type=F32)
    low_cols = lax.dynamic_slice_in_dim(middle_low, core * 512, 512, 1)
    grad_out = jnp.einsum("nd,ne->de", heads, low_cols, preferred_element_type=F32)
    gu_sum = scatter_chips(
        jnp.concatenate([grad_gate.astype(BF16), grad_out[:, :256].astype(BF16)], axis=1),
        jnp.concatenate([grad_up.astype(BF16), grad_out[:, 256:].astype(BF16)], axis=1),
    )
    gu_own = own_rows(gu_sum, core)
    own_gu = (
        gu_own[..., : FF // 2]
        .reshape(2, 2, drows, chips, frows)
        .transpose(2, 1, 3, 0, 4)
        .reshape(drows, 2 * FF)
    )
    own_out = gu_own[..., FF // 2 :].transpose(2, 0, 1, 3).reshape(drows, D)

    down_part = jnp.dot(hidden, w_down_mine, preferred_element_type=F32)
    output = (middle[:rows] + down_part[:rows]) + swap(down_part[rows:].astype(BF16)).astype(F32)
    output = output.astype(BF16).reshape(1, rows, D)

    ext_grad, conv_part, logit_low, bias_part = on_core(
        fourth_kernel,
        (
            sds((2, 2 * frame, 768), BF16),
            sds((2, CONV, 768), F32),
            sds((2, tall, DK), BF16),
            sds((2, 2, DK), F32),
        ),
        [
            lead(tall, 768),
            lead(2 * frame, 768),
            lead(CONV, 768),
            lead(tall, DK),
            lead(4, rows, rows),
            lead(4, rows, 2 * DK),
            quarter(),
            quarter(),
            columns(tall, 256),
            columns(tall, 256),
            columns(tall, 256),
            columns(tall, 256),
        ],
        (lead(2 * frame, 768), lead(CONV, 768), lead(tall, DK), lead(2, DK)),
        8_000_000_000,
        "delta_back",
    )(qkv, pre, conv_mine, rates, inverse, factors, states, adjoints, fresh, fresh_grad, query_grad, key_grad)
    ext_frames = ext_grad.reshape(2, 2, frame, 768)
    sent_back = lax.ppermute(
        ext_frames[:, :, :HALO], SEQ, [(i + 1, i) for i in range(seq_devices - 1)]
    )
    grad_q = jnp.einsum("nd,pnf->pdf", normed, ext_grad, preferred_element_type=F32).astype(BF16)
    q_sum = scatter_chips(grad_q[0], grad_q[1])
    q_own = own_rows(q_sum, core)
    own_qkv = (
        q_own.reshape(2, 2, drows, 3, 256).transpose(2, 3, 0, 1, 4).reshape(drows, 3 * D)
    )

    normed_tokens = normed.reshape(2, frame, D)[:, HALO:].reshape(tall, D)
    grad_beta = jnp.einsum(
        "nd,pnh->dph", normed_tokens, logit_low[:, :, :2], preferred_element_type=F32
    ).reshape(D, half)
    tail = ext_frames[:, :, frame - HALO :].astype(F32) + sent_back.astype(F32)
    pre_low = jnp.concatenate(
        [ext_frames[:, :, HALO : frame - HALO], tail.astype(BF16)], axis=2
    ).reshape(2, tall, 768)
    normed_part = (
        jnp.einsum("nf,df->nd", pre_low[0], w_q[0], preferred_element_type=F32)
        + jnp.einsum("nf,df->nd", pre_low[1], w_q[1], preferred_element_type=F32)
        + jnp.einsum("pnh,pdh->nd", logit_low, beta_pairs, preferred_element_type=F32)
    )
    normed_grad = normed_part[:rows] + swap(normed_part[rows:].astype(BF16)).astype(F32)
    x32 = x_both[:rows]
    scale_one = lax.rsqrt(jnp.mean(x32 * x32, axis=-1, keepdims=True) + EPS)
    unit_one = x32 * scale_one
    grad_norm1 = jnp.sum(normed_grad * unit_one, axis=0)
    inner_one = normed_grad * gain_one
    grad_input = middle_grad[:rows] + scale_one * (
        inner_one - unit_one * jnp.mean(inner_one * unit_one, axis=-1, keepdims=True)
    )
    grad_input = grad_input.reshape(1, rows, D)

    beta_full = jnp.where(
        first,
        jnp.pad(grad_beta, ((0, 0), (0, half))),
        jnp.pad(grad_beta, ((0, 0), (half, 0))),
    )
    conv_cols = conv_part.reshape(2, CONV, 3, 256).transpose(2, 0, 3, 1).reshape(3, 512, CONV)
    conv_full = jnp.where(
        first,
        jnp.pad(conv_cols, ((0, 0), (0, 512), (0, 0))),
        jnp.pad(conv_cols, ((0, 0), (512, 0), (0, 0))),
    )
    bias_heads = bias_part[:, :, :2].transpose(1, 0, 2).reshape(2, half)
    bias_heads = jnp.where(
        first,
        jnp.pad(bias_heads, ((0, 0), (0, half))),
        jnp.pad(bias_heads, ((0, 0), (half, 0))),
    )
    bias_grad = jnp.sum(choose_both[:, :, None] * bias_heads[:, None, :], axis=0)
    head_grad = gain_part[0, 0] + gain_part[1, 0]
    pack = jnp.concatenate(
        [
            grad_norm1,
            grad_norm2,
            beta_full.reshape(-1),
            conv_full.reshape(-1),
            bias_grad.reshape(-1),
            head_grad,
        ]
    )
    pack = jnp.pad(pack, (0, -pack.shape[0] % 1024)).reshape(-1, DK)
    pack = reduce_small(pack).reshape(-1)
    me = lax.axis_index(ALL)
    at = 2 * D
    own_g1 = lax.dynamic_slice_in_dim(pack[:D], me * drows, drows)
    own_g2 = lax.dynamic_slice_in_dim(pack[D:at], me * drows, drows)
    own_beta = lax.dynamic_slice_in_dim(
        pack[at : at + D * H].reshape(D, H), me * drows, drows
    )
    at += D * H
    own_conv = lax.dynamic_slice_in_dim(
        pack[at : at + 3 * D * CONV].reshape(3 * D, CONV), me * grows, grows
    )
    at += 3 * D * CONV
    bias_total = pack[at : at + NDOM * H].reshape(NDOM, H)
    at += NDOM * H
    gain_total = pack[at : at + DK]
    return (
        output,
        grad_input,
        own_g1,
        own_qkv,
        own_beta,
        own_conv,
        bias_total,
        gain_total,
        own_out,
        own_g2,
        own_gu,
        own_down,
    )


def solution(mesh):
    seq, batch = mesh.shape["seq"], mesh.shape["batch"]
    fine = Mesh(mesh.devices.reshape(seq // 2, 2, batch // 2, 2), ALL)
    tokens = P(("x", "core"), ("z", "y"), None)
    rows = P(ALL, None)
    vector = P(ALL)
    return jax.shard_map(
        shards,
        mesh=fine,
        in_specs=(
            tokens,
            P(("x", "core")),
            vector,
            rows,
            rows,
            rows,
            P(),
            P(),
            rows,
            vector,
            rows,
            rows,
            tokens,
        ),
        out_specs=(
            tokens,
            tokens,
            vector,
            rows,
            rows,
            rows,
            P(),
            P(),
            rows,
            vector,
            rows,
            rows,
        ),
        check_vma=False,
    )
```

time: 1710 us -> 570 us (0.33)
  waiting for transfers between devices: 979 us -> 185 us
  blocking collectives: 207 us -> 0 us
  matrix products: 207 us -> 39.7 us
  other arithmetic: 200 us -> 64.5 us
  starting transfers between devices: 5.77 us -> 96.5 us
  Pallas kernels: 0 us -> 65.3 us
  local copies, waits for them, and re-layouts: 85.2 us -> 105 us
    reduce_scatter x8 -> x0, waiting for transfers between devices: 555 us -> none  [the longest x1 196 us: shards(): lax.psum_scatter(grad_gate_up.astype(jnp.bfloat16), 'seq', scatter_dimens...]
    all_gather x9 -> x0, waiting for transfers between devices: 336 us -> none  [the longest x1 159 us: shards(): lax.all_gather(part_gu, 'seq', axis=0, tiled=True)]
    dot_general x101 -> x17, matrix products: 199 us -> 39.7 us  [the longest x1 6.26 us: shards(): jnp.einsum('nd,fd->nf', g_both, w_down_mine, preferred_element_type=F32)]
    ppermute x2 -> x67, waiting for transfers between devices: 5.58 us -> 159 us  [the longest x53 155 us: turned(): return lax.ppermute(a, axis, [(i, (i + by) % n) for i in range(n)])]
    all_gather x9 -> x0, blocking collectives: 135 us -> none  [the longest x1 30.9 us: shards(): lax.all_gather(part_conv, 'seq', axis=0, tiled=True)]
    another operation x6 -> x42, other arithmetic: 160 us -> 28.9 us  [the longest x30 19.1 us: gather_axis(): jnp.stack([jnp.where(first, a, got[0]), jnp.where(first, got[0], a)], axi...]
    unnamed x25 -> x0, waiting for transfers between devices: 82.6 us -> none
    ppermute x2 -> x67, starting transfers between devices: 4.27 us -> 78.2 us  [the longest x53 72 us: turned(): return lax.ppermute(a, axis, [(i, (i + by) % n) for i in range(n)])]
  transfers between devices with their start and end apart: 23 -> 71, of which waited for: 17 -> 26; matrix products, arithmetic and copies ran while one was open for 22% -> 31% of each run, Pallas kernels for 0% -> 12%
where the time goes in v1:
time: 570 us; the launch traced here: 559 us
  waiting for transfers between devices  185 us (32%)
  local copies, waits for them, and re-layouts  105 us (18%)
  starting transfers between devices  96.5 us (17%)
  Pallas kernels  65.3 us (11%)
  other arithmetic  64.5 us (11%)
  matrix products  39.7 us (7%)
    ppermute x53, waiting for transfers between devices, turned(): return lax.ppermute(a, axis, [(i, (i + by) % n) for i in range(n)])  155 us
    ppermute x53, starting transfers between devices, turned(): return lax.ppermute(a, axis, [(i, (i + by) % n) for i in range(n)])  72 us
    unnamed x212, local copies, waits for them, and re-layouts  38.6 us
    pallas_call x1, Pallas kernels, shards(): on_core(first_kernel, (sds((2 * frame, D), BF16), sds((2, 2 * frame, 768)...  35.9 us
    all_to_all x1, waiting for transfers between devices, scan_states(): return (lax.all_to_all(states, SEQ, 0, 0, tiled=True), every)  25.2 us
    another operation x30, other arithmetic, gather_axis(): jnp.stack([jnp.where(first, a, got[0]), jnp.where(first, got[0], a)], axi...  19.1 us
    pallas_call x1, Pallas kernels, shards(): on_core(fourth_kernel, (sds((2, 2 * frame, 768), BF16), sds((2, CONV, 768...  15.2 us
  transfers between devices with their start and end apart: 71, of which 26 were waited for; matrix products, arithmetic and copies ran while one was open for 31% of the time, Pallas kernels for 12%

profile of v1, /device:TPU:0, one launch (start us, length us, event | category | flops | bytes accessed | tf_op | source)
XLA Modules:
  0.0 559.5 jit_solution(937832407600595662)
XLA Ops:
  2.4 5.0 collective-permute-start.26
  35.5 3.8 collective-permute-done.7
  70.5 3.9 collective-permute-start.18
  87.6 23.7 %collective-permute-done.19 = bf16[2,64,1664]{2,1,0:T(8,128)(2,1)} collective-permute-done((bf16[2,64,1664]{2,1,0:T(8,128)(2,1)}, bf16[2,64,1664]{2,1,0:T(8,128)(2,1)}, u32[]{:S(2)}, u32[]{:S(2)}) %collective-permute-start.19) | collective-permute-done | bytes 426016 | tf_op jit(solution)/shard_map/ppermute | solution.py:32
  123.7 22.2 %collective-permute-done.15 = bf16[4,2,64,768]{3,2,0,1:T(8,128)(2,1)S(1)} collective-permute-done((bf16[4,2,64,768]{3,2,0,1:T(8,128)(2,1)S(1)}, bf16[4,2,64,768]{3,2,0,1:T(8,128)(2,1)S(1)}, u32[]{:S(2)}, u32[]{:S(2)}) %collective-permute-start.15) | collective-permute-done | bytes 786464 | tf_op jit(solution)/shard_map/ppermute | solution.py:32
  151.6 35.9 %delta_local.1 = (bf16[544,1024]{1,0:T(8,128)(2,1)S(1)}, bf16[2,544,768]{2,1,0:T(8,128)(2,1)}, bf16[2,512,768]{2,1,0:T(8,128)(2,1)}, bf16[2,4,256,256]{3,2,1,0:T...) custom-call(bf16[544,1024]{1,0:T(8,128)(2,1)S(1)} %pad_maximum_fusio, ...), custom_call_target="tpu_custom_call" | custom-call | flops 10000000000 | bytes 8000000 | tf_op jit(solution)/shard_map/delta_local/pallas_call | solution.py:538
  190.2 4.5 all-to-all-start
  211.1 4.2 all-to-all-start.1
  217.8 25.2 %all-to-all-done.1.s_ref = bf16[8,128,128]{2,1,0:T(8,128)(2,1)S(1)} async-done(((bf16[8,128,128]{2,1,0:T(8,128)(2,1)}), bf16[8,128,128]{2,1,0:T(8,128)(2,1)S(1)}, u32[]{:S(2)}, u32[]{:S(2)}) %all-to-all-start.1) | async-done | bytes 262176 | tf_op jit(solution)/shard_map/all_to_all | solution.py:403
  265.8 6.3 %multiply_convert_fusion.1 = (bf16[512,1408]{1,0:T(8,128)(2,1)S(1)}, bf16[512,1408]{1,0:T(8,128)(2,1)}, bf16[512,1408]{1,0:T(8,128)(2,1)}) fusion(f32[512,1408]{1,0:T(8,128)S(1)} %fusion.8, f32[512,1408]{1,0:T(8,128)} %fusion.4, bf16[1408,512]{1,0:T(8,128)(2,1)S(1)} %bitcast.482, bf16[1408,512]{1,0:T(8,128)(2,1)S(1)} %bitcast.484, ...), kind=kOutput, calls=%fused_computation.15 | convolution fusion | flops 1495793664 | bytes 14024704 | tf_op jit(solution)/shard_map/nd,fd->nf/dot_general | solution.py:594
  288.6 3.5 convolution_convert_fusion.1
  293.1 11.3 %collective-permute-done.60 = bf16[4,2,88,512]{3,2,0,1:T(8,128)(2,1)S(1)} collective-permute-done((bf16[4,2,88,512]{3,2,0,1:T(8,128)(2,1)S(1)}, bf16[4,2,88,512]{3,2,0,1:T(8,128)(2,1)S(1)}, u32[]{:S(2)}, u32[]{:S(2)}) %collective-permute-start.60) | collective-permute-done | bytes 720928 | tf_op jit(solution)/shard_map/ppermute | solution.py:32
  316.4 6.0 %delta_back_local.1 = (bf16[2,4,128,128]{3,2,1,0:T(8,128)(2,1)}, f32[512,512]{1,0:T(8,128)S(1)}, f32[512,512]{1,0:T(8,128)S(1)}, f32[512,512]{1,0:T(8,128)S(1)}, f32[2,8,128]{2,1,0:T(8,128)S(1)}) custom-call(bf16[2,512,768]{2,1,0:T(8,128)(2,1)} %get-tuple-element.31.qkv_ref, bf16[2,4,256,256]{3,2,1,0:T(8,128)(2,1)S(1)} %copy-done.2, ...), custom_call_target="tpu_custom_call" | custom-call | flops 4000000000 | bytes 8000000 | tf_op jit(solution)/shard_map/delta_back_local/pallas_call | solution.py:612
  325.4 4.5 all-to-all-start.2
  347.7 5.0 all-to-all-start.3
  352.8 3.9 collective-permute-start.66
  361.7 13.9 %collective-permute-done.65 = bf16[2,88,512]{2,1,0:T(8,128)(2,1)S(1)} collective-permute-done((bf16[2,88,512]{2,1,0:T(8,128)(2,1)S(1)}, bf16[2,88,512]{2,1,0:T(8,128)(2,1)S(1)}, u32[]{:S(2)}, u32[]{:S(2)}) %collective-permute-start.65) | collective-permute-done | bytes 180256 | tf_op jit(solution)/shard_map/ppermute | solution.py:32
  382.1 15.2 %delta_back.1 = (bf16[2,544,768]{2,1,0:T(8,128)(2,1)}, f32[2,4,768]{2,1,0:T(4,128)S(1)}, bf16[2,512,128]{2,1,0:T(8,128)(2,1)S(1)}, f32[2,2,128]{2,1,0:T(2,128)S(1)}) custom-call(bf16[2,512,768]{2,1,0:T(8,128)(2,1)} %get-tuple-element.31.qkv_ref, bf16[2,544,768]{2,1,0:T(8,128)(2,1)} %get-tuple-element.35.pre_ref, f32[2,4,768]{2,1,0:T(4,128)S(1)} %bitcast.445, ...), custom_call_target="tpu_custom_call" | custom-call | flops 8000000000 | bytes 8000000 | tf_op jit(solution)/shard_map/delta_back/pallas_call | solution.py:666
  400.9 4.1 convert_bitcast_fusion
  448.2 4.4 collective-permute-done.39
  454.1 13.4 %collective-permute-done.40 = f32[184,128]{1,0:T(8,128)S(1)} collective-permute-done((f32[184,128]{1,0:T(8,128)S(1)}, f32[184,128]{1,0:T(8,128)S(1)}, u32[]{:S(2)}, u32[]{:S(2)}) %collective-permute-start.40) | collective-permute-done | bytes 94240 | tf_op jit(solution)/shard_map/ppermute | solution.py:32
  474.3 4.3 collective-permute-done.42
  479.3 5.7 %collective-permute-done.43 = f32[184,128]{1,0:T(8,128)S(1)} collective-permute-done((f32[184,128]{1,0:T(8,128)S(1)}, f32[184,128]{1,0:T(8,128)S(1)}, u32[]{:S(2)}, u32[]{:S(2)}) %collective-permute-start.43) | collective-permute-done | bytes 94240 | tf_op jit(solution)/shard_map/ppermute | solution.py:32
  517.7 27.6 %collective-permute-done.57 = bf16[2,64,1664]{2,1,0:T(8,128)(2,1)} collective-permute-done((bf16[2,64,1664]{2,1,0:T(8,128)(2,1)}, bf16[2,64,1664]{2,1,0:T(8,128)(2,1)}, u32[]{:S(2)}, u32[]{:S(2)}) %collective-permute-start.57) | collective-permute-done | bytes 426016 | tf_op jit(solution)/shard_map/ppermute | solution.py:32
  (579 shorter events, 298.4 us)
Async XLA Ops:
  2.4 47.0 %collective-permute-start.26 = (bf16[2,88,512]{2,0,1:T(2,128)(2,1)}, bf16[2,88,512]{2,0,1:T(2,128)(2,1)}, u32[]{:S(2)}, u32[]{:S(2)}) collective-permute-start(bf16[2,88,512]{2,0,1:T(2,128)(2,1)} %bitcast.81), channel_id=1, source_target_pairs={{0,24},{8,0},{16,8},{24,16},{1,25},{9,1},{17,9},{25,17},{2,26},{10... | collective-permute-start | bytes 540680 | tf_op jit(solution)/shard_map/ppermute | solution.py:32
  7.5 43.5 %collective-permute-start.27 = (bf16[2,88,512]{2,0,1:T(2,128)(2,1)}, bf16[2,88,512]{2,0,1:T(2,128)(2,1)}, u32[]{:S(2)}, u32[]{:S(2)}) collective-permute-start(bf16[2,88,512]{2,0,1:T(2,128)(2,1)} %bitcast.81), channel_id=1, source_target_pairs={{0,16},{8,24},{16,0},{24,8},{1,17},{9,25},{17,1},{25,9},{2,18},{10... | collective-permute-start | bytes 540680 | tf_op jit(solution)/shard_map/ppermute | solution.py:32
  7.5 46.6 %collective-permute-start.28 = (bf16[2,88,512]{2,0,1:T(2,128)(2,1)}, bf16[2,88,512]{2,0,1:T(2,128)(2,1)}, u32[]{:S(2)}, u32[]{:S(2)}) collective-permute-start(bf16[2,88,512]{2,0,1:T(2,128)(2,1)} %bitcast.81), channel_id=1, source_target_pairs={{0,8},{8,16},{16,24},{24,0},{1,9},{9,17},{17,25},{25,1},{2,10},{10... | collective-permute-start | bytes 540680 | tf_op jit(solution)/shard_map/ppermute | solution.py:32
  14.9 47.1 %collective-permute-start.17 = (bf16[2,32,1664]{2,1,0:T(8,128)(2,1)}, bf16[2,32,1664]{2,1,0:T(8,128)(2,1)}, u32[]{:S(2)}, u32[]{:S(2)}) collective-permute-start(bf16[2,32,1664]{2,1,0:T(8,128)(2,1)} %fusion.64), channel_id=1, source_target_pairs={{0,1},{1,0},{2,3},{3,2},{4,5},{5,4},{6,7},{7,6},{8,9},{9,8},{10,11... | collective-permute-start | bytes 638984 | tf_op jit(solution)/shard_map/ppermute | solution.py:27
  49.2 216.6 %collective-permute-start.34 = (bf16[256,1024]{1,0:T(8,128)(2,1)}, bf16[256,1024]{1,0:T(8,128)(2,1)}, u32[]{:S(2)}, u32[]{:S(2)}) collective-permute-start(bf16[256,1024]{1,0:T(8,128)(2,1)} %bitcast.492), channel_id=1, source_target_pairs={{0,1},{1,0},{2,3},{3,2},{4,5},{5,4},{6,7},{7,6},{8,9},{9,8},{10,11... | collective-permute-start | bytes 1572872 | tf_op jit(solution)/shard_map/ppermute | solution.py:27
  75.5 35.8 %collective-permute-start.19 = (bf16[2,64,1664]{2,1,0:T(8,128)(2,1)}, bf16[2,64,1664]{2,1,0:T(8,128)(2,1)}, u32[]{:S(2)}, u32[]{:S(2)}) collective-permute-start(bf16[2,64,1664]{2,1,0:T(8,128)(2,1)} %pad_maximum_fusion.31), channel_id=1, source_target_pairs={{0,16},{8,24},{16,0},{24,8},{1,17},{9,25},{17,1},{25,9},{2,18},{10... | collective-permute-start | bytes 1277960 | tf_op jit(solution)/shard_map/ppermute | solution.py:32
  77.4 36.4 %collective-permute-start.20 = (bf16[2,64,1664]{2,1,0:T(8,128)(2,1)}, bf16[2,64,1664]{2,1,0:T(8,128)(2,1)}, u32[]{:S(2)}, u32[]{:S(2)}) collective-permute-start(bf16[2,64,1664]{2,1,0:T(8,128)(2,1)} %pad_maximum_fusion.31), channel_id=1, source_target_pairs={{0,8},{8,16},{16,24},{24,0},{1,9},{9,17},{17,25},{25,1},{2,10},{10... | collective-permute-start | bytes 1277960 | tf_op jit(solution)/shard_map/ppermute | solution.py:32
  80.5 37.7 %collective-permute-start.14 = (bf16[4,64,768]{2,1,0:T(8,128)(2,1)}, bf16[4,64,768]{2,1,0:T(8,128)(2,1)}, u32[]{:S(2)}, u32[]{:S(2)}) collective-permute-start(bf16[4,64,768]{2,1,0:T(8,128)(2,1)} %get-tuple-element.125), channel_id=1, source_target_pairs={{0,4},{4,0},{1,5},{5,1},{2,6},{6,2},{3,7},{7,3},{8,12},{12,8},{9,1... | collective-permute-start | bytes 1179656 | tf_op jit(solution)/shard_map/ppermute | solution.py:32
  85.0 35.0 %collective-permute-start.12 = (bf16[4,64,768]{2,1,0:T(8,128)(2,1)S(1)}, bf16[4,64,768]{2,1,0:T(8,128)(2,1)S(1)}, u32[]{:S(2)}, u32[]{:S(2)}) collective-permute-start(bf16[4,64,768]{2,1,0:T(8,128)(2,1)S(1)} %copy-done.72), channel_id=1, source_target_pairs={{0,2},{2,0},{1,3},{3,1},{4,6},{6,4},{5,7},{7,5},{8,10},{10,8},{9,1... | collective-permute-start | bytes 1179656 | tf_op jit(solution)/shard_map/ppermute | solution.py:32
  111.3 104.0 %collective-permute-start.32 = (bf16[4,2,88,512]{3,2,0,1:T(8,128)(2,1)}, bf16[4,2,88,512]{3,2,0,1:T(8,128)(2,1)}, u32[]{:S(2)}, u32[]{:S(2)}) collective-permute-start(bf16[4,2,88,512]{3,2,0,1:T(8,128)(2,1)} %pad_maximum_fusion.27), channel_id=1, source_target_pairs={{0,2},{2,0},{1,3},{3,1},{4,6},{6,4},{5,7},{7,5},{8,10},{10,8},{9,1... | collective-permute-start | bytes 2162696 | tf_op jit(solution)/shard_map/ppermute | solution.py:32
  113.8 140.3 %collective-permute-start.30 = (bf16[4,2,88,512]{3,2,0,1:T(8,128)(2,1)}, bf16[4,2,88,512]{3,2,0,1:T(8,128)(2,1)}, u32[]{:S(2)}, u32[]{:S(2)}) collective-permute-start(bf16[4,2,88,512]{3,2,0,1:T(8,128)(2,1)} %pad_maximum_fusion.26), channel_id=1, source_target_pairs={{0,4},{4,0},{1,5},{5,1},{2,6},{6,2},{3,7},{7,3},{8,12},{12,8},{9,1... | collective-permute-start | bytes 2162696 | tf_op jit(solution)/shard_map/ppermute | solution.py:32
  145.9 48.9 %collective-permute-start.23 = (bf16[4,64,1664]{2,1,0:T(8,128)(2,1)}, bf16[4,64,1664]{2,1,0:T(8,128)(2,1)}, u32[]{:S(2)}, u32[]{:S(2)}) collective-permute-start(bf16[4,64,1664]{2,1,0:T(8,128)(2,1)} %get-tuple-element.102), channel_id=1, source_target_pairs={{0,4},{4,0},{1,5},{5,1},{2,6},{6,2},{3,7},{7,3},{8,12},{12,8},{9,1... | collective-permute-start | bytes 2555912 | tf_op jit(solution)/shard_map/ppermute | solution.py:32
  149.1 50.0 %collective-permute-start.21 = (bf16[4,64,1664]{2,1,0:T(8,128)(2,1)}, bf16[4,64,1664]{2,1,0:T(8,128)(2,1)}, u32[]{:S(2)}, u32[]{:S(2)}) collective-permute-start(bf16[4,64,1664]{2,1,0:T(8,128)(2,1)} %get-tuple-element.101), channel_id=1, source_target_pairs={{0,2},{2,0},{1,3},{3,1},{4,6},{6,4},{5,7},{7,5},{8,10},{10,8},{9,1... | collective-permute-start | bytes 2555912 | tf_op jit(solution)/shard_map/ppermute | solution.py:32
  198.1 48.7 %collective-permute-start.24 = (bf16[4,2,64,1664]{3,2,0,1:T(8,128)(2,1)}, bf16[4,2,64,1664]{3,2,0,1:T(8,128)(2,1)}, u32[]{:S(2)}, u32[]{:S(2)}) collective-permute-start(bf16[4,2,64,1664]{3,2,0,1:T(8,128)(2,1)} %pad_maximum_fusion.11), channel_id=1, source_target_pairs={{0,2},{2,0},{1,3},{3,1},{4,6},{6,4},{5,7},{7,5},{8,10},{10,8},{9,1... | collective-permute-start | bytes 5111816 | tf_op jit(solution)/shard_map/ppermute | solution.py:32
  202.5 46.8 %collective-permute-start.22 = (bf16[4,2,64,1664]{3,2,0,1:T(8,128)(2,1)}, bf16[4,2,64,1664]{3,2,0,1:T(8,128)(2,1)}, u32[]{:S(2)}, u32[]{:S(2)}) collective-permute-start(bf16[4,2,64,1664]{3,2,0,1:T(8,128)(2,1)} %pad_maximum_fusion.10), channel_id=1, source_target_pairs={{0,4},{4,0},{1,5},{5,1},{2,6},{6,2},{3,7},{7,3},{8,12},{12,8},{9,1... | collective-permute-start | bytes 5111816 | tf_op jit(solution)/shard_map/ppermute | solution.py:32
  305.4 36.3 %collective-permute-start.61 = (bf16[4,88,512]{2,1,0:T(8,128)(2,1)}, bf16[4,88,512]{2,1,0:T(8,128)(2,1)}, u32[]{:S(2)}, u32[]{:S(2)}) collective-permute-start(bf16[4,88,512]{2,1,0:T(8,128)(2,1)} %dynamic-slice_bitcast_fusion.14), channel_id=1, source_target_pairs={{0,2},{2,0},{1,3},{3,1},{4,6},{6,4},{5,7},{7,5},{8,10},{10,8},{9,1... | collective-permute-start | bytes 1081352 | tf_op jit(solution)/shard_map/ppermute | solution.py:32
  335.9 101.1 %collective-permute-start.52 = (bf16[4,2,64,1664]{3,2,1,0:T(8,128)(2,1)}, bf16[4,2,64,1664]{3,2,1,0:T(8,128)(2,1)}, u32[]{:S(2)}, u32[]{:S(2)}) collective-permute-start(bf16[4,2,64,1664]{3,2,1,0:T(8,128)(2,1)} %dynamic-slice_bitcast_fusion), channel_id=1, source_target_pairs={{0,4},{4,0},{1,5},{5,1},{2,6},{6,2},{3,7},{7,3},{8,12},{12,8},{9,1... | collective-permute-start | bytes 5111816 | tf_op jit(solution)/shard_map/ppermute | solution.py:32
  341.0 100.2 %collective-permute-start.54 = (bf16[4,2,64,1664]{3,2,0,1:T(8,128)(2,1)}, bf16[4,2,64,1664]{3,2,0,1:T(8,128)(2,1)}, u32[]{:S(2)}, u32[]{:S(2)}) collective-permute-start(bf16[4,2,64,1664]{3,2,0,1:T(8,128)(2,1)} %bitcast.434), channel_id=1, source_target_pairs={{0,2},{2,0},{1,3},{3,1},{4,6},{6,4},{5,7},{7,5},{8,10},{10,8},{9,1... | collective-permute-start | bytes 5111816 | tf_op jit(solution)/shard_map/ppermute | solution.py:32
  439.8 55.3 %collective-permute-start.53 = (bf16[4,64,1664]{2,1,0:T(8,128)(2,1)}, bf16[4,64,1664]{2,1,0:T(8,128)(2,1)}, u32[]{:S(2)}, u32[]{:S(2)}) collective-permute-start(bf16[4,64,1664]{2,1,0:T(8,128)(2,1)} %dynamic-slice_bitcast_fusion.4), channel_id=1, source_target_pairs={{0,2},{2,0},{1,3},{3,1},{4,6},{6,4},{5,7},{7,5},{8,10},{10,8},{9,1... | collective-permute-start | bytes 2555912 | tf_op jit(solution)/shard_map/ppermute | solution.py:32
  444.2 52.4 %collective-permute-start.55 = (bf16[4,64,1664]{2,1,0:T(8,128)(2,1)}, bf16[4,64,1664]{2,1,0:T(8,128)(2,1)}, u32[]{:S(2)}, u32[]{:S(2)}) collective-permute-start(bf16[4,64,1664]{2,1,0:T(8,128)(2,1)} %dynamic-slice_bitcast_fusion.3), channel_id=1, source_target_pairs={{0,4},{4,0},{1,5},{5,1},{2,6},{6,2},{3,7},{7,3},{8,12},{12,8},{9,1... | collective-permute-start | bytes 2555912 | tf_op jit(solution)/shard_map/ppermute | solution.py:32
  446.9 42.5 %collective-permute-start.45 = (bf16[4,64,768]{2,1,0:T(8,128)(2,1)}, bf16[4,64,768]{2,1,0:T(8,128)(2,1)}, u32[]{:S(2)}, u32[]{:S(2)}) collective-permute-start(bf16[4,64,768]{2,1,0:T(8,128)(2,1)} %dynamic-slice_bitcast_fusion.12), channel_id=1, source_target_pairs={{0,2},{2,0},{1,3},{3,1},{4,6},{6,4},{5,7},{7,5},{8,10},{10,8},{9,1... | collective-permute-start | bytes 1179656 | tf_op jit(solution)/shard_map/ppermute | solution.py:32
  502.3 43.0 %collective-permute-start.57 = (bf16[2,64,1664]{2,1,0:T(8,128)(2,1)}, bf16[2,64,1664]{2,1,0:T(8,128)(2,1)}, u32[]{:S(2)}, u32[]{:S(2)}) collective-permute-start(bf16[2,64,1664]{2,1,0:T(8,128)(2,1)} %get-tuple-element.112), channel_id=1, source_target_pairs={{0,16},{8,24},{16,0},{24,8},{1,17},{9,25},{17,1},{25,9},{2,18},{10... | collective-permute-start | bytes 1277960 | tf_op jit(solution)/shard_map/ppermute | solution.py:32
  503.9 41.3 %collective-permute-start.56 = (bf16[2,64,1664]{2,1,0:T(8,128)(2,1)S(1)}, bf16[2,64,1664]{2,1,0:T(8,128)(2,1)}, u32[]{:S(2)}, u32[]{:S(2)}) collective-permute-start(bf16[2,64,1664]{2,1,0:T(8,128)(2,1)S(1)} %get-tuple-element.111), channel_id=1, source_target_pairs={{0,8},{8,16},{16,24},{24,0},{1,9},{9,17},{17,25},{25,1},{2,10},{10... | collective-permute-start | bytes 1277960 | tf_op jit(solution)/shard_map/ppermute | solution.py:32
  514.4 37.0 %collective-permute-start.51 = (f32[2,32,768]{2,1,0:T(8,128)}, f32[2,32,768]{2,1,0:T(8,128)}, u32[]{:S(2)}, u32[]{:S(2)}) collective-permute-start(f32[2,32,768]{2,1,0:T(8,128)} %dynamic-slice_bitcast_fusion.15), channel_id=1, source_target_pairs={{0,1},{1,0},{2,3},{3,2},{4,5},{5,4},{6,7},{7,6},{8,9},{9,8},{10,11... | collective-permute-start | bytes 589832 | tf_op jit(solution)/shard_map/ppermute | solution.py:27
  (136 other events, 1210.4 us)

commit v2 on v1

v2 whole, which is shorter than its diff:
```python
import functools

import jax
import jax.numpy as jnp
from jax import lax
from jax.experimental import pallas as pl
from jax.experimental.pallas import tpu as pltpu
from jax.sharding import Mesh
from jax.sharding import PartitionSpec as P

D = 1024
H = 8
DK = 128
FF = 2816
CONV = 4
NDOM = 4
EPS = 1e-06
HALO = 16
F32 = jnp.float32
BF16 = jnp.bfloat16
SEQ = ("z", "y")
ALL = ("z", "y", "x", "core")
VMEM_LIMIT = 48 * 1024 * 1024


def swap(a):
    return lax.ppermute(a, "core", [(0, 1), (1, 0)])


def turned(a, axis, by):
    n = lax.axis_size(axis)
    return lax.ppermute(a, axis, [(i, (i + by) % n) for i in range(n)])


def after(a, *others):
    return lax.optimization_barrier((a, others))[0]


def in_place(parts, me):
    n = len(parts)
    if n == 2:
        first = me == 0
        return [jnp.where(first, *parts), jnp.where(first, *parts[::-1])]
    if n <= 4:
        return [lax.select_n((me - i) % n, *parts) for i in range(n)]
    back = parts[:0:-1] + parts[:1]
    wide = jnp.stack(back + back)
    return list(lax.dynamic_slice_in_dim(wide, n - 1 - me, n, axis=0))


def fetched(a, axis):
    return [a] + [turned(a, axis, k) for k in range(1, lax.axis_size(axis))]


def gather_axis(a, axis, dim):
    if lax.axis_size(axis) == 1:
        return jnp.expand_dims(a, dim)
    return jnp.stack(in_place(fetched(a, axis), lax.axis_index(axis)), axis=dim)


def sends(a, axis, dim):
    n, me = lax.axis_size(axis), lax.axis_index(axis)
    own = lax.dynamic_index_in_dim(a, me, dim, False)
    got = [
        turned(lax.dynamic_index_in_dim(a, (me + k) % n, dim, False), axis, k) for k in range(1, n)
    ]
    return own, got


def added(own, got):
    total = own.astype(F32)
    for part in got:
        total = total + part.astype(F32)
    return total


def stacked_near(parts):
    return jnp.stack([a[0] for a in parts]), jnp.stack([a[1] for a in parts])


def gather_near(one, two):
    return fetched(one, "x"), fetched(two, "y")


def gather_last(ones, twos):
    one = jnp.stack(in_place(ones, lax.axis_index("x")))
    two = jnp.stack(in_place(twos, lax.axis_index("y")))
    return fetched(one, "y"), fetched(two, "x")


def gather_end(ones, twos):
    one = jnp.stack(in_place(ones, lax.axis_index("y")))
    two = jnp.stack(in_place(twos, lax.axis_index("x")), axis=1)
    return one, two


def scatter_near(one, two):
    nz, ny, nx = (lax.axis_size(a) for a in ("z", "y", "x"))
    n = one.shape[-1]
    return (
        sends(one.reshape(nz, ny, nx, -1, n), "y", 1),
        sends(two.reshape(nz, ny, nx, -1, n), "x", 2),
    )


def scatter_mid(stage):
    one, two = (added(*s).astype(BF16) for s in stage)
    return sends(one, "x", 1), sends(two, "y", 1)


def scatter_far(stage):
    one, two = (added(*s).astype(BF16) for s in stage)
    return sends(jnp.stack([one, two], axis=1), "z", 0)


def scatter_first(total):
    nz, ny, nx = (lax.axis_size(a) for a in ("z", "y", "x"))
    return sends(total.reshape(nz, ny, nx, -1, total.shape[-1]), "z", 0)


def scatter_second(stage):
    total = added(*stage).astype(BF16)
    n = total.shape[-1] // 2
    return sends(total[..., :n], "x", 1), sends(total[..., n:], "y", 0)


def scatter_third(stage):
    one, two = (added(*s).astype(BF16) for s in stage)
    return sends(one, "y", 0), sends(two, "x", 0)


def core_pick(a, core):
    return (
        lax.dynamic_index_in_dim(a, core, 0, False),
        lax.dynamic_index_in_dim(a, 1 - core, 0, False),
    )


def chip_rows(mine, got, core):
    first = core == 0
    return jnp.concatenate(
        [jnp.where(first, mine, got), jnp.where(first, got, mine)], axis=-2
    )


def own_rows(total, core):
    k, both, n = total.shape
    parts = total.reshape(k, 2, both // 2, n).transpose(1, 0, 2, 3)
    mine, other = core_pick(parts, core)
    got = swap(other)
    first = core == 0
    return jnp.stack([jnp.where(first, mine, got), jnp.where(first, got, mine)], axis=0)


def sum_axis(a, axis):
    every = gather_axis(a, axis, 0)
    total = every[0]
    for k in range(1, every.shape[0]):
        total = total + every[k]
    return total


def dot1(a, b, dims=((1,), (0,))):
    return lax.dot_general(
        a.astype(BF16), b.astype(BF16), (dims, ((), ())), preferred_element_type=F32
    )


TN = ((0,), (0,))
NT = ((1,), (1,))


def split(a):
    high = a.astype(BF16)
    return high, (a - high.astype(F32)).astype(BF16)


def dot3(a, b):
    ah, al = split(a)
    bh, bl = split(b)
    return dot1(ah, bh) + (dot1(ah, bl) + dot1(al, bh))


def sigmoid(v):
    return 1.0 / (1.0 + jnp.exp(-v))


def grid_masks(n):
    i = lax.broadcasted_iota(jnp.int32, (n, n), 0)
    j = lax.broadcasted_iota(jnp.int32, (n, n), 1)
    return i, j


def unit_inverses(lowers, i, j):
    n = lowers[0].shape[0]
    level = jnp.where(i > j, i ^ j, 0)
    eye = jnp.where(i == j, 1.0, 0.0).astype(F32)
    highs = [a.astype(BF16) for a in lowers]
    lows = [(a - h.astype(F32)).astype(BF16) for a, h in zip(lowers, highs)]
    inverses = [eye - jnp.where(level == 1, a, 0.0) for a in lowers]
    size = 2
    while size < n:
        corner = (level >= size) & (level < 2 * size)
        lefts = [t.astype(BF16) for t in inverses]
        inner = [dot1(jnp.where(corner, h, jnp.zeros_like(h)), t) for h, t in zip(highs, lefts)]
        inverses = [t - dot1(b, c) for t, b, c in zip(inverses, lefts, inner)]
        size *= 2
    parts = [split(t) for t in inverses]
    rests = [
        eye - t - (dot1(h, th) + (dot1(h, tl) + dot1(lo, th)))
        for t, h, lo, (th, tl) in zip(inverses, highs, lows, parts)
    ]
    return [t + dot1(th, r) for t, (th, _), r in zip(inverses, parts, rests)]


def conv_of(ext, taps, rows):
    total = taps[0:1, :] * ext[HALO - 3 : HALO - 3 + rows]
    for i in range(1, CONV):
        total = total + taps[i : i + 1, :] * ext[HALO - 3 + i : HALO - 3 + i + rows]
    return total


def first_kernel(half, count, me_ref, *refs):
    parts, refs = refs[:count], refs[count:]
    if half == 0:
        x_ref, g_ref, beta_ref, cv_ref, bias_ref = refs[:5]
        n_ref, w_ref, pre_ref, qkv_ref, t_ref, wu_ref, pd_ref, b_ref, sem = refs[5:]
    else:
        n_ref, beta_ref, cv_ref, bias_ref = refs[:4]
        w_ref, pre_ref, qkv_ref, t_ref, wu_ref, pd_ref, b_ref, sem = refs[-8:]
    rows = qkv_ref.shape[1] // 2
    frame = rows + HALO
    copies = []
    for k, part in enumerate(parts):
        place = lax.rem(me_ref[half] + (count - k), count)
        inner = part.shape[0]
        for i in range(inner):
            to = w_ref.at[:, place, i] if half == 0 else w_ref.at[:, i, place]
            copies.append(pltpu.make_async_copy(part.at[i], to, sem.at[k * inner + i]))
            copies[-1].start()
    if half == 0:
        x = x_ref[...].astype(F32)
        scale = lax.rsqrt(jnp.mean(x * x, axis=-1, keepdims=True) + EPS)
        n_ref[...] = (x * scale * g_ref[...]).astype(BF16)
    normed = n_ref[...]
    for copy in copies:
        copy.wait()
    pre_ref[0] = dot1(normed, w_ref[...].reshape(D, 768)).astype(BF16)
    linear = dot1(normed, beta_ref[0])
    i, j = grid_masks(rows)
    keys, rights, lowers = [], [], []
    for q in range(2):
        rate = sigmoid(linear[q * frame + HALO : (q + 1) * frame] + bias_ref[0, q : q + 1, :])
        b_ref[0, q * rows : (q + 1) * rows, :] = rate
        ext = pre_ref[0, q * frame : (q + 1) * frame, :].astype(F32)
        conv = conv_of(ext, cv_ref[0], rows)
        act = conv * sigmoid(conv)
        for h in range(2):
            place = pl.ds(q * rows, rows)
            parts = []
            for kind in range(3):
                lane = (kind * 2 + h) * DK
                one = act[:, lane : lane + DK]
                if kind < 2:
                    one = one * lax.rsqrt(jnp.sum(one * one, axis=-1, keepdims=True) + EPS)
                if kind == 0:
                    one = one * DK ** (-0.5)
                one = one.astype(BF16)
                qkv_ref[0, place, lane : lane + DK] = one
                parts.append(one)
            key, value = parts[1], parts[2]
            col = rate[:, h : h + 1]
            keys.append(key)
            rights.append(jnp.concatenate([key, value], axis=1).astype(F32) * col)
            lowers.append(jnp.where(i > j, dot1(key, key, NT) * col, 0.0))
    inverses = unit_inverses(lowers, i, j)
    boths = [dot3(t, r) for t, r in zip(inverses, rights)]
    for p in range(4):
        t_ref[0, p] = inverses[p].astype(BF16)
        wu_ref[0, p] = boths[p].astype(BF16)
    for p in range(4):
        pd_ref[0, p] = dot1(keys[p], boths[p], TN).astype(BF16)


def state_kernel(pd_ref, s_ref):
    count = pd_ref.shape[0]
    state = jnp.zeros((DK, DK), F32)
    for s in range(count):
        s_ref[s] = state.astype(BF16)
        if s + 1 < count:
            high, low = split(state)
            move = pd_ref[s, :, :DK]
            state = state - (dot1(move, high) + dot1(move, low)) + pd_ref[s, :, DK:].astype(F32)


def adjoint_kernel(pd_ref, g_ref, l_ref):
    count = pd_ref.shape[0]
    adjoint = jnp.zeros((DK, DK), F32)
    for s in range(count - 1, -1, -1):
        l_ref[s] = adjoint.astype(BF16)
        if s > 0:
            high, low = split(adjoint)
            move = pd_ref[s, :, :DK]
            adjoint = (
                adjoint - (dot1(move, high, TN) + dot1(move, low, TN)) + g_ref[s].astype(F32)
            )


def pair_places(rows):
    return [
        (q * 2 + h, pl.ds(q * rows, rows), pl.ds(h * DK, DK), h) for q in range(2) for h in range(2)
    ]


def kind_lanes(kind, h):
    return pl.ds((kind * 2 + h) * DK, DK)


def second_kernel(qkv_ref, wu_ref, s_ref, hg_ref, f_ref, m_ref, h_ref):
    rows = qkv_ref.shape[1] // 2
    i, j = grid_masks(rows)
    pairs = pair_places(rows)
    queries = [qkv_ref[0, at, kind_lanes(0, h)] for _, at, _, h in pairs]
    keys = [qkv_ref[0, at, kind_lanes(1, h)] for _, at, _, h in pairs]
    scores = [jnp.where(i >= j, dot1(a, b, NT), 0.0).astype(BF16) for a, b in zip(queries, keys)]
    freshes = [
        (wu_ref[0, p, :, DK:].astype(F32) - dot1(wu_ref[0, p, :, :DK], s_ref[p])).astype(BF16)
        for p, _, _, _ in pairs
    ]
    mixes = [
        dot1(queries[p], s_ref[p]) + dot1(scores[p], freshes[p]) for p, _, _, _ in pairs
    ]
    for p, at, lanes, _ in pairs:
        mixed = mixes[p]
        scale = lax.rsqrt(jnp.mean(mixed * mixed, axis=-1, keepdims=True) + EPS)
        f_ref[at, lanes] = freshes[p]
        m_ref[at, lanes] = mixed
        h_ref[at, lanes] = (mixed * scale * hg_ref[...]).astype(BF16)


def third_kernel(qkv_ref, wu_ref, s_ref, f_ref, m_ref, dh_ref, hg_ref, sg_ref, gf_ref, gq_ref, gk_ref, ghg_ref):
    rows = qkv_ref.shape[1] // 2
    i, j = grid_masks(rows)
    gain = hg_ref[...]
    gain_grad = jnp.zeros((1, DK), F32)
    pairs = pair_places(rows)
    queries = [qkv_ref[0, at, kind_lanes(0, h)] for _, at, _, h in pairs]
    keys = [qkv_ref[0, at, kind_lanes(1, h)] for _, at, _, h in pairs]
    scores = [jnp.where(i >= j, dot1(a, b, NT), 0.0).astype(BF16) for a, b in zip(queries, keys)]
    grads = []
    for _, at, lanes, _ in pairs:
        mixed = m_ref[at, lanes]
        up = dh_ref[at, lanes].astype(F32)
        scale = lax.rsqrt(jnp.mean(mixed * mixed, axis=-1, keepdims=True) + EPS)
        unit = mixed * scale
        gain_grad = gain_grad + jnp.sum(up * unit, axis=0, keepdims=True)
        inner = up * gain
        grad = scale * (inner - unit * jnp.mean(inner * unit, axis=-1, keepdims=True))
        grads.append(grad.astype(BF16))
    ghg_ref[0] = jnp.broadcast_to(gain_grad, ghg_ref.shape[1:])
    fresh_grads = [dot1(a, g, TN) for a, g in zip(scores, grads)]
    starts = [
        dot1(queries[p], grads[p], TN) - dot1(wu_ref[0, p, :, :DK], fresh_grads[p], TN)
        for p in range(4)
    ]
    score_grads = [
        jnp.where(i >= j, dot1(grads[p], f_ref[at, lanes], NT), 0.0).astype(BF16)
        for p, at, lanes, _ in pairs
    ]
    for p, at, lanes, _ in pairs:
        gf_ref[at, lanes] = fresh_grads[p]
        sg_ref[0, p] = starts[p].astype(BF16)
        gq_ref[at, lanes] = dot1(grads[p], s_ref[p], NT) + dot1(score_grads[p], keys[p])
        gk_ref[at, lanes] = dot1(score_grads[p], queries[p], TN)


def fourth_kernel(qkv_ref, pre_ref, cv_ref, b_ref, t_ref, wu_ref, s_ref, l_ref, f_ref, gf_ref, gq_ref, gk_ref, eg_ref, gc_ref, lg_ref, gb_ref):
    rows = qkv_ref.shape[1] // 2
    frame = rows + HALO
    i, j = grid_masks(rows)
    lane = lax.broadcasted_iota(jnp.int32, (rows, DK), 1)
    pairs = pair_places(rows)
    keys = [qkv_ref[0, at, kind_lanes(1, h)] for _, at, _, h in pairs]
    values = [qkv_ref[0, at, kind_lanes(2, h)] for _, at, _, h in pairs]
    cols = [b_ref[0, at, h : h + 1] for _, at, _, h in pairs]
    fresh_grads = [
        gf_ref[at, lanes] + dot1(keys[p], l_ref[p]) for p, at, lanes, _ in pairs
    ]
    lows = [g.astype(BF16) for g in fresh_grads]
    factor_grads = [
        jnp.concatenate([-dot1(lows[p], s_ref[p], NT).astype(BF16), lows[p]], axis=1)
        for p in range(4)
    ]
    solved = [dot1(t_ref[0, p], factor_grads[p], TN) for p in range(4)]
    inners = [dot1(k, k, NT) for k in keys]
    system_grads = [
        jnp.where(i > j, -dot1(solved[p], wu_ref[0, p], NT), 0.0) for p in range(4)
    ]
    inner_grads = [(g * c).astype(BF16) for g, c in zip(system_grads, cols)]
    key_grads = [
        gk_ref[at, lanes]
        + dot1(f_ref[at, lanes], l_ref[p], NT)
        + cols[p] * solved[p][:, :DK]
        + dot1(inner_grads[p], keys[p])
        + dot1(inner_grads[p], keys[p], TN)
        for p, at, lanes, _ in pairs
    ]
    rate_grads = [
        (
            jnp.sum(
                solved[p][:, :DK] * keys[p].astype(F32) + solved[p][:, DK:] * values[p].astype(F32),
                axis=-1,
                keepdims=True,
            )
            + jnp.sum(system_grads[p] * inners[p], axis=-1, keepdims=True)
        )
        * cols[p]
        * (1.0 - cols[p])
        for p in range(4)
    ]
    for q in range(2):
        place = pl.ds(q * rows, rows)
        logit = jnp.where(
            lane == 0, rate_grads[2 * q], jnp.where(lane == 1, rate_grads[2 * q + 1], 0.0)
        )
        lg_ref[0, place, :] = logit.astype(BF16)
        gb_ref[0, q : q + 1, :] = jnp.sum(logit, axis=0, keepdims=True)
    zero = jnp.zeros((HALO, DK), F32)
    for kind in range(3):
        for h in range(2):
            at = kind_lanes(kind, h)
            tap = cv_ref[0, :, at]
            conv_grad = [jnp.zeros((1, DK), F32) for _ in range(CONV)]
            for q in range(2):
                p = q * 2 + h
                ext = pre_ref[0, q * frame : (q + 1) * frame, at].astype(F32)
                views = [ext[HALO - 3 + t : HALO - 3 + t + rows] for t in range(CONV)]
                conv = tap[0:1, :] * views[0]
                for t in range(1, CONV):
                    conv = conv + tap[t : t + 1, :] * views[t]
                sig = sigmoid(conv)
                act = conv * sig
                if kind == 0:
                    grad = gq_ref[q * rows : (q + 1) * rows, h * DK : (h + 1) * DK] * DK ** (-0.5)
                elif kind == 1:
                    grad = key_grads[p]
                else:
                    grad = cols[p] * solved[p][:, DK:]
                if kind < 2:
                    scale = lax.rsqrt(jnp.sum(act * act, axis=-1, keepdims=True) + EPS)
                    unit = act * scale
                    grad = scale * (grad - unit * jnp.sum(grad * unit, axis=-1, keepdims=True))
                grad = grad * (sig * (1.0 + conv * (1.0 - sig)))
                wide = jnp.concatenate([zero, grad, zero], axis=0)
                total = tap[0:1, :] * wide[3 : 3 + frame]
                for t in range(1, CONV):
                    total = total + tap[t : t + 1, :] * wide[3 - t : 3 - t + frame]
                eg_ref[0, q * frame : (q + 1) * frame, at] = total.astype(BF16)
                for t in range(CONV):
                    conv_grad[t] = conv_grad[t] + jnp.sum(grad * views[t], axis=0, keepdims=True)
            for t in range(CONV):
                gc_ref[0, t : t + 1, at] = conv_grad[t]


def lead(*shape):
    return pl.BlockSpec((1,) + shape, lambda p: (p,) + (0,) * len(shape))


def at_half(half, *shape):
    return pl.BlockSpec((1,) + shape, lambda p: (half,) + (0,) * len(shape))


def whole(*shape):
    return pl.BlockSpec(shape, lambda p: (0,) * len(shape))


def columns(rows, cols):
    return pl.BlockSpec((rows, cols), lambda p: (0, p))


def quarter():
    return pl.BlockSpec((4, DK, DK), lambda p: (p, 0, 0))


def cost(microseconds):
    return pl.CostEstimate(
        flops=int(microseconds * 1.15e9), bytes_accessed=0, transcendentals=0
    )


def on_core(kernel, outs, in_specs, out_specs, name, microseconds):
    return pl.pallas_call(
        kernel,
        out_shape=outs,
        grid=(2,),
        in_specs=in_specs,
        out_specs=out_specs,
        compiler_params=pltpu.CompilerParams(
            vmem_limit_bytes=VMEM_LIMIT, dimension_semantics=("arbitrary",)
        ),
        cost_estimate=cost(microseconds),
        name=name,
    )


def sds(shape, kind):
    return jax.ShapeDtypeStruct(shape, kind)


def all_ranges(a):
    if lax.axis_size("z") * lax.axis_size("y") == a.shape[0]:
        return lax.all_to_all(a, SEQ, 0, 0, tiled=True)
    return lax.all_gather(a, SEQ)


def scan_states(every):
    count = lax.axis_size("z") * lax.axis_size("y")
    if every.ndim == 3:
        return pl.pallas_call(
            state_kernel,
            out_shape=sds((count, DK, DK), BF16),
            cost_estimate=cost(3),
            name="state_scan",
        )(every)

    def step(s, state):
        one = lax.dynamic_index_in_dim(every, s, 0, False).astype(F32)
        moved = jnp.einsum(
            "pij,pjk->pik", one[:, :, :DK], state, precision=lax.Precision.HIGHEST
        )
        return state - moved + one[:, :, DK:]

    start = jnp.zeros((every.shape[1], DK, DK), F32)
    return lax.fori_loop(0, lax.axis_index(SEQ), step, start).astype(BF16)


def scan_adjoints(every, grads):
    count = lax.axis_size("z") * lax.axis_size("y")
    if every.ndim == 3:
        return pl.pallas_call(
            adjoint_kernel,
            out_shape=sds((count, DK, DK), BF16),
            cost_estimate=cost(3),
            name="adjoint_scan",
        )(every, grads)

    def step(k, adjoint):
        s = count - 1 - k
        one = lax.dynamic_index_in_dim(every, s, 0, False).astype(F32)
        moved = jnp.einsum(
            "pji,pjk->pik", one[:, :, :DK], adjoint, precision=lax.Precision.HIGHEST
        )
        return adjoint - moved + lax.dynamic_index_in_dim(grads, s, 0, False).astype(F32)

    start = jnp.zeros((every.shape[1], DK, DK), F32)
    steps = count - 1 - lax.axis_index(SEQ)
    return lax.fori_loop(0, steps, step, start).astype(BF16)


def own_range(a):
    if lax.axis_size("z") * lax.axis_size("y") == H:
        return lax.all_to_all(a, SEQ, 0, 0, tiled=True)
    return a


def shards(
    inputs,
    domain_ids,
    norm1_gain,
    w_qkv,
    w_beta,
    conv_weight,
    domain_bias,
    head_gain,
    w_out,
    norm2_gain,
    w_gate_up,
    w_down,
    cotangent,
):
    core = lax.axis_index("core")
    nz, ny, nx = (lax.axis_size(a) for a in ("z", "y", "x"))
    z, y, x = (lax.axis_index(a) for a in ("z", "y", "x"))
    chips = nz * ny * nx
    seq_devices = nz * ny
    rows = inputs.shape[1]
    frame = rows + HALO
    tall = 2 * rows
    drows = w_qkv.shape[0]
    both_rows = 2 * drows
    frows = w_down.shape[0]
    grows = conv_weight.shape[0]
    first = core == 0
    half = H // 2
    fence = lax.optimization_barrier

    q_mine, q_other = core_pick(
        w_qkv.reshape(drows, 3, 2, 2, 256).transpose(2, 3, 0, 1, 4).reshape(2, 2, drows, 768), core
    )
    q_got = swap(q_other)
    small = jnp.concatenate(
        [norm1_gain, norm2_gain, w_beta.reshape(-1), conv_weight.reshape(-1)]
    )
    n_small = small.shape[0]
    small = jnp.pad(small, (0, 768 - n_small)).reshape(1, 768)
    small_got = swap(small)
    x_own = inputs.reshape(rows, D)
    halo = lax.ppermute(
        x_own[rows - HALO :], SEQ, [(i, i + 1) for i in range(seq_devices - 1)]
    )
    small = jnp.stack([jnp.where(first, small, small_got), jnp.where(first, small_got, small)])
    small = jnp.pad(small, ((0, 0), (0, 7), (0, 0)))
    q_part = jnp.concatenate([chip_rows(q_mine, q_got, core), small], axis=1)
    q_part, halo, x_own, w_gate_up, w_out, w_down, cotangent = fence(
        (q_part, halo, x_own, w_gate_up, w_out, w_down, cotangent)
    )

    q_far = fetched(q_part, "z")
    down_ones, down_twos = gather_last(
        *gather_near(w_down[:, : D // 2], w_down[:, D // 2 :])
    )
    out_cols = w_out.reshape(drows, 2, 2, 256).transpose(1, 2, 0, 3)
    gu_cols = (
        w_gate_up.reshape(drows, 2, chips, 2, frows)
        .transpose(3, 1, 0, 2, 4)
        .reshape(2, 2, drows, FF // 2)
    )
    gu_mine, gu_other = core_pick(jnp.concatenate([gu_cols, out_cols], axis=-1), core)
    gu_part = chip_rows(gu_mine, swap(gu_other), core)
    choose = (domain_ids[0] == jnp.arange(NDOM, dtype=jnp.int32)).astype(BF16)
    bias_own = jnp.sum(domain_bias.astype(F32) * choose.astype(F32)[:, None], axis=0)
    extra = jnp.pad(jnp.concatenate([bias_own.astype(BF16), choose]), (0, D - H - NDOM))
    extra = jnp.pad(extra.reshape(1, D), ((0, HALO - 1), (0, 0)))
    frame_own = jnp.concatenate([halo, x_own, extra], axis=0)
    frame_other = swap(frame_own)
    g_own = cotangent.reshape(rows, D)
    g_other = swap(g_own)
    q_far, gu_part, frame_own, frame_other, g_own, g_other = fence(
        (q_far, gu_part, frame_own, frame_other, g_own, g_other)
    )

    q_sorted = in_place(q_far, z)
    q_ones, q_twos = gather_near(*stacked_near([a[:, :both_rows] for a in q_sorted]))
    smalls = jnp.stack([a[:, both_rows] for a in q_sorted])
    smalls = gather_axis(gather_axis(smalls, "x", 1), "y", 1)
    ends = sorted({1, nz - 1})
    gu_ends = [turned(gu_part, "z", k) for k in ends]
    q_ones, q_twos, smalls, gu_part = fence((q_ones, q_twos, smalls, gu_part))

    q_ones, q_twos = gather_last(q_ones, q_twos)
    gu_far = [gu_part, gu_ends[0]]
    gu_far += [turned(gu_part, "z", k) for k in range(2, nz - 1)]
    gu_far += gu_ends[1:]
    smalls = smalls.reshape(2 * chips, 768)[:, :n_small]
    gain_one = smalls[:, :drows].reshape(1, D).astype(F32)
    gain_two = smalls[:, drows : 2 * drows].reshape(1, D).astype(F32)
    full_beta = smalls[:, 2 * drows : 2 * drows + drows * H].reshape(D, 2, half)
    full_conv = smalls[:, 2 * drows + drows * H :].reshape(3, 2, 2, 256, CONV)
    beta_mine = lax.dynamic_index_in_dim(full_beta, core, 1, False)
    conv_mine = (
        lax.dynamic_index_in_dim(full_conv, core, 1, False)
        .transpose(1, 3, 0, 2)
        .reshape(2, CONV, 768)
        .astype(F32)
    )
    beta_pairs = jnp.pad(
        beta_mine.reshape(D, 2, 2).transpose(1, 0, 2), ((0, 0), (0, 0), (0, DK - 2))
    )
    x_frames = jnp.concatenate([frame_own[:frame], frame_other[:frame]], axis=0)
    bias_both = jnp.stack([frame_own[frame, :H], frame_other[frame, :H]]).astype(F32)
    choose_both = jnp.stack(
        [frame_own[frame, H : H + NDOM], frame_other[frame, H : H + NDOM]]
    ).astype(F32)
    bias_mine = lax.dynamic_index_in_dim(bias_both.reshape(2, 2, half), core, 1, False)
    bias_pairs = jnp.pad(
        bias_mine.reshape(2, 2, 2).transpose(1, 0, 2), ((0, 0), (0, 0), (0, DK - 2))
    )
    x_both = jnp.concatenate(
        [frame_own[HALO:frame], frame_other[HALO:frame]], axis=0
    ).astype(F32)
    g_both = jnp.concatenate([g_own, g_other], axis=0)
    (
        q_ones,
        q_twos,
        gu_far,
        gain_one,
        gain_two,
        beta_pairs,
        conv_mine,
        bias_pairs,
        x_frames,
        x_both,
        g_both,
        down_ones,
        down_twos,
    ) = fence(
        (
            q_ones,
            q_twos,
            gu_far,
            gain_one,
            gain_two,
            beta_pairs,
            conv_mine,
            bias_pairs,
            x_frames,
            x_both,
            g_both,
            down_ones,
            down_twos,
        )
    )

    if both_rows % 16 == 0:
        w_shape = sds((nz, ny, nx, both_rows, 768), BF16)
    else:
        w_shape = sds((1, 1, 1, D, 768), BF16)
        q_ones, q_twos = (
            [a.transpose(2, 0, 1, 3, 4).reshape(1, 1, D, 768)] for a in gather_end(q_ones, q_twos)
        )
    place = jnp.stack([y, x]).astype(jnp.int32)
    kept = (
        sds((2, 2 * frame, 768), BF16),
        sds((2, tall, 768), BF16),
        sds((2, 4, rows, rows), BF16),
        sds((2, 4, rows, 2 * DK), BF16),
        sds((2, 4, DK, 2 * DK), BF16),
        sds((2, tall, DK), F32),
    )
    anywhere = pl.BlockSpec(memory_space=pl.ANY)

    def local(number, parts, ins, in_specs, outs, out_specs, held):
        fixed = [at_half(number, D, DK), at_half(number, CONV, 768), at_half(number, 2, DK)]
        first_held = 1 + len(parts) + len(ins) + 3
        return pl.pallas_call(
            functools.partial(first_kernel, number, len(parts)),
            out_shape=outs + (w_shape,) + kept,
            grid=(1,),
            in_specs=[pl.BlockSpec(memory_space=pltpu.SMEM)]
            + [anywhere] * len(parts)
            + in_specs
            + fixed
            + [anywhere] * len(held),
            out_specs=out_specs
            + (whole(*w_shape.shape),)
            + tuple(at_half(number, *k.shape[1:]) for k in kept),
            scratch_shapes=[pltpu.SemaphoreType.DMA((len(parts) * parts[0].shape[0],))],
            input_output_aliases={
                first_held + k: len(outs) + 1 + k for k in range(len(held))
            },
            compiler_params=pltpu.CompilerParams(vmem_limit_bytes=VMEM_LIMIT),
            cost_estimate=cost(10),
            name="delta_local",
        )(place, *parts, *ins, beta_pairs, conv_mine, bias_pairs, *held)

    gu_stacks = stacked_near(in_place(gu_far, z))
    gu_ones, gu_twos = gather_near(*gu_stacks)
    down_part = jnp.concatenate(gather_end(down_ones, down_twos), axis=-1)
    down_ends = [turned(down_part, "z", k) for k in ends]
    normed, w_q_one, *held = local(
        0,
        q_ones,
        (after(x_frames, gu_stacks, down_part), gain_one),
        [whole(2 * frame, D), whole(1, D)],
        (sds((2 * frame, D), BF16),),
        (whole(2 * frame, D),),
        (),
    )
    w_q_two, *held = local(
        1,
        q_twos,
        (normed,),
        [whole(2 * frame, D)],
        (),
        (),
        tuple(held),
    )
    pre, qkv, inverse, factors, pd, rates = held
    w_q_one = w_q_one.reshape(D, 768)
    w_q_two = w_q_two.reshape(D, 768)
    (
        normed,
        w_q_one,
        w_q_two,
        pre,
        qkv,
        inverse,
        factors,
        pd,
        rates,
        gu_ones,
        gu_twos,
        down_part,
        down_ends[0],
    ) = fence(
        (
            normed,
            w_q_one,
            w_q_two,
            pre,
            qkv,
            inverse,
            factors,
            pd,
            rates,
            gu_ones,
            gu_twos,
            down_part,
            down_ends[0],
        )
    )

    every = all_ranges(pd.reshape(H, DK, 2 * DK))
    gu_ones, gu_twos = gather_last(gu_ones, gu_twos)
    every, down_ends = fence((every, down_ends))

    states = scan_states(every)
    down_part = after(down_part, states)
    down_far = [down_part, down_ends[0]]
    down_far += [turned(down_part, "z", k) for k in range(2, nz - 1)]
    down_far += down_ends[1:]
    states = own_range(states)
    gain_head = head_gain.astype(F32).reshape(1, DK)
    fresh, mixed, heads_mine = on_core(
        second_kernel,
        (sds((tall, 512), BF16), sds((tall, 512), F32), sds((tall, 512), BF16)),
        [lead(tall, 768), lead(4, rows, 2 * DK), quarter(), whole(1, DK)],
        (columns(tall, 256), columns(tall, 256), columns(tall, 256)),
        "delta_mix",
        2,
    )(qkv, factors, states, gain_head)
    heads_got = swap(heads_mine)
    gu_ones, gu_twos, down_far, states, fresh, mixed, heads_mine, heads_got = fence(
        (gu_ones, gu_twos, down_far, states, fresh, mixed, heads_mine, heads_got)
    )

    gu_one, gu_two = (
        a.transpose(2, 0, 1, 3, 4).reshape(D, -1) for a in gather_end(gu_ones, gu_twos)
    )
    w_gate, w_up = gu_one[:, : FF // 2], gu_two[:, : FF // 2]
    out_mine = jnp.concatenate([gu_one[:, FF // 2 :], gu_two[:, FF // 2 :]], axis=1)
    out_got = swap(out_mine)
    full_out = jnp.concatenate(
        [jnp.where(first, out_mine, out_got), jnp.where(first, out_got, out_mine)], axis=1
    )
    heads_got = jnp.concatenate([heads_got[rows:], heads_got[:rows]], axis=0)
    heads = jnp.concatenate(
        [jnp.where(first, heads_mine, heads_got), jnp.where(first, heads_got, heads_mine)], axis=1
    )
    middle = x_both + jnp.dot(heads, full_out, preferred_element_type=F32)
    scale_two = lax.rsqrt(jnp.mean(middle * middle, axis=-1, keepdims=True) + EPS)
    unit_two = middle * scale_two
    normed_two = (unit_two * gain_two).astype(BF16)
    gate = jnp.dot(normed_two, w_gate, preferred_element_type=F32)
    up = jnp.dot(normed_two, w_up, preferred_element_type=F32)
    w_down_mine = jnp.stack(in_place(after(down_far, gate, up), z)).reshape(chips * frows, D)
    sig = jax.nn.sigmoid(gate)
    hidden = (gate * sig * up).astype(BF16)
    hidden_grad = jnp.einsum("nd,fd->nf", g_both, w_down_mine, preferred_element_type=F32)
    up_grad = (hidden_grad * gate * sig).astype(BF16)
    gate_grad = (hidden_grad * up * sig * (1.0 + gate * (1.0 - sig))).astype(BF16)
    hidden, up_grad, gate_grad = fence((hidden, up_grad, gate_grad))

    normed_two_part = jnp.einsum(
        "nf,df->nd", gate_grad, w_gate, preferred_element_type=F32
    ) + jnp.einsum("nf,df->nd", up_grad, w_up, preferred_element_type=F32)
    part_low = normed_two_part.astype(BF16)
    part_got = swap(part_low)
    grad_down = jnp.einsum(
        "nf,nd->fd", after(hidden, part_low), g_both, preferred_element_type=F32
    ).astype(BF16)
    down_stage = scatter_near(grad_down[:, : D // 2], grad_down[:, D // 2 :])
    rows_two = after(normed_two, grad_down)
    grad_gate = jnp.einsum("nd,nf->df", rows_two, gate_grad, preferred_element_type=F32)
    grad_up = jnp.einsum("nd,nf->df", rows_two, up_grad, preferred_element_type=F32)
    grad_gate, grad_up = grad_gate.astype(BF16), grad_up.astype(BF16)
    part_got = after(part_got, grad_gate, grad_up)
    part_got = jnp.concatenate([part_got[rows:], part_got[:rows]], axis=0)
    normed_two_grad = normed_two_part + part_got.astype(F32)
    grad_norm2 = jnp.sum(normed_two_grad[:rows] * unit_two[:rows], axis=0)
    inner = normed_two_grad * gain_two
    middle_grad = g_both.astype(F32) + scale_two * (
        inner - unit_two * jnp.mean(inner * unit_two, axis=-1, keepdims=True)
    )
    middle_low = middle_grad.astype(BF16)
    out_rows = lax.dynamic_slice_in_dim(full_out, core * 512, 512, 0)
    heads_grad = jnp.einsum("ne,de->nd", middle_low, out_rows, preferred_element_type=F32)
    start_grad, fresh_grad, query_grad, key_grad, gain_part = on_core(
        third_kernel,
        (
            sds((2, 4, DK, DK), BF16),
            sds((tall, 512), F32),
            sds((tall, 512), F32),
            sds((tall, 512), F32),
            sds((2, 8, DK), F32),
        ),
        [
            lead(tall, 768),
            lead(4, rows, 2 * DK),
            quarter(),
            columns(tall, 256),
            columns(tall, 256),
            columns(tall, 256),
            whole(1, DK),
        ],
        (
            lead(4, DK, DK),
            columns(tall, 256),
            columns(tall, 256),
            columns(tall, 256),
            lead(8, DK),
        ),
        "delta_back_local",
        5,
    )(qkv, factors, states, fresh, mixed, heads_grad, gain_head)
    (
        start_grad,
        fresh_grad,
        query_grad,
        key_grad,
        gain_part,
        down_stage,
        grad_gate,
        grad_up,
        grad_norm2,
        middle_grad,
        middle_low,
        hidden,
    ) = fence(
        (
            start_grad,
            fresh_grad,
            query_grad,
            key_grad,
            gain_part,
            down_stage,
            grad_gate,
            grad_up,
            grad_norm2,
            middle_grad[:rows],
            middle_low,
            hidden,
        )
    )

    start_grads = all_ranges(start_grad.reshape(H, DK, DK))
    down_stage = scatter_mid(down_stage)
    gu_stage = scatter_near(grad_gate, grad_up)
    low_cols = lax.dynamic_slice_in_dim(middle_low, core * 512, 512, 1)
    grad_out = jnp.einsum("nd,ne->de", heads, low_cols, preferred_element_type=F32).astype(BF16)
    adjoints = scan_adjoints(every, start_grads)
    gu_stage = scatter_mid(after(gu_stage, adjoints))
    adjoints = own_range(adjoints)
    down_part = jnp.dot(hidden, w_down_mine, preferred_element_type=F32)
    output = (middle[:rows] + down_part[:rows]) + swap(down_part[rows:].astype(BF16)).astype(F32)
    output = output.astype(BF16).reshape(1, rows, D)
    adjoints = after(adjoints, gu_stage[0][0], gu_stage[1][0], grad_out, output)
    down_stage = scatter_far(after(down_stage, adjoints))
    out_stage = scatter_first(after(grad_out, adjoints))
    adjoints = after(adjoints, down_stage[0], out_stage[0])
    ext_grad, conv_part, logit_low, bias_part = on_core(
        fourth_kernel,
        (
            sds((2, 2 * frame, 768), BF16),
            sds((2, CONV, 768), F32),
            sds((2, tall, DK), BF16),
            sds((2, 2, DK), F32),
        ),
        [
            lead(tall, 768),
            lead(2 * frame, 768),
            lead(CONV, 768),
            lead(tall, DK),
            lead(4, rows, rows),
            lead(4, rows, 2 * DK),
            quarter(),
            quarter(),
            columns(tall, 256),
            columns(tall, 256),
            columns(tall, 256),
            columns(tall, 256),
        ],
        (lead(2 * frame, 768), lead(CONV, 768), lead(tall, DK), lead(2, DK)),
        "delta_back",
        15,
    )(qkv, pre, conv_mine, rates, inverse, factors, states, adjoints, fresh, fresh_grad, query_grad, key_grad)
    ext_grad, conv_part, logit_low, bias_part, gu_stage, down_stage, out_stage = fence(
        (ext_grad, conv_part, logit_low, bias_part, gu_stage, down_stage, out_stage)
    )

    ext_frames = ext_grad.reshape(2, 2, frame, 768)
    grad_q = [
        jnp.einsum("nd,nf->df", normed, e, preferred_element_type=F32).astype(BF16)
        for e in (ext_grad[0], ext_grad[1])
    ]
    q_stage = scatter_near(*grad_q)
    ext_frames = after(ext_frames, grad_q)
    sent_back = lax.ppermute(
        ext_frames[:, :, :HALO], SEQ, [(i + 1, i) for i in range(seq_devices - 1)]
    )
    gu_stage = scatter_far(gu_stage)
    out_stage = scatter_second(after(out_stage, grad_q))
    tail = ext_frames[:, :, frame - HALO :].astype(F32) + sent_back.astype(F32)
    pre_low = jnp.concatenate(
        [ext_frames[:, :, HALO : frame - HALO], tail.astype(BF16)], axis=2
    ).reshape(2, tall, 768)
    normed_part = (
        jnp.einsum("nf,df->nd", pre_low[0], w_q_one, preferred_element_type=F32)
        + jnp.einsum("nf,df->nd", pre_low[1], w_q_two, preferred_element_type=F32)
        + jnp.einsum("pnh,pdh->nd", logit_low, beta_pairs, preferred_element_type=F32)
    )
    normed_grad = normed_part[:rows] + swap(normed_part[rows:].astype(BF16)).astype(F32)
    normed_tokens = normed.reshape(2, frame, D)[:, HALO:].reshape(tall, D)
    grad_beta = jnp.einsum(
        "nd,pnh->dph", normed_tokens, logit_low[:, :, :2], preferred_element_type=F32
    ).reshape(D, half)
    q_stage, out_stage, normed_grad, grad_beta, x_both = fence(
        (q_stage, out_stage, normed_grad, grad_beta, x_both)
    )

    q_stage = scatter_mid(q_stage)
    out_stage = scatter_third(out_stage)
    x32 = x_both[:rows]
    scale_one = lax.rsqrt(jnp.mean(x32 * x32, axis=-1, keepdims=True) + EPS)
    unit_one = x32 * scale_one
    grad_norm1 = jnp.sum(normed_grad * unit_one, axis=0)
    inner_one = normed_grad * gain_one
    grad_input = middle_grad + scale_one * (
        inner_one - unit_one * jnp.mean(inner_one * unit_one, axis=-1, keepdims=True)
    )
    grad_input = grad_input.reshape(1, rows, D)
    beta_full = jnp.where(
        first,
        jnp.pad(grad_beta, ((0, 0), (0, half))),
        jnp.pad(grad_beta, ((0, 0), (half, 0))),
    )
    conv_cols = conv_part.reshape(2, CONV, 3, 256).transpose(2, 0, 3, 1).reshape(3, 512, CONV)
    conv_full = jnp.where(
        first,
        jnp.pad(conv_cols, ((0, 0), (0, 512), (0, 0))),
        jnp.pad(conv_cols, ((0, 0), (512, 0), (0, 0))),
    )
    bias_heads = bias_part[:, :, :2].transpose(1, 0, 2).reshape(2, half)
    bias_heads = jnp.where(
        first,
        jnp.pad(bias_heads, ((0, 0), (0, half))),
        jnp.pad(bias_heads, ((0, 0), (half, 0))),
    )
    bias_grad = jnp.sum(choose_both[:, :, None] * bias_heads[:, None, :], axis=0)
    head_grad = gain_part[0, 0] + gain_part[1, 0]
    pack = jnp.concatenate(
        [
            grad_norm1,
            grad_norm2,
            beta_full.reshape(-1),
            conv_full.reshape(-1),
            bias_grad.reshape(-1),
            head_grad,
        ]
    )
    pack = jnp.pad(pack, (0, -pack.shape[0] % 1024)).reshape(-1, DK)
    pack = sum_axis(pack + swap(pack), "x")
    q_stage, gu_stage, out_stage, pack, grad_input = fence(
        (q_stage, gu_stage, out_stage, pack, grad_input)
    )

    q_stage = scatter_far(q_stage)
    pack = sum_axis(pack, "y")
    gu_own = own_rows(added(*gu_stage), core)
    own_gu = (
        gu_own.reshape(2, 2, drows, chips, frows).transpose(2, 1, 3, 0, 4).reshape(drows, 2 * FF)
    )
    own_down = added(*down_stage).transpose(1, 0, 2).reshape(frows, D)
    out_total = jnp.concatenate([added(*s) for s in out_stage], axis=-1)
    out_own = own_rows(out_total.reshape(1, both_rows, D // 2), core)
    own_out = out_own.transpose(2, 0, 1, 3).reshape(drows, D)
    q_stage, pack, own_gu, own_down, own_out = fence((q_stage, pack, own_gu, own_down, own_out))

    pack = sum_axis(pack, "z").reshape(-1)
    q_own = own_rows(added(*q_stage), core)
    own_qkv = (
        q_own.reshape(2, 2, drows, 3, 256).transpose(2, 3, 0, 1, 4).reshape(drows, 3 * D)
    )
    me = lax.axis_index(ALL)
    at = 2 * D
    own_g1 = lax.dynamic_slice_in_dim(pack[:D], me * drows, drows)
    own_g2 = lax.dynamic_slice_in_dim(pack[D:at], me * drows, drows)
    own_beta = lax.dynamic_slice_in_dim(
        pack[at : at + D * H].reshape(D, H), me * drows, drows
    )
    at += D * H
    own_conv = lax.dynamic_slice_in_dim(
        pack[at : at + 3 * D * CONV].reshape(3 * D, CONV), me * grows, grows
    )
    at += 3 * D * CONV
    bias_total = pack[at : at + NDOM * H].reshape(NDOM, H)
    at += NDOM * H
    gain_total = pack[at : at + DK]
    return (
        output,
        grad_input,
        own_g1,
        own_qkv,
        own_beta,
        own_conv,
        bias_total,
        gain_total,
        own_out,
        own_g2,
        own_gu,
        own_down,
    )


def solution(mesh):
    seq, batch = mesh.shape["seq"], mesh.shape["batch"]
    fine = Mesh(mesh.devices.reshape(seq // 2, 2, batch // 2, 2), ALL)
    tokens = P(("x", "core"), ("z", "y"), None)
    rows = P(ALL, None)
    vector = P(ALL)
    return jax.shard_map(
        shards,
        mesh=fine,
        in_specs=(
            tokens,
            P(("x", "core")),
            vector,
            rows,
            rows,
            rows,
            P(),
            P(),
            rows,
            vector,
            rows,
            rows,
            tokens,
        ),
        out_specs=(
            tokens,
            tokens,
            vector,
            rows,
            rows,
            rows,
            P(),
            P(),
            rows,
            vector,
            rows,
            rows,
        ),
        check_vma=False,
    )
```

time: 570 us -> 485 us (0.85)
  waiting for transfers between devices: 185 us -> 128 us
  local copies, waits for them, and re-layouts: 105 us -> 88.3 us
  Pallas kernels: 65.3 us -> 49.3 us
  starting transfers between devices: 96.5 us -> 106 us
    ppermute x53 -> x56, waiting for transfers between devices: 155 us -> 97 us  [turned(): return lax.ppermute(a, axis, [(i, (i + by) % n) for i in range(n)])]
    unnamed x212 -> x197, local copies, waits for them, and re-layouts: 38.6 us -> 22.6 us
    pallas_call x3 -> x4, Pallas kernels: 41.7 us -> 26.9 us  [the longest x2 21.2 us: local(): pl.pallas_call(functools.partial(first_kernel, number, len(parts)), out_s...]
    ppermute x53 -> x56, starting transfers between devices: 72 us -> 80.6 us  [turned(): return lax.ppermute(a, axis, [(i, (i + by) % n) for i in range(n)])]
    squeeze x12 -> x17, local copies, waits for them, and re-layouts: 11 us -> 16.7 us  [sends(): lax.dynamic_index_in_dim(a, (me + k) % n, dim, False)]
    another operation x40 -> x36, other arithmetic: 28.8 us -> 23.1 us  [the longest x6 5.3 us: scatter_far(): return sends(jnp.stack([one, two], axis=1), 'z', 0)]
    dot_general x6 -> x7, matrix products: 15.8 us -> 17.2 us  [the longest x2 6.52 us: shards(): jnp.einsum('nd,nf->df', normed, e, preferred_element_type=F32).astype(BF16)]
  transfers between devices with their start and end apart: 71 -> 76, of which waited for: 26 -> 25; matrix products, arithmetic and copies ran while one was open for 31% -> 25% of each run, Pallas kernels for 12% -> 10%
where the time goes in v2:
time: 485 us; the launch traced here: 476 us
  waiting for transfers between devices  128 us (26%)
  starting transfers between devices  106 us (22%)
  local copies, waits for them, and re-layouts  88.3 us (18%)
  other arithmetic  63 us (13%)
  Pallas kernels  49.3 us (10%)
  matrix products  36.8 us (8%)
    ppermute x56, waiting for transfers between devices, turned(): return lax.ppermute(a, axis, [(i, (i + by) % n) for i in range(n)])  97 us
    ppermute x56, starting transfers between devices, turned(): return lax.ppermute(a, axis, [(i, (i + by) % n) for i in range(n)])  80.6 us
    all_to_all x2, waiting for transfers between devices, own_range(): return lax.all_to_all(a, SEQ, 0, 0, tiled=True)  24.6 us
    unnamed x197, local copies, waits for them, and re-layouts  22.6 us
    pallas_call x2, Pallas kernels, local(): pl.pallas_call(functools.partial(first_kernel, number, len(parts)), out_s...  21.2 us
    squeeze x17, local copies, waits for them, and re-layouts, sends(): lax.dynamic_index_in_dim(a, (me + k) % n, dim, False)  16.7 us
    pallas_call x1, Pallas kernels, shards(): on_core(fourth_kernel, (sds((2, 2 * frame, 768), BF16), sds((2, CONV, 768...  15.5 us
  transfers between devices with their start and end apart: 76, of which 25 were waited for; matrix products, arithmetic and copies ran while one was open for 25% of the time, Pallas kernels for 10%

profile of v2, /device:TPU:0, one launch (start us, length us, event | category | flops | bytes accessed | tf_op | source)
XLA Modules:
  0.0 475.7 jit_solution(11575964966323584089)
XLA Ops:
  4.6 4.4 collective-permute-start.2
  12.5 3.7 collective-permute-start.5
  28.5 7.0 %collective-permute-done.4 = bf16[2,72,768]{2,1,0:T(8,128)(2,1)} collective-permute-done((bf16[2,72,768]{2,1,0:T(8,128)(2,1)S(1)}, bf16[2,72,768]{2,1,0:T(8,128)(2,1)}, u32[]{:S(2)}, u32[]{:S(2)}) %collective-permute-start.4) | collective-permute-done | bytes 221216 | tf_op jit(solution)/shard_map/ppermute | solution.py:32
  45.6 5.5 %collective-permute-done.12 = bf16[4,2,2,768]{3,2,0,1:T(2,128)(2,1)S(1)} collective-permute-done((bf16[4,2,2,768]{3,2,0,1:T(2,128)(2,1)S(1)}, bf16[4,2,2,768]{3,2,0,1:T(2,128)(2,1)S(1)}, u32[]{:S(2)}, u32[]{:S(2)}) %collective-permute-start.12) | collective-permute-done | bytes 24608 | tf_op jit(solution)/shard_map/ppermute | solution.py:32
  77.9 13.9 %collective-permute-done.16 = bf16[2,64,1664]{2,1,0:T(8,128)(2,1)} collective-permute-done((bf16[2,64,1664]{2,1,0:T(8,128)(2,1)}, bf16[2,64,1664]{2,1,0:T(8,128)(2,1)}, u32[]{:S(2)}, u32[]{:S(2)}) %collective-permute-start.16) | collective-permute-done | bytes 426016 | tf_op jit(solution)/shard_map/ppermute | solution.py:32
  100.6 11.2 %delta_local.2 = (bf16[544,1024]{1,0:T(8,128)(2,1)}, bf16[4,2,2,64,768]{4,3,2,1,0:T(8,128)(2,1)}, bf16[2,544,768]{2,1,0:T(8,128)(2,1)}, bf16[2,512,768]{2,1,0:T(...) custom-call(s32[2]{0:T(128)S(1)} %pad_add_fusion.me_ref, ...), custom_call_target="tpu_custom_call" | custom-call | flops 11500000256 | tf_op jit(solution)/shard_map/delta_local/pallas_call | solution.py:735
  111.8 9.9 %delta_local.3 = (bf16[4,2,2,64,768]{4,3,2,1,0:T(8,128)(2,1)}, bf16[2,544,768]{2,1,0:T(8,128)(2,1)}, bf16[2,512,768]{2,1,0:T(8,128)(2,1)}, bf16[2,4,256,256]{3,2...) custom-call(s32[2]{0:T(128)S(1)} %pad_add_fusion.me_ref, ...), custom_call_target="tpu_custom_call", output_to_operand_aliasing={{1}: (7, {}), {2}: (8, {}), {3}: (9, {}), {4}: (10, {}), {5... | custom-call | flops 11500000256 | tf_op jit(solution)/shard_map/delta_local/pallas_call | solution.py:735
  140.4 6.1 %all-to-all-done.pd_ref = bf16[8,128,256]{2,1,0:T(8,128)(2,1)S(1)} async-done(((bf16[8,128,256]{2,1,0:T(8,128)(2,1)}), bf16[8,128,256]{2,1,0:T(8,128)(2,1)S(1)}, u32[]{:S(2)}, u32[]{:S(2)}) %all-to-all-start) | async-done | bytes 524320 | tf_op jit(solution)/shard_map/all_to_all | solution.py:512
  150.2 3.9 all-to-all-start.1
  157.1 24.3 %all-to-all-done.1.s_ref = bf16[8,128,128]{2,1,0:T(8,128)(2,1)S(1)} async-done(((bf16[8,128,128]{2,1,0:T(8,128)(2,1)}), bf16[8,128,128]{2,1,0:T(8,128)(2,1)S(1)}, u32[]{:S(2)}, u32[]{:S(2)}) %all-to-all-start.1) | async-done | bytes 262176 | tf_op jit(solution)/shard_map/all_to_all | solution.py:562
  184.7 8.6 %collective-permute-done.28 = bf16[2,2,88,1024]{3,2,1,0:T(8,128)(2,1)} collective-permute-done((bf16[2,2,88,1024]{3,2,1,0:T(8,128)(2,1)}, bf16[2,2,88,1024]{3,2,1,0:T(8,128)(2,1)}, u32[]{:S(2)}, u32[]{:S(2)}) %collective-permute-start.28) | collective-permute-done | bytes 720928 | tf_op jit(solution)/shard_map/ppermute | solution.py:32
  221.0 3.7 multiply_convert_fusion
  245.8 5.1 %delta_back_local.1 = (bf16[2,4,128,128]{3,2,1,0:T(8,128)(2,1)}, f32[512,512]{1,0:T(8,128)S(1)}, f32[512,512]{1,0:T(8,128)S(1)}, f32[512,512]{1,0:T(8,128)S(1)}, f32[2,8,128]{2,1,0:T(8,128)S(1)}) custom-call(bf16[2,512,768]{2,1,0:T(8,128)(2,1)} %get-tuple-element.271.qkv_ref, bf16[2,4,256,256]{3,2,1,0:T(8,128)(2,1)S(1)} %copy-done.3, ...), custom_call_target="tpu_custom_call" | custom-call | flops 5750000128 | tf_op jit(solution)/shard_map/delta_back_local/pallas_call | solution.py:888
  254.1 4.1 all-to-all-start.2
  260.3 3.8 dynamic-slice_bitcast_fusion.2
  277.0 5.7 %all-to-all-start.3 = ((bf16[8,128,128]{2,1,0:T(8,128)(2,1)}), bf16[8,128,128]{2,1,0:T(8,128)(2,1)S(1)}, u32[]{:S(2)}, u32[]{:S(2)}) async-start(bf16[8,128,128]{2,1,0:T(8,128)(2,1)} %adjoint_scan.1), calls=%async_computation.3 | async-start | bytes 524288 | tf_op jit(solution)/shard_map/all_to_all | solution.py:562
  285.6 15.3 %collective-permute-done.35 = bf16[4,2,64,1408]{3,2,1,0:T(8,128)(2,1)} collective-permute-done((bf16[4,2,64,1408]{3,2,1,0:T(8,128)(2,1)}, bf16[4,2,64,1408]{3,2,1,0:T(8,128)(2,1)}, u32[]{:S(2)}, u32[]{:S(2)}) %collective-permute-start.35) | collective-permute-done | bytes 1441824 | tf_op jit(solution)/shard_map/ppermute | solution.py:32
  327.0 4.6 collective-permute-done.42
  333.7 15.5 %delta_back.1 = (bf16[2,544,768]{2,1,0:T(8,128)(2,1)}, f32[2,4,768]{2,1,0:T(4,128)S(1)}, bf16[2,512,128]{2,1,0:T(8,128)(2,1)S(1)}, f32[2,2,128]{2,1,0:T(2,128)S(1)}) custom-call(bf16[2,512,768]{2,1,0:T(8,128)(2,1)} %get-tuple-element.271.qkv_ref, bf16[2,544,768]{2,1,0:T(8,128)(2,1)} %get-tuple-element.308.pre_ref, f32[2,4,768]{2,1,0:T(4,128)S(1)} %bitcast.387, ...), custom_call_target="tpu_custom_call" | custom-call | flops 17250000896 | tf_op jit(solution)/shard_map/delta_back/pallas_call | solution.py:961
  349.3 4.0 collective-permute-done.45
  354.4 3.9 convolution_convert_fusion.3
  366.9 10.5 %collective-permute-start.57 = (bf16[2,64,1408]{2,1,0:T(8,128)(2,1)}, bf16[2,64,1408]{2,1,0:T(8,128)(2,1)}, u32[]{:S(2)}, u32[]{:S(2)}) collective-permute-start(bf16[2,64,1408]{2,1,0:T(8,128)(2,1)} %get-tuple-element.497), channel_id=1, source_target_pairs={{0,24},{8,0},{16,8},{24,16},{1,25},{9,1},{17,9},{25,17},{2,26},{10... | collective-permute-start | bytes 1081352 | tf_op jit(solution)/shard_map/ppermute | solution.py:32
  448.6 7.7 %collective-permute-done.63 = bf16[2,64,768]{2,1,0:T(8,128)(2,1)S(1)} collective-permute-done((bf16[2,64,768]{2,1,0:T(8,128)(2,1)S(1)}, bf16[2,64,768]{2,1,0:T(8,128)(2,1)S(1)}, u32[]{:S(2)}, u32[]{:S(2)}) %collective-permute-start.63) | collective-permute-done | bytes 196640 | tf_op jit(solution)/shard_map/ppermute | solution.py:32
  461.3 5.7 %collective-permute-done.69 = f32[184,128]{1,0:T(8,128)S(1)} collective-permute-done((f32[184,128]{1,0:T(8,128)S(1)}, f32[184,128]{1,0:T(8,128)S(1)}, u32[]{:S(2)}, u32[]{:S(2)}) %collective-permute-start.69) | collective-permute-done | bytes 94240 | tf_op jit(solution)/shard_map/ppermute | solution.py:32
  (583 shorter events, 283.7 us)
Async XLA Ops:
  28.0 31.3 %collective-permute-start.19 = (bf16[2,88,512]{2,1,0:T(8,128)(2,1)}, bf16[2,88,512]{2,1,0:T(8,128)(2,1)}, u32[]{:S(2)}, u32[]{:S(2)}) collective-permute-start(bf16[2,88,512]{2,1,0:T(8,128)(2,1)} %pad_maximum_fusion.24), channel_id=1, source_target_pairs={{0,4},{4,0},{1,5},{5,1},{2,6},{6,2},{3,7},{7,3},{8,12},{12,8},{9,1... | collective-permute-start | bytes 540680 | tf_op jit(solution)/shard_map/ppermute | solution.py:32
  35.5 25.8 %collective-permute-start.21 = (bf16[2,88,512]{2,1,0:T(8,128)(2,1)}, bf16[2,88,512]{2,1,0:T(8,128)(2,1)}, u32[]{:S(2)}, u32[]{:S(2)}) collective-permute-start(bf16[2,88,512]{2,1,0:T(8,128)(2,1)} %pad_maximum_fusion.25), channel_id=1, source_target_pairs={{0,2},{2,0},{1,3},{3,1},{4,6},{6,4},{5,7},{7,5},{8,10},{10,8},{9,1... | collective-permute-start | bytes 540680 | tf_op jit(solution)/shard_map/ppermute | solution.py:32
  52.0 39.8 %collective-permute-start.14 = (bf16[2,4,64,768]{3,2,1,0:T(8,128)(2,1)S(1)}, bf16[2,4,64,768]{3,2,1,0:T(8,128)(2,1)S(1)}, u32[]{:S(2)}, u32[]{:S(2)}) collective-permute-start(bf16[2,4,64,768]{3,2,1,0:T(8,128)(2,1)S(1)} %pad_maximum_fusion.16.refs_0_), channel_id=1, source_target_pairs={{0,2},{2,0},{1,3},{3,1},{4,6},{6,4},{5,7},{7,5},{8,10},{10,8},{9,1... | collective-permute-start | bytes 2359304 | tf_op jit(solution)/shard_map/ppermute | solution.py:32
  52.8 39.1 %collective-permute-start.13 = (bf16[2,4,64,768]{3,2,1,0:T(8,128)(2,1)S(1)}, bf16[2,4,64,768]{3,2,1,0:T(8,128)(2,1)}, u32[]{:S(2)}, u32[]{:S(2)}) collective-permute-start(bf16[2,4,64,768]{3,2,1,0:T(8,128)(2,1)S(1)} %pad_maximum_fusion.15.refs_0_), channel_id=1, source_target_pairs={{0,4},{4,0},{1,5},{5,1},{2,6},{6,2},{3,7},{7,3},{8,12},{12,8},{9,1... | collective-permute-start | bytes 2359304 | tf_op jit(solution)/shard_map/ppermute | solution.py:32
  61.3 30.5 %collective-permute-start.16 = (bf16[2,64,1664]{2,1,0:T(8,128)(2,1)}, bf16[2,64,1664]{2,1,0:T(8,128)(2,1)}, u32[]{:S(2)}, u32[]{:S(2)}) collective-permute-start(bf16[2,64,1664]{2,1,0:T(8,128)(2,1)} %pad_maximum_fusion.20), channel_id=1, source_target_pairs={{0,16},{8,24},{16,0},{24,8},{1,17},{9,25},{17,1},{25,9},{2,18},{10... | collective-permute-start | bytes 1277960 | tf_op jit(solution)/shard_map/ppermute | solution.py:32
  94.9 45.6 %collective-permute-start.27 = (bf16[2,2,88,1024]{3,2,1,0:T(8,128)(2,1)}, bf16[2,2,88,1024]{3,2,1,0:T(8,128)(2,1)}, u32[]{:S(2)}, u32[]{:S(2)}) collective-permute-start(bf16[2,2,88,1024]{3,2,1,0:T(8,128)(2,1)} %maximum_maximum_fusion), channel_id=1, source_target_pairs={{0,24},{8,0},{16,8},{24,16},{1,25},{9,1},{17,9},{25,17},{2,26},{10... | collective-permute-start | bytes 2162696 | tf_op jit(solution)/shard_map/ppermute | solution.py:32
  97.0 31.0 %collective-permute-start.24 = (bf16[2,2,88,1024]{3,2,1,0:T(8,128)(2,1)}, bf16[2,2,88,1024]{3,2,1,0:T(8,128)(2,1)S(1)}, u32[]{:S(2)}, u32[]{:S(2)}) collective-permute-start(bf16[2,2,88,1024]{3,2,1,0:T(8,128)(2,1)} %maximum_maximum_fusion), channel_id=1, source_target_pairs={{0,8},{8,16},{16,24},{24,0},{1,9},{9,17},{17,25},{25,1},{2,10},{10... | collective-permute-start | bytes 2162696 | tf_op jit(solution)/shard_map/ppermute | solution.py:32
  99.1 28.8 %collective-permute-start.22 = (bf16[4,64,1664]{2,1,0:T(8,128)(2,1)S(1)}, bf16[4,64,1664]{2,1,0:T(8,128)(2,1)S(1)}, u32[]{:S(2)}, u32[]{:S(2)}) collective-permute-start(bf16[4,64,1664]{2,1,0:T(8,128)(2,1)S(1)} %pad_maximum_fusion.12), channel_id=1, source_target_pairs={{0,2},{2,0},{1,3},{3,1},{4,6},{6,4},{5,7},{7,5},{8,10},{10,8},{9,1... | collective-permute-start | bytes 2555912 | tf_op jit(solution)/shard_map/ppermute | solution.py:32
  100.0 27.9 %collective-permute-start.23 = (bf16[4,64,1664]{2,1,0:T(8,128)(2,1)S(1)}, bf16[4,64,1664]{2,1,0:T(8,128)(2,1)S(1)}, u32[]{:S(2)}, u32[]{:S(2)}) collective-permute-start(bf16[4,64,1664]{2,1,0:T(8,128)(2,1)S(1)} %pad_maximum_fusion.13), channel_id=1, source_target_pairs={{0,4},{4,0},{1,5},{5,1},{2,6},{6,2},{3,7},{7,3},{8,12},{12,8},{9,1... | collective-permute-start | bytes 2555912 | tf_op jit(solution)/shard_map/ppermute | solution.py:32
  136.3 56.9 %collective-permute-start.26 = (bf16[2,4,64,1664]{3,2,1,0:T(8,128)(2,1)}, bf16[2,4,64,1664]{3,2,1,0:T(8,128)(2,1)}, u32[]{:S(2)}, u32[]{:S(2)}) collective-permute-start(bf16[2,4,64,1664]{3,2,1,0:T(8,128)(2,1)} %pad_maximum_fusion.5), channel_id=1, source_target_pairs={{0,2},{2,0},{1,3},{3,1},{4,6},{6,4},{5,7},{7,5},{8,10},{10,8},{9,1... | collective-permute-start | bytes 5111816 | tf_op jit(solution)/shard_map/ppermute | solution.py:32
  138.5 54.7 %collective-permute-start.25 = (bf16[2,4,64,1664]{3,2,0,1:T(8,128)(2,1)}, bf16[2,4,64,1664]{3,2,0,1:T(8,128)(2,1)}, u32[]{:S(2)}, u32[]{:S(2)}) collective-permute-start(bf16[2,4,64,1664]{3,2,0,1:T(8,128)(2,1)} %pad_maximum_fusion.4), channel_id=1, source_target_pairs={{0,4},{4,0},{1,5},{5,1},{2,6},{6,2},{3,7},{7,3},{8,12},{12,8},{9,1... | collective-permute-start | bytes 5111816 | tf_op jit(solution)/shard_map/ppermute | solution.py:32
  150.2 31.3 %all-to-all-start.1 = ((bf16[8,128,128]{2,1,0:T(8,128)(2,1)}), bf16[8,128,128]{2,1,0:T(8,128)(2,1)S(1)}, u32[]{:S(2)}, u32[]{:S(2)}) async-start(bf16[8,128,128]{2,1,0:T(8,128)(2,1)} %state_scan.1), calls=%async_computation.1 | async-start | bytes 524288 | tf_op jit(solution)/shard_map/all_to_all | solution.py:562
  154.2 39.1 %collective-permute-start.28 = (bf16[2,2,88,1024]{3,2,1,0:T(8,128)(2,1)}, bf16[2,2,88,1024]{3,2,1,0:T(8,128)(2,1)}, u32[]{:S(2)}, u32[]{:S(2)}) collective-permute-start(bf16[2,2,88,1024]{3,2,1,0:T(8,128)(2,1)} %maximum_maximum_fusion), channel_id=1, source_target_pairs={{0,16},{8,24},{16,0},{24,8},{1,17},{9,25},{17,1},{25,9},{2,18},{10... | collective-permute-start | bytes 2162696 | tf_op jit(solution)/shard_map/ppermute | solution.py:32
  264.1 36.9 %collective-permute-start.35 = (bf16[4,2,64,1408]{3,2,1,0:T(8,128)(2,1)}, bf16[4,2,64,1408]{3,2,1,0:T(8,128)(2,1)}, u32[]{:S(2)}, u32[]{:S(2)}) collective-permute-start(bf16[4,2,64,1408]{3,2,1,0:T(8,128)(2,1)} %get-tuple-element.473), channel_id=1, source_target_pairs={{0,4},{4,0},{1,5},{5,1},{2,6},{6,2},{3,7},{7,3},{8,12},{12,8},{9,1... | collective-permute-start | bytes 4325384 | tf_op jit(solution)/shard_map/ppermute | solution.py:32
  267.8 34.7 %collective-permute-start.36 = (bf16[4,2,64,1408]{3,2,1,0:T(8,128)(2,1)}, bf16[4,2,64,1408]{3,2,1,0:T(8,128)(2,1)}, u32[]{:S(2)}, u32[]{:S(2)}) collective-permute-start(bf16[4,2,64,1408]{3,2,1,0:T(8,128)(2,1)} %get-tuple-element.471), channel_id=1, source_target_pairs={{0,2},{2,0},{1,3},{3,1},{4,6},{6,4},{5,7},{7,5},{8,10},{10,8},{9,1... | collective-permute-start | bytes 4325384 | tf_op jit(solution)/shard_map/ppermute | solution.py:32
  270.6 39.0 %collective-permute-start.37 = (bf16[4,88,512]{2,1,0:T(8,128)(2,1)}, bf16[4,88,512]{2,1,0:T(8,128)(2,1)}, u32[]{:S(2)}, u32[]{:S(2)}) collective-permute-start(bf16[4,88,512]{2,1,0:T(8,128)(2,1)} %get-tuple-element.541), channel_id=1, source_target_pairs={{0,2},{2,0},{1,3},{3,1},{4,6},{6,4},{5,7},{7,5},{8,10},{10,8},{9,1... | collective-permute-start | bytes 1081352 | tf_op jit(solution)/shard_map/ppermute | solution.py:32
  272.0 37.6 %collective-permute-start.38 = (bf16[4,88,512]{2,1,0:T(8,128)(2,1)}, bf16[4,88,512]{2,1,0:T(8,128)(2,1)}, u32[]{:S(2)}, u32[]{:S(2)}) collective-permute-start(bf16[4,88,512]{2,1,0:T(8,128)(2,1)} %get-tuple-element.539), channel_id=1, source_target_pairs={{0,4},{4,0},{1,5},{5,1},{2,6},{6,2},{3,7},{7,3},{8,12},{12,8},{9,1... | collective-permute-start | bytes 1081352 | tf_op jit(solution)/shard_map/ppermute | solution.py:32
  277.0 31.9 %all-to-all-start.3 = ((bf16[8,128,128]{2,1,0:T(8,128)(2,1)}), bf16[8,128,128]{2,1,0:T(8,128)(2,1)S(1)}, u32[]{:S(2)}, u32[]{:S(2)}) async-start(bf16[8,128,128]{2,1,0:T(8,128)(2,1)} %adjoint_scan.1), calls=%async_computation.3 | async-start | bytes 524288 | tf_op jit(solution)/shard_map/all_to_all | solution.py:562
  317.3 36.0 %collective-permute-start.39 = (bf16[4,64,1408]{2,1,0:T(8,128)(2,1)S(1)}, bf16[4,64,1408]{2,1,0:T(8,128)(2,1)S(1)}, u32[]{:S(2)}, u32[]{:S(2)}) collective-permute-start(bf16[4,64,1408]{2,1,0:T(8,128)(2,1)S(1)} %copy-done.62), channel_id=1, source_target_pairs={{0,2},{2,0},{1,3},{3,1},{4,6},{6,4},{5,7},{7,5},{8,10},{10,8},{9,1... | collective-permute-start | bytes 2162696 | tf_op jit(solution)/shard_map/ppermute | solution.py:32
  319.2 30.1 %collective-permute-start.46 = (bf16[2,2,64,512]{3,2,1,0:T(8,128)(2,1)S(1)}, bf16[2,2,64,512]{3,2,1,0:T(8,128)(2,1)S(1)}, u32[]{:S(2)}, u32[]{:S(2)}) collective-permute-start(bf16[2,2,64,512]{3,2,1,0:T(8,128)(2,1)S(1)} %get-tuple-element.511), channel_id=1, source_target_pairs={{0,24},{8,0},{16,8},{24,16},{1,25},{9,1},{17,9},{25,17},{2,26},{10... | collective-permute-start | bytes 786440 | tf_op jit(solution)/shard_map/ppermute | solution.py:32
  321.9 31.4 %collective-permute-start.45 = (bf16[2,2,64,512]{3,2,1,0:T(8,128)(2,1)S(1)}, bf16[2,2,64,512]{3,2,1,0:T(8,128)(2,1)S(1)}, u32[]{:S(2)}, u32[]{:S(2)}) collective-permute-start(bf16[2,2,64,512]{3,2,1,0:T(8,128)(2,1)S(1)} %get-tuple-element.512), channel_id=1, source_target_pairs={{0,16},{8,24},{16,0},{24,8},{1,17},{9,25},{17,1},{25,9},{2,18},{10... | collective-permute-start | bytes 786440 | tf_op jit(solution)/shard_map/ppermute | solution.py:32
  325.0 28.3 %collective-permute-start.44 = (bf16[2,2,64,512]{3,2,1,0:T(8,128)(2,1)S(1)}, bf16[2,2,64,512]{3,2,1,0:T(8,128)(2,1)S(1)}, u32[]{:S(2)}, u32[]{:S(2)}) collective-permute-start(bf16[2,2,64,512]{3,2,1,0:T(8,128)(2,1)S(1)} %get-tuple-element.513), channel_id=1, source_target_pairs={{0,8},{8,16},{16,24},{24,0},{1,9},{9,17},{17,25},{25,1},{2,10},{10... | collective-permute-start | bytes 786440 | tf_op jit(solution)/shard_map/ppermute | solution.py:32
  366.9 53.6 %collective-permute-start.57 = (bf16[2,64,1408]{2,1,0:T(8,128)(2,1)}, bf16[2,64,1408]{2,1,0:T(8,128)(2,1)}, u32[]{:S(2)}, u32[]{:S(2)}) collective-permute-start(bf16[2,64,1408]{2,1,0:T(8,128)(2,1)} %get-tuple-element.497), channel_id=1, source_target_pairs={{0,24},{8,0},{16,8},{24,16},{1,25},{9,1},{17,9},{25,17},{2,26},{10... | collective-permute-start | bytes 1081352 | tf_op jit(solution)/shard_map/ppermute | solution.py:32
  403.3 26.6 %collective-permute-start.56 = (bf16[2,64,1408]{2,1,0:T(8,128)(2,1)}, bf16[2,64,1408]{2,1,0:T(8,128)(2,1)}, u32[]{:S(2)}, u32[]{:S(2)}) collective-permute-start(bf16[2,64,1408]{2,1,0:T(8,128)(2,1)} %get-tuple-element.500), channel_id=1, source_target_pairs={{0,16},{8,24},{16,0},{24,8},{1,17},{9,25},{17,1},{25,9},{2,18},{10... | collective-permute-start | bytes 1081352 | tf_op jit(solution)/shard_map/ppermute | solution.py:32
  (146 other events, 1203.7 us)

commit v3 on v2

--- a/solution.py
+++ b/solution.py
@@ -20,7 +20,7 @@
 BF16 = jnp.bfloat16
 SEQ = ("z", "y")
 ALL = ("z", "y", "x", "core")
-VMEM_LIMIT = 48 * 1024 * 1024
+VMEM_LIMIT = 60 * 1024 * 1024
 
 
 def swap(a):
@@ -58,13 +58,17 @@
     return jnp.stack(in_place(fetched(a, axis), lax.axis_index(axis)), axis=dim)
 
 
+def shares(a, axis, dim):
+    n, me = lax.axis_size(axis), lax.axis_index(axis)
+    return [lax.dynamic_index_in_dim(a, (me + k) % n, dim, False) for k in range(n)]
+
+
+def sent(parts, axis):
+    return parts[0], [turned(a, axis, k) for k, a in enumerate(parts) if k]
+
+
 def sends(a, axis, dim):
-    n, me = lax.axis_size(axis), lax.axis_index(axis)
-    own = lax.dynamic_index_in_dim(a, me, dim, False)
-    got = [
-        turned(lax.dynamic_index_in_dim(a, (me + k) % n, dim, False), axis, k) for k in range(1, n)
-    ]
-    return own, got
+    return sent(shares(a, axis, dim), axis)
 
 
 def added(own, got):
@@ -74,59 +78,65 @@
     return total
 
 
-def stacked_near(parts):
-    return jnp.stack([a[0] for a in parts]), jnp.stack([a[1] for a in parts])
-
-
-def gather_near(one, two):
-    return fetched(one, "x"), fetched(two, "y")
-
-
-def gather_last(ones, twos):
-    one = jnp.stack(in_place(ones, lax.axis_index("x")))
-    two = jnp.stack(in_place(twos, lax.axis_index("y")))
-    return fetched(one, "y"), fetched(two, "x")
-
-
-def gather_end(ones, twos):
-    one = jnp.stack(in_place(ones, lax.axis_index("y")))
-    two = jnp.stack(in_place(twos, lax.axis_index("x")), axis=1)
-    return one, two
-
-
-def scatter_near(one, two):
-    nz, ny, nx = (lax.axis_size(a) for a in ("z", "y", "x"))
-    n = one.shape[-1]
-    return (
-        sends(one.reshape(nz, ny, nx, -1, n), "y", 1),
-        sends(two.reshape(nz, ny, nx, -1, n), "x", 2),
-    )
-
-
-def scatter_mid(stage):
-    one, two = (added(*s).astype(BF16) for s in stage)
-    return sends(one, "x", 1), sends(two, "y", 1)
-
-
-def scatter_far(stage):
-    one, two = (added(*s).astype(BF16) for s in stage)
-    return sends(jnp.stack([one, two], axis=1), "z", 0)
-
-
-def scatter_first(total):
-    nz, ny, nx = (lax.axis_size(a) for a in ("z", "y", "x"))
-    return sends(total.reshape(nz, ny, nx, -1, total.shape[-1]), "z", 0)
-
-
-def scatter_second(stage):
+def crossed(a, early, by):
+    n = lax.axis_size("x")
+    pairs = []
+    for y in range(n):
+        for x in range(n):
+            for core in range(2):
+                along_x = (core == 0) == early
+                to_x = (x + by) % n if along_x else x
+                to_y = y if along_x else (y + by) % n
+                pairs.append(((y * n + x) * 2 + core, (to_y * n + to_x) * 2 + core))
+    return lax.ppermute(a, ("y", "x", "core"), pairs)
+
+
+def cross_place(early):
+    along_x = (lax.axis_index("core") == 0) == early
+    return jnp.where(along_x, lax.axis_index("x"), lax.axis_index("y"))
+
+
+def cross_fetched(a, early):
+    return [a] + [crossed(a, early, k) for k in range(1, lax.axis_size("x"))]
+
+
+def cross_stack(parts):
+    return jnp.stack(in_place(parts, cross_place(True)))
+
+
+def cross_end(parts):
+    every = jnp.stack(in_place(parts, cross_place(False)))
+    first = lax.axis_index("core") == 0
+    return jnp.where(first, every, jnp.swapaxes(every, 0, 1)).transpose(2, 0, 1, 3, 4)
+
+
+def grid_of(a):
+    nz, ny, nx = (lax.axis_size(axis) for axis in ("z", "y", "x"))
+    return a.reshape(nz, ny, nx, -1, a.shape[-1])
+
+
+def late_shares(a):
+    n = lax.axis_size("x")
+    first = lax.axis_index("core") == 0
+    y, x = lax.axis_index("y"), lax.axis_index("x")
+    return [
+        jnp.where(
+            first,
+            lax.dynamic_index_in_dim(a, (y + k) % n, 1, False),
+            lax.dynamic_index_in_dim(a, (x + k) % n, 2, False),
+        )
+        for k in range(n)
+    ]
+
+
+def early_shares(stage):
     total = added(*stage).astype(BF16)
-    n = total.shape[-1] // 2
-    return sends(total[..., :n], "x", 1), sends(total[..., n:], "y", 0)
-
-
-def scatter_third(stage):
-    one, two = (added(*s).astype(BF16) for s in stage)
-    return sends(one, "y", 0), sends(two, "x", 0)
+    n, me = lax.axis_size("x"), cross_place(True)
+    return [lax.dynamic_index_in_dim(total, (me + k) % n, 1, False) for k in range(n)]
+
+
+def cross_sent(parts, early):
+    return parts[0], [crossed(a, early, k) for k, a in enumerate(parts) if k]
 
 
 def core_pick(a, core):
@@ -144,19 +154,59 @@
 
 
 def own_rows(total, core):
-    k, both, n = total.shape
-    parts = total.reshape(k, 2, both // 2, n).transpose(1, 0, 2, 3)
-    mine, other = core_pick(parts, core)
+    mine, other = core_pick(total.reshape(2, -1, total.shape[-1]), core)
     got = swap(other)
     first = core == 0
     return jnp.stack([jnp.where(first, mine, got), jnp.where(first, got, mine)], axis=0)
 
 
-def sum_axis(a, axis):
-    every = gather_axis(a, axis, 0)
-    total = every[0]
-    for k in range(1, every.shape[0]):
-        total = total + every[k]
+def z_sum(a):
+    parts = in_place([p if k == 0 else turned(p, "z", k) for k, p in enumerate(shares(a, "z", 0))], lax.axis_index("z"))
+    total = parts[0]
+    for part in parts[1:]:
+        total = total + part
+    return total
+
+
+def plane_step(a, k):
+    n = lax.axis_size("x")
+    ky, kx = divmod(k, n)
+    pairs = [(j * n + i, (j + ky) % n * n + (i + kx) % n) for j in range(n) for i in range(n)]
+    return lax.ppermute(a, ("y", "x"), pairs)
+
+
+def plane_fetched(a):
+    return [a] + [plane_step(a, k) for k in range(1, lax.axis_size("x") ** 2)]
+
+
+def plane_order(parts):
+    n = lax.axis_size("x")
+    rows_of = [in_place(parts[k * n : (k + 1) * n], lax.axis_index("x")) for k in range(n)]
+    columns_of = [in_place([r[i] for r in rows_of], lax.axis_index("y")) for i in range(n)]
+    return [[columns_of[i][j] for i in range(n)] for j in range(n)]
+
+
+def plane_stack(parts):
+    return jnp.stack([jnp.stack(row) for row in plane_order(parts)])
+
+
+def plane_shares(a):
+    n = lax.axis_size("x")
+    y, x = lax.axis_index("y"), lax.axis_index("x")
+    out = []
+    for k in range(n * n):
+        ky, kx = divmod(k, n)
+        one = lax.dynamic_index_in_dim(a, (y + ky) % n, 1, False)
+        out.append(lax.dynamic_index_in_dim(one, (x + kx) % n, 1, False))
+    return out
+
+
+def plane_sum(shares):
+    parts = [a if k == 0 else plane_step(a, k) for k, a in enumerate(shares)]
+    total = None
+    for row in plane_order(parts):
+        for part in row:
+            total = part if total is None else total + part
     return total
 
 
@@ -231,12 +281,18 @@
     rows = qkv_ref.shape[1] // 2
     frame = rows + HALO
     copies = []
+    columns_of = pl.ds(half * 768, 768)
     for k, part in enumerate(parts):
-        place = lax.rem(me_ref[half] + (count - k), count)
         inner = part.shape[0]
+        late = lax.rem(jnp.where(me_ref[0] == 0, me_ref[1], me_ref[2]) + (count - k), count)
         for i in range(inner):
-            to = w_ref.at[:, place, i] if half == 0 else w_ref.at[:, i, place]
-            copies.append(pltpu.make_async_copy(part.at[i], to, sem.at[k * inner + i]))
+            to_y = jnp.where(me_ref[0] == 0, late, i)
+            to_x = jnp.where(me_ref[0] == 0, i, late)
+            copies.append(
+                pltpu.make_async_copy(
+                    part.at[i, :, :, columns_of], w_ref.at[:, to_y, to_x], sem.at[k * inner + i]
+                )
+            )
             copies[-1].start()
     if half == 0:
         x = x_ref[...].astype(F32)
@@ -595,7 +651,7 @@
     fence = lax.optimization_barrier
 
     q_mine, q_other = core_pick(
-        w_qkv.reshape(drows, 3, 2, 2, 256).transpose(2, 3, 0, 1, 4).reshape(2, 2, drows, 768), core
+        w_qkv.reshape(drows, 3, 2, 2, 256).transpose(2, 0, 3, 1, 4).reshape(2, drows, 1536), core
     )
     q_got = swap(q_other)
     small = jnp.concatenate(
@@ -608,25 +664,27 @@
     halo = lax.ppermute(
         x_own[rows - HALO :], SEQ, [(i, i + 1) for i in range(seq_devices - 1)]
     )
-    small = jnp.stack([jnp.where(first, small, small_got), jnp.where(first, small_got, small)])
-    small = jnp.pad(small, ((0, 0), (0, 7), (0, 0)))
-    q_part = jnp.concatenate([chip_rows(q_mine, q_got, core), small], axis=1)
+    small = jnp.concatenate(
+        [jnp.where(first, small, small_got), jnp.where(first, small_got, small)], axis=1
+    )
+    small = jnp.pad(small, ((0, 7), (0, 0)))
+    q_part = jnp.concatenate([chip_rows(q_mine, q_got, core), small], axis=0)
     q_part, halo, x_own, w_gate_up, w_out, w_down, cotangent = fence(
         (q_part, halo, x_own, w_gate_up, w_out, w_down, cotangent)
     )
 
     q_far = fetched(q_part, "z")
-    down_ones, down_twos = gather_last(
-        *gather_near(w_down[:, : D // 2], w_down[:, D // 2 :])
-    )
     out_cols = w_out.reshape(drows, 2, 2, 256).transpose(1, 2, 0, 3)
     gu_cols = (
         w_gate_up.reshape(drows, 2, chips, 2, frows)
         .transpose(3, 1, 0, 2, 4)
         .reshape(2, 2, drows, FF // 2)
     )
-    gu_mine, gu_other = core_pick(jnp.concatenate([gu_cols, out_cols], axis=-1), core)
-    gu_part = chip_rows(gu_mine, swap(gu_other), core)
+    wide_cols = jnp.concatenate(
+        [gu_cols[:, 0], gu_cols[:, 1], out_cols[:, 0], out_cols[:, 1]], axis=-1
+    )
+    wide_mine, wide_other = core_pick(wide_cols, core)
+    wide_part = chip_rows(wide_mine, swap(wide_other), core)
     choose = (domain_ids[0] == jnp.arange(NDOM, dtype=jnp.int32)).astype(BF16)
     bias_own = jnp.sum(domain_bias.astype(F32) * choose.astype(F32)[:, None], axis=0)
     extra = jnp.pad(jnp.concatenate([bias_own.astype(BF16), choose]), (0, D - H - NDOM))
@@ -635,23 +693,21 @@
     frame_other = swap(frame_own)
     g_own = cotangent.reshape(rows, D)
     g_other = swap(g_own)
-    q_far, gu_part, frame_own, frame_other, g_own, g_other = fence(
-        (q_far, gu_part, frame_own, frame_other, g_own, g_other)
+    q_far, frame_own, frame_other, g_own, g_other, wide_part, w_down = fence(
+        (q_far, frame_own, frame_other, g_own, g_other, wide_part, w_down)
     )
 
     q_sorted = in_place(q_far, z)
-    q_ones, q_twos = gather_near(*stacked_near([a[:, :both_rows] for a in q_sorted]))
-    smalls = jnp.stack([a[:, both_rows] for a in q_sorted])
-    smalls = gather_axis(gather_axis(smalls, "x", 1), "y", 1)
+    q_parts = cross_fetched(jnp.stack([a[:both_rows] for a in q_sorted]), True)
+    smalls = jnp.stack([a[both_rows].reshape(2, 768) for a in q_sorted])
+    smalls = plane_fetched(smalls)
     ends = sorted({1, nz - 1})
-    gu_ends = [turned(gu_part, "z", k) for k in ends]
-    q_ones, q_twos, smalls, gu_part = fence((q_ones, q_twos, smalls, gu_part))
-
-    q_ones, q_twos = gather_last(q_ones, q_twos)
-    gu_far = [gu_part, gu_ends[0]]
-    gu_far += [turned(gu_part, "z", k) for k in range(2, nz - 1)]
-    gu_far += gu_ends[1:]
-    smalls = smalls.reshape(2 * chips, 768)[:, :n_small]
+    wide_z = [wide_part, turned(wide_part, "z", 1)]
+    q_parts, wide_z, w_down = fence((q_parts, wide_z, w_down))
+
+    q_parts = cross_fetched(cross_stack(q_parts), False)
+    wide_z += [turned(wide_z[0], "z", k) for k in range(2, nz - 1)]
+    smalls = plane_stack(smalls).transpose(2, 0, 1, 3, 4).reshape(2 * chips, 768)[:, :n_small]
     gain_one = smalls[:, :drows].reshape(1, D).astype(F32)
     gain_two = smalls[:, drows : 2 * drows].reshape(1, D).astype(F32)
     full_beta = smalls[:, 2 * drows : 2 * drows + drows * H].reshape(D, 2, half)
@@ -680,9 +736,9 @@
     ).astype(F32)
     g_both = jnp.concatenate([g_own, g_other], axis=0)
     (
-        q_ones,
-        q_twos,
-        gu_far,
+        q_parts,
+        wide_z,
+        w_down,
         gain_one,
         gain_two,
         beta_pairs,
@@ -691,13 +747,11 @@
         x_frames,
         x_both,
         g_both,
-        down_ones,
-        down_twos,
     ) = fence(
         (
-            q_ones,
-            q_twos,
-            gu_far,
+            q_parts,
+            wide_z,
+            w_down,
             gain_one,
             gain_two,
             beta_pairs,
@@ -706,8 +760,6 @@
             x_frames,
             x_both,
             g_both,
-            down_ones,
-            down_twos,
         )
     )
 
@@ -715,10 +767,8 @@
         w_shape = sds((nz, ny, nx, both_rows, 768), BF16)
     else:
         w_shape = sds((1, 1, 1, D, 768), BF16)
-        q_ones, q_twos = (
-            [a.transpose(2, 0, 1, 3, 4).reshape(1, 1, D, 768)] for a in gather_end(q_ones, q_twos)
-        )
-    place = jnp.stack([y, x]).astype(jnp.int32)
+        q_parts = [cross_end(q_parts).reshape(1, 1, D, 1536)]
+    place = jnp.stack([core, y, x]).astype(jnp.int32)
     kept = (
         sds((2, 2 * frame, 768), BF16),
         sds((2, tall, 768), BF16),
@@ -753,23 +803,27 @@
             name="delta_local",
         )(place, *parts, *ins, beta_pairs, conv_mine, bias_pairs, *held)
 
-    gu_stacks = stacked_near(in_place(gu_far, z))
-    gu_ones, gu_twos = gather_near(*gu_stacks)
-    down_part = jnp.concatenate(gather_end(down_ones, down_twos), axis=-1)
-    down_ends = [turned(down_part, "z", k) for k in ends]
+    wide_z += [turned(wide_z[0], "z", k) for k in ends[1:]]
     normed, w_q_one, *held = local(
         0,
-        q_ones,
-        (after(x_frames, gu_stacks, down_part), gain_one),
+        q_parts,
+        (x_frames, gain_one),
         [whole(2 * frame, D), whole(1, D)],
         (sds((2 * frame, D), BF16),),
         (whole(2 * frame, D),),
         (),
     )
+    normed, w_q_one, held, wide_z, q_parts, w_down = fence(
+        (normed, w_q_one, held, wide_z, q_parts, w_down)
+    )
+
+    wide_stack = jnp.stack(in_place(wide_z, z)).reshape(nz * both_rows, -1)
+    wide_parts = cross_fetched(wide_stack, True)
+    down_z = fetched(w_down, "z")
     w_q_two, *held = local(
         1,
-        q_twos,
-        (normed,),
+        q_parts,
+        (after(normed, wide_stack),),
         [whole(2 * frame, D)],
         (),
         (),
@@ -788,10 +842,7 @@
         factors,
         pd,
         rates,
-        gu_ones,
-        gu_twos,
-        down_part,
-        down_ends[0],
+        down_z,
     ) = fence(
         (
             normed,
@@ -803,22 +854,19 @@
             factors,
             pd,
             rates,
-            gu_ones,
-            gu_twos,
-            down_part,
-            down_ends[0],
+            down_z,
         )
     )
 
     every = all_ranges(pd.reshape(H, DK, 2 * DK))
-    gu_ones, gu_twos = gather_last(gu_ones, gu_twos)
-    every, down_ends = fence((every, down_ends))
+    down_stack = jnp.stack(in_place(down_z, z))
+    down_parts = cross_fetched(down_stack, True)
+    wide_stack = cross_stack(after(wide_parts, pd))
+    every, wide_stack = fence((every, wide_stack))
 
     states = scan_states(every)
-    down_part = after(down_part, states)
-    down_far = [down_part, down_ends[0]]
-    down_far += [turned(down_part, "z", k) for k in range(2, nz - 1)]
-    down_far += down_ends[1:]
+    down_parts = cross_fetched(cross_stack(after(down_parts, states)), False)
+    wide_parts = cross_fetched(after(wide_stack, states), False)
     states = own_range(states)
     gain_head = head_gain.astype(F32).reshape(1, DK)
     fresh, mixed, heads_mine = on_core(
@@ -830,15 +878,15 @@
         2,
     )(qkv, factors, states, gain_head)
     heads_got = swap(heads_mine)
-    gu_ones, gu_twos, down_far, states, fresh, mixed, heads_mine, heads_got = fence(
-        (gu_ones, gu_twos, down_far, states, fresh, mixed, heads_mine, heads_got)
-    )
-
-    gu_one, gu_two = (
-        a.transpose(2, 0, 1, 3, 4).reshape(D, -1) for a in gather_end(gu_ones, gu_twos)
-    )
-    w_gate, w_up = gu_one[:, : FF // 2], gu_two[:, : FF // 2]
-    out_mine = jnp.concatenate([gu_one[:, FF // 2 :], gu_two[:, FF // 2 :]], axis=1)
+    wide_parts, states, fresh, mixed, heads_mine, heads_got = fence(
+        (wide_parts, states, fresh, mixed, heads_mine, heads_got)
+    )
+
+    wide = [a.reshape(a.shape[0], nz, both_rows, -1) for a in wide_parts]
+    cuts = ((0, FF // 2), (FF // 2, FF), (FF, FF + D // 2))
+    w_gate, w_up, out_mine = (
+        cross_end([a[..., lo:hi] for a in wide]).reshape(D, hi - lo) for lo, hi in cuts
+    )
     out_got = swap(out_mine)
     full_out = jnp.concatenate(
         [jnp.where(first, out_mine, out_got), jnp.where(first, out_got, out_mine)], axis=1
@@ -853,7 +901,7 @@
     normed_two = (unit_two * gain_two).astype(BF16)
     gate = jnp.dot(normed_two, w_gate, preferred_element_type=F32)
     up = jnp.dot(normed_two, w_up, preferred_element_type=F32)
-    w_down_mine = jnp.stack(in_place(after(down_far, gate, up), z)).reshape(chips * frows, D)
+    w_down_mine = cross_end(after(down_parts, gate, up)).reshape(chips * frows, D)
     sig = jax.nn.sigmoid(gate)
     hidden = (gate * sig * up).astype(BF16)
     hidden_grad = jnp.einsum("nd,fd->nf", g_both, w_down_mine, preferred_element_type=F32)
@@ -869,12 +917,12 @@
     grad_down = jnp.einsum(
         "nf,nd->fd", after(hidden, part_low), g_both, preferred_element_type=F32
     ).astype(BF16)
-    down_stage = scatter_near(grad_down[:, : D // 2], grad_down[:, D // 2 :])
-    rows_two = after(normed_two, grad_down)
-    grad_gate = jnp.einsum("nd,nf->df", rows_two, gate_grad, preferred_element_type=F32)
-    grad_up = jnp.einsum("nd,nf->df", rows_two, up_grad, preferred_element_type=F32)
-    grad_gate, grad_up = grad_gate.astype(BF16), grad_up.astype(BF16)
-    part_got = after(part_got, grad_gate, grad_up)
+    down_stage = cross_sent(late_shares(grid_of(grad_down)), False)
+    grad_gate = jnp.einsum(
+        "nd,nf->df", after(normed_two, grad_down), gate_grad, preferred_element_type=F32
+    )
+    gate_stage = cross_sent(late_shares(grid_of(grad_gate.astype(BF16))), False)
+    part_got = after(part_got, grad_gate)
     part_got = jnp.concatenate([part_got[rows:], part_got[:rows]], axis=0)
     normed_two_grad = normed_two_part + part_got.astype(F32)
     grad_norm2 = jnp.sum(normed_two_grad[:rows] * unit_two[:rows], axis=0)
@@ -919,11 +967,7 @@
         query_grad,
         key_grad,
         gain_part,
-        down_stage,
-        grad_gate,
-        grad_up,
-        grad_norm2,
-        middle_grad,
+        up_grad,
         middle_low,
         hidden,
     ) = fence(
@@ -933,31 +977,35 @@
             query_grad,
             key_grad,
             gain_part,
-            down_stage,
-            grad_gate,
-            grad_up,
-            grad_norm2,
-            middle_grad[:rows],
+            up_grad,
             middle_low,
             hidden,
         )
     )
 
     start_grads = all_ranges(start_grad.reshape(H, DK, DK))
-    down_stage = scatter_mid(down_stage)
-    gu_stage = scatter_near(grad_gate, grad_up)
+    grad_up = jnp.einsum("nd,nf->df", normed_two, up_grad, preferred_element_type=F32)
     low_cols = lax.dynamic_slice_in_dim(middle_low, core * 512, 512, 1)
-    grad_out = jnp.einsum("nd,ne->de", heads, low_cols, preferred_element_type=F32).astype(BF16)
-    adjoints = scan_adjoints(every, start_grads)
-    gu_stage = scatter_mid(after(gu_stage, adjoints))
-    adjoints = own_range(adjoints)
-    down_part = jnp.dot(hidden, w_down_mine, preferred_element_type=F32)
+    grad_out = jnp.einsum("nd,ne->de", heads, low_cols, preferred_element_type=F32)
+    up_shares = [
+        jnp.concatenate(cut, axis=-1)
+        for cut in zip(*(late_shares(grid_of(a.astype(BF16))) for a in (grad_up, grad_out)))
+    ]
+    up_stage = cross_sent(up_shares, False)
+    adjoints = scan_adjoints(every, after(start_grads, up_shares))
+    down_shares = early_shares(after(down_stage, adjoints))
+    down_stage = cross_sent(down_shares, True)
+    gate_shares = early_shares(after(gate_stage, down_shares))
+    gate_stage = cross_sent(gate_shares, True)
+    up_shares = early_shares(after(up_stage, adjoints))
+    up_stage = cross_sent(up_shares, True)
+    down_part = jnp.dot(after(hidden, adjoints), w_down_mine, preferred_element_type=F32)
     output = (middle[:rows] + down_part[:rows]) + swap(down_part[rows:].astype(BF16)).astype(F32)
     output = output.astype(BF16).reshape(1, rows, D)
-    adjoints = after(adjoints, gu_stage[0][0], gu_stage[1][0], grad_out, output)
-    down_stage = scatter_far(after(down_stage, adjoints))
-    out_stage = scatter_first(after(grad_out, adjoints))
-    adjoints = after(adjoints, down_stage[0], out_stage[0])
+    adjoints = own_range(adjoints)
+    down_shares = shares(added(*after(down_stage, gate_shares)).astype(BF16), "z", 0)
+    down_stage = sent(down_shares, "z")
+    adjoints = after(adjoints, up_shares, down_shares, output)
     ext_grad, conv_part, logit_low, bias_part = on_core(
         fourth_kernel,
         (
@@ -984,8 +1032,8 @@
         "delta_back",
         15,
     )(qkv, pre, conv_mine, rates, inverse, factors, states, adjoints, fresh, fresh_grad, query_grad, key_grad)
-    ext_grad, conv_part, logit_low, bias_part, gu_stage, down_stage, out_stage = fence(
-        (ext_grad, conv_part, logit_low, bias_part, gu_stage, down_stage, out_stage)
+    ext_grad, conv_part, logit_low, bias_part, gate_stage, up_stage, down_stage = fence(
+        (ext_grad, conv_part, logit_low, bias_part, gate_stage, up_stage, down_stage)
     )
 
     ext_frames = ext_grad.reshape(2, 2, frame, 768)
@@ -993,13 +1041,18 @@
         jnp.einsum("nd,nf->df", normed, e, preferred_element_type=F32).astype(BF16)
         for e in (ext_grad[0], ext_grad[1])
     ]
-    q_stage = scatter_near(*grad_q)
-    ext_frames = after(ext_frames, grad_q)
+    q_shares = [
+        jnp.concatenate(cut, axis=-1) for cut in zip(*(late_shares(grid_of(g)) for g in grad_q))
+    ]
+    ext_frames, gate_stage, up_stage, q_shares = fence(
+        (ext_frames, gate_stage, up_stage, q_shares)
+    )
+    q_stage = cross_sent(q_shares, False)
     sent_back = lax.ppermute(
         ext_frames[:, :, :HALO], SEQ, [(i + 1, i) for i in range(seq_devices - 1)]
     )
-    gu_stage = scatter_far(gu_stage)
-    out_stage = scatter_second(after(out_stage, grad_q))
+    wide_part = jnp.concatenate([added(*gate_stage), added(*up_stage)], axis=-1).astype(BF16)
+    wide_stage = sent(shares(wide_part, "z", 0), "z")
     tail = ext_frames[:, :, frame - HALO :].astype(F32) + sent_back.astype(F32)
     pre_low = jnp.concatenate(
         [ext_frames[:, :, HALO : frame - HALO], tail.astype(BF16)], axis=2
@@ -1010,25 +1063,25 @@
         + jnp.einsum("pnh,pdh->nd", logit_low, beta_pairs, preferred_element_type=F32)
     )
     normed_grad = normed_part[:rows] + swap(normed_part[rows:].astype(BF16)).astype(F32)
-    normed_tokens = normed.reshape(2, frame, D)[:, HALO:].reshape(tall, D)
-    grad_beta = jnp.einsum(
-        "nd,pnh->dph", normed_tokens, logit_low[:, :, :2], preferred_element_type=F32
-    ).reshape(D, half)
-    q_stage, out_stage, normed_grad, grad_beta, x_both = fence(
-        (q_stage, out_stage, normed_grad, grad_beta, x_both)
-    )
-
-    q_stage = scatter_mid(q_stage)
-    out_stage = scatter_third(out_stage)
+    q_stage, normed_grad, normed, conv_part, logit_low, x_both = fence(
+        (q_stage, normed_grad, normed, conv_part, logit_low, x_both)
+    )
+
+    q_shares, normed_grad, x_both = fence((early_shares(q_stage), normed_grad, x_both))
+    q_stage = cross_sent(q_shares, True)
     x32 = x_both[:rows]
     scale_one = lax.rsqrt(jnp.mean(x32 * x32, axis=-1, keepdims=True) + EPS)
     unit_one = x32 * scale_one
     grad_norm1 = jnp.sum(normed_grad * unit_one, axis=0)
     inner_one = normed_grad * gain_one
-    grad_input = middle_grad + scale_one * (
+    grad_input = middle_grad[:rows] + scale_one * (
         inner_one - unit_one * jnp.mean(inner_one * unit_one, axis=-1, keepdims=True)
     )
     grad_input = grad_input.reshape(1, rows, D)
+    normed_tokens = normed.reshape(2, frame, D)[:, HALO:].reshape(tall, D)
+    grad_beta = jnp.einsum(
+        "nd,pnh->dph", normed_tokens, logit_low[:, :, :2], preferred_element_type=F32
+    ).reshape(D, half)
     beta_full = jnp.where(
         first,
         jnp.pad(grad_beta, ((0, 0), (0, half))),
@@ -1047,55 +1100,55 @@
         jnp.pad(bias_heads, ((0, 0), (half, 0))),
     )
     bias_grad = jnp.sum(choose_both[:, :, None] * bias_heads[:, None, :], axis=0)
-    head_grad = gain_part[0, 0] + gain_part[1, 0]
+    shared = jnp.concatenate([bias_grad.reshape(-1), gain_part[0, 0] + gain_part[1, 0]])
+    shared = jnp.broadcast_to(shared, (2 * chips, shared.shape[0]))
     pack = jnp.concatenate(
         [
-            grad_norm1,
-            grad_norm2,
-            beta_full.reshape(-1),
-            conv_full.reshape(-1),
-            bias_grad.reshape(-1),
-            head_grad,
-        ]
-    )
-    pack = jnp.pad(pack, (0, -pack.shape[0] % 1024)).reshape(-1, DK)
-    pack = sum_axis(pack + swap(pack), "x")
-    q_stage, gu_stage, out_stage, pack, grad_input = fence(
-        (q_stage, gu_stage, out_stage, pack, grad_input)
-    )
-
-    q_stage = scatter_far(q_stage)
-    pack = sum_axis(pack, "y")
-    gu_own = own_rows(added(*gu_stage), core)
+            grad_norm2.reshape(2 * chips, drows),
+            beta_full.reshape(2 * chips, drows * H),
+            conv_full.reshape(2 * chips, grows * CONV),
+            shared,
+        ],
+        axis=1,
+    )
+    pack = jnp.pad(pack, ((0, 0), (0, -pack.shape[1] % DK)))
+    norm_rows = jnp.pad(grad_norm1.reshape(2 * chips, drows), ((0, 0), (0, DK - drows)))
+    pack = jnp.concatenate([norm_rows, pack], axis=1).reshape(chips, 2, -1)
+    pack_own = lax.dynamic_index_in_dim(pack, core, 1, False)
+    pack_got = swap(lax.dynamic_index_in_dim(pack, 1 - core, 1, False))
+    pack = plane_shares((pack_own + pack_got).reshape(nz, ny, nx, -1))
+    q_stage, pack, grad_input, wide_stage = fence((q_stage, pack, grad_input, wide_stage))
+
+    q_shares = fence(shares(added(*q_stage).astype(BF16), "z", 0))
+    q_stage = sent(q_shares, "z")
+    pack = plane_sum(pack)
+    own_down = added(*down_stage)
+    wide_own = own_rows(added(*wide_stage), core)
     own_gu = (
-        gu_own.reshape(2, 2, drows, chips, frows).transpose(2, 1, 3, 0, 4).reshape(drows, 2 * FF)
-    )
-    own_down = added(*down_stage).transpose(1, 0, 2).reshape(frows, D)
-    out_total = jnp.concatenate([added(*s) for s in out_stage], axis=-1)
-    out_own = own_rows(out_total.reshape(1, both_rows, D // 2), core)
-    own_out = out_own.transpose(2, 0, 1, 3).reshape(drows, D)
+        wide_own[..., :FF]
+        .reshape(2, drows, 2, chips, frows)
+        .transpose(1, 2, 3, 0, 4)
+        .reshape(drows, 2 * FF)
+    )
+    own_out = wide_own[..., FF:].transpose(1, 0, 2).reshape(drows, D)
     q_stage, pack, own_gu, own_down, own_out = fence((q_stage, pack, own_gu, own_down, own_out))
 
-    pack = sum_axis(pack, "z").reshape(-1)
+    mine = z_sum(pack)
     q_own = own_rows(added(*q_stage), core)
     own_qkv = (
-        q_own.reshape(2, 2, drows, 3, 256).transpose(2, 3, 0, 1, 4).reshape(drows, 3 * D)
-    )
-    me = lax.axis_index(ALL)
-    at = 2 * D
-    own_g1 = lax.dynamic_slice_in_dim(pack[:D], me * drows, drows)
-    own_g2 = lax.dynamic_slice_in_dim(pack[D:at], me * drows, drows)
-    own_beta = lax.dynamic_slice_in_dim(
-        pack[at : at + D * H].reshape(D, H), me * drows, drows
-    )
-    at += D * H
-    own_conv = lax.dynamic_slice_in_dim(
-        pack[at : at + 3 * D * CONV].reshape(3 * D, CONV), me * grows, grows
-    )
-    at += 3 * D * CONV
-    bias_total = pack[at : at + NDOM * H].reshape(NDOM, H)
+        q_own.reshape(2, drows, 2, 3, 256).transpose(1, 3, 0, 2, 4).reshape(drows, 3 * D)
+    )
+    own_g1 = mine[:drows]
+    at = DK
+    own_g2 = mine[at : at + drows]
+    at += drows
+    own_beta = mine[at : at + drows * H].reshape(drows, H)
+    at += drows * H
+    own_conv = mine[at : at + grows * CONV].reshape(grows, CONV)
+    at += grows * CONV
+    bias_total = mine[at : at + NDOM * H].reshape(NDOM, H)
     at += NDOM * H
-    gain_total = pack[at : at + DK]
+    gain_total = mine[at : at + DK]
     return (
         output,
         grad_input,
@@ -1114,7 +1167,8 @@
 
 def solution(mesh):
     seq, batch = mesh.shape["seq"], mesh.shape["batch"]
-    fine = Mesh(mesh.devices.reshape(seq // 2, 2, batch // 2, 2), ALL)
+    plane = batch // 2
+    fine = Mesh(mesh.devices.reshape(seq // plane, plane, plane, 2), ALL)
     tokens = P(("x", "core"), ("z", "y"), None)
     rows = P(ALL, None)
     vector = P(ALL)

time: 485 us -> 430 us (0.89)
  local copies, waits for them, and re-layouts: 88.3 us -> 53.2 us
  starting transfers between devices: 106 us -> 86.8 us
    ppermute x56 -> x21, starting transfers between devices: 80.6 us -> 33.3 us  [turned(): return lax.ppermute(a, axis, [(i, (i + by) % n) for i in range(n)])]
    ppermute x56 -> x21, waiting for transfers between devices: 97 us -> 62.3 us  [turned(): return lax.ppermute(a, axis, [(i, (i + by) % n) for i in range(n)])]
    ppermute x0 -> x20, starting transfers between devices: none -> 23.1 us  [the longest x14 16 us: crossed(): return lax.ppermute(a, ('y', 'x', 'core'), pairs)]
    all_to_all x2, waiting for transfers between devices: 24.6 us -> 38.7 us  [own_range(): return lax.all_to_all(a, SEQ, 0, 0, tiled=True)]
    squeeze x17 -> x7, local copies, waits for them, and re-layouts: 16.7 us -> 4.75 us  [the longest x4 3.78 us: early_shares(): lax.dynamic_index_in_dim(total, (me + k) % n, 1, False)]
    all_to_all x2, waiting for transfers between devices: 6.11 us -> 15.9 us  [all_ranges(): return lax.all_to_all(a, SEQ, 0, 0, tiled=True)]
    unnamed x197 -> x114, local copies, waits for them, and re-layouts: 22.6 us -> 12.8 us
    ppermute x0 -> x20, waiting for transfers between devices: none -> 7.71 us  [the longest x14 7.7 us: crossed(): return lax.ppermute(a, ('y', 'x', 'core'), pairs)]
  transfers between devices with their start and end apart: 76 -> 60, of which waited for: 25 -> 15; matrix products, arithmetic and copies ran while one was open for 25% -> 29% of each run, Pallas kernels for 10% -> 12%
where the time goes in v3:
time: 430 us; the launch traced here: 422 us
  waiting for transfers between devices  125 us (29%)
  starting transfers between devices  86.8 us (20%)
  other arithmetic  64 us (15%)
  Pallas kernels  53.5 us (12%)
  local copies, waits for them, and re-layouts  53.2 us (12%)
  matrix products  35.9 us (8%)
    ppermute x21, waiting for transfers between devices, turned(): return lax.ppermute(a, axis, [(i, (i + by) % n) for i in range(n)])  62.3 us
    all_to_all x2, waiting for transfers between devices, own_range(): return lax.all_to_all(a, SEQ, 0, 0, tiled=True)  38.7 us
    ppermute x21, starting transfers between devices, turned(): return lax.ppermute(a, axis, [(i, (i + by) % n) for i in range(n)])  33.3 us
    pallas_call x2, Pallas kernels, local(): pl.pallas_call(functools.partial(first_kernel, number, len(parts)), out_s...  21.7 us
    pallas_call x1, Pallas kernels, shards(): on_core(fourth_kernel, (sds((2, 2 * frame, 768), BF16), sds((2, CONV, 768...  16.4 us
    ppermute x14, starting transfers between devices, crossed(): return lax.ppermute(a, ('y', 'x', 'core'), pairs)  16 us
    all_to_all x2, waiting for transfers between devices, all_ranges(): return lax.all_to_all(a, SEQ, 0, 0, tiled=True)  15.9 us
    unnamed x114, local copies, waits for them, and re-layouts  12.8 us
  transfers between devices with their start and end apart: 60, of which 15 were waited for; matrix products, arithmetic and copies ran while one was open for 29% of the time, Pallas kernels for 12%

profile of v3, /device:TPU:0, one launch (start us, length us, event | category | flops | bytes accessed | tf_op | source)
XLA Modules:
  0.0 421.5 jit_solution(5500438059253920576)
XLA Ops:
  4.6 4.4 %collective-permute-start.2 = (bf16[16,1024]{1,0:T(8,128)(2,1)S(1)}, bf16[16,1024]{1,0:T(8,128)(2,1)S(1)}, u32[]{:S(2)}, u32[]{:S(2)}) collective-permute-start(bf16[16,1024]{1,0:T(8,128)(2,1)S(1)} %slice_bitcast_fusion.7), channel_id=1, source_target_pairs={{0,4},{4,8},{8,12},{12,16},{16,20},{20,24},{24,28},{1,5},{5,9},{9,... | collective-permute-start | bytes 98312 | tf_op jit(solution)/shard_map/ppermute | solution.py:664
  15.6 3.6 collective-permute-start.5
  20.9 4.1 collective-permute-done.5
  25.0 13.3 %collective-permute-done.4 = bf16[72,1536]{1,0:T(8,128)(2,1)S(1)} collective-permute-done((bf16[72,1536]{1,0:T(8,128)(2,1)S(1)}, bf16[72,1536]{1,0:T(8,128)(2,1)S(1)}, u32[]{:S(2)}, u32[]{:S(2)}) %collective-permute-start.4) | collective-permute-done | bytes 221216 | tf_op jit(solution)/shard_map/ppermute | solution.py:32
  45.7 8.1 %collective-permute-done.10 = bf16[64,3328]{1,0:T(8,128)(2,1)S(1)} collective-permute-done((bf16[64,3328]{1,0:T(8,128)(2,1)S(1)}, bf16[64,3328]{1,0:T(8,128)(2,1)S(1)}, u32[]{:S(2)}, u32[]{:S(2)}) %collective-permute-start.10) | collective-permute-done | bytes 426016 | tf_op jit(solution)/shard_map/ppermute | solution.py:32
  70.2 12.7 %collective-permute-done.12 = bf16[64,3328]{1,0:T(8,128)(2,1)S(1)} collective-permute-done((bf16[64,3328]{1,0:T(8,128)(2,1)S(1)}, bf16[64,3328]{1,0:T(8,128)(2,1)S(1)}, u32[]{:S(2)}, u32[]{:S(2)}) %collective-permute-start.12) | collective-permute-done | bytes 426016 | tf_op jit(solution)/shard_map/ppermute | solution.py:32
  85.5 10.8 %delta_local.2 = (bf16[544,1024]{1,0:T(8,128)(2,1)}, bf16[4,2,2,64,768]{4,3,2,1,0:T(8,128)(2,1)}, bf16[2,544,768]{2,1,0:T(8,128)(2,1)}, bf16[2,512,768]{2,1,0:T(...) custom-call(s32[3]{0:T(128)} %pad_add_fusion.me_ref, ...), custom_call_target="tpu_custom_call" | custom-call | flops 11500000256 | tf_op jit(solution)/shard_map/delta_local/pallas_call | solution.py:785
  100.8 10.9 %delta_local.3 = (bf16[4,2,2,64,768]{4,3,2,1,0:T(8,128)(2,1)}, bf16[2,544,768]{2,1,0:T(8,128)(2,1)}, bf16[2,512,768]{2,1,0:T(8,128)(2,1)}, bf16[2,4,256,256]{3,2...) custom-call(s32[3]{0:T(128)} %pad_add_fusion.me_ref, ...), custom_call_target="tpu_custom_call", output_to_operand_aliasing={{1}: (7, {}), {2}: (8, {}), {3}: (9, {}), {4}: (10, {}), {5... | custom-call | flops 11500000256 | tf_op jit(solution)/shard_map/delta_local/pallas_call | solution.py:785
  114.9 4.1 all-to-all-start
  119.6 13.8 %all-to-all-done.pd_ref = bf16[8,128,256]{2,1,0:T(8,128)(2,1)} async-done(((bf16[8,128,256]{2,1,0:T(8,128)(2,1)}), bf16[8,128,256]{2,1,0:T(8,128)(2,1)}, u32[]{:S(2)}, u32[]{:S(2)}) %all-to-all-start) | async-done | bytes 524320 | tf_op jit(solution)/shard_map/all_to_all | solution.py:568
  139.8 4.3 %all-to-all-start.1 = ((bf16[8,128,128]{2,1,0:T(8,128)(2,1)}), bf16[8,128,128]{2,1,0:T(8,128)(2,1)}, u32[]{:S(2)}, u32[]{:S(2)}) async-start(bf16[8,128,128]{2,1,0:T(8,128)(2,1)} %state_scan.1), calls=%async_computation.1 | async-start | bytes 524288 | tf_op jit(solution)/shard_map/all_to_all | solution.py:618
  148.2 38.7 %all-to-all-done.1.s_ref = bf16[8,128,128]{2,1,0:T(8,128)(2,1)} async-done(((bf16[8,128,128]{2,1,0:T(8,128)(2,1)}), bf16[8,128,128]{2,1,0:T(8,128)(2,1)}, u32[]{:S(2)}, u32[]{:S(2)}) %all-to-all-start.1) | async-done | bytes 262176 | tf_op jit(solution)/shard_map/all_to_all | solution.py:618
  186.9 3.7 delta_mix.1
  213.8 3.7 multiply_convert_fusion
  237.7 5.9 %delta_back_local.1 = (bf16[2,4,128,128]{3,2,1,0:T(8,128)(2,1)}, f32[512,512]{1,0:T(8,128)}, f32[512,512]{1,0:T(8,128)}, f32[512,512]{1,0:T(8,128)}, f32[2,8,128]{2,1,0:T(8,128)}) custom-call(bf16[2,512,768]{2,1,0:T(8,128)(2,1)} %get-tuple-element.269.qkv_ref, bf16[2,4,256,256]{3,2,1,0:T(8,128)(2,1)} %get-tuple-element.270.wu_ref, ...), custom_call_target="tpu_custom_call" | custom-call | flops 5750000128 | tf_op jit(solution)/shard_map/delta_back_local/pallas_call | solution.py:936
  246.7 4.2 all-to-all-start.2
  250.9 3.5 convolution_convert_fusion
  266.8 4.0 all-to-all-start.3
  270.9 4.1 fusion.69
  283.4 5.8 %collective-permute-done.30 = bf16[4,88,1024]{2,1,0:T(8,128)(2,1)S(1)} collective-permute-done((bf16[4,88,1024]{2,1,0:T(8,128)(2,1)S(1)}, bf16[4,88,1024]{2,1,0:T(8,128)(2,1)S(1)}, u32[]{:S(2)}, u32[]{:S(2)}) %collective-permute-start.30) | collective-permute-done | bytes 720928 | tf_op jit(solution)/shard_map/ppermute | solution.py:91
  297.9 16.4 %delta_back.1 = (bf16[2,544,768]{2,1,0:T(8,128)(2,1)}, f32[2,4,768]{2,1,0:T(4,128)}, bf16[2,512,128]{2,1,0:T(8,128)(2,1)}, f32[2,2,128]{2,1,0:T(2,128)}) custom-call(bf16[2,512,768]{2,1,0:T(8,128)(2,1)} %get-tuple-element.269.qkv_ref, bf16[2,544,768]{2,1,0:T(8,128)(2,1)} %get-tuple-element.308.pre_ref, f32[2,4,768]{2,1,0:T(4,128)} %bitcast.418, ...), custom_call_target="tpu_custom_call" | custom-call | flops 17250000896 | tf_op jit(solution)/shard_map/delta_back/pallas_call | solution.py:1009
  340.8 4.4 %collective-permute-start.44 = (bf16[64,3328]{1,0:T(8,128)(2,1)}, bf16[64,3328]{1,0:T(8,128)(2,1)}, u32[]{:S(2)}, u32[]{:S(2)}) collective-permute-start(bf16[64,3328]{1,0:T(8,128)(2,1)} %get-tuple-element.451), channel_id=1, source_target_pairs={{0,24},{8,0},{16,8},{24,16},{1,25},{9,1},{17,9},{25,17},{2,26},{10... | collective-permute-start | bytes 1277960 | tf_op jit(solution)/shard_map/ppermute | solution.py:32
  372.4 10.4 %collective-permute-done.43 = bf16[64,3328]{1,0:T(8,128)(2,1)} collective-permute-done((bf16[64,3328]{1,0:T(8,128)(2,1)}, bf16[64,3328]{1,0:T(8,128)(2,1)}, u32[]{:S(2)}, u32[]{:S(2)}) %collective-permute-start.43) | collective-permute-done | bytes 426016 | tf_op jit(solution)/shard_map/ppermute | solution.py:32
  399.2 7.7 %collective-permute-done.46 = bf16[64,1536]{1,0:T(8,128)(2,1)S(1)} collective-permute-done((bf16[64,1536]{1,0:T(8,128)(2,1)S(1)}, bf16[64,1536]{1,0:T(8,128)(2,1)S(1)}, u32[]{:S(2)}, u32[]{:S(2)}) %collective-permute-start.46) | collective-permute-done | bytes 196640 | tf_op jit(solution)/shard_map/ppermute | solution.py:32
  (448 shorter events, 215.1 us)
Async XLA Ops:
  19.2 19.2 %collective-permute-start.4 = (bf16[72,1536]{1,0:T(8,128)(2,1)S(1)}, bf16[72,1536]{1,0:T(8,128)(2,1)S(1)}, u32[]{:S(2)}, u32[]{:S(2)}) collective-permute-start(bf16[72,1536]{1,0:T(8,128)(2,1)S(1)} %pad_maximum_fusion.27), channel_id=1, source_target_pairs={{0,16},{8,24},{16,0},{24,8},{1,17},{9,25},{17,1},{25,9},{2,18},{10... | collective-permute-start | bytes 663560 | tf_op jit(solution)/shard_map/ppermute | solution.py:32
  19.2 19.2 %collective-permute-start.3 = (bf16[72,1536]{1,0:T(8,128)(2,1)S(1)}, bf16[72,1536]{1,0:T(8,128)(2,1)S(1)}, u32[]{:S(2)}, u32[]{:S(2)}) collective-permute-start(bf16[72,1536]{1,0:T(8,128)(2,1)S(1)} %pad_maximum_fusion.27), channel_id=1, source_target_pairs={{0,8},{8,16},{16,24},{24,0},{1,9},{9,17},{17,25},{25,1},{2,10},{10... | collective-permute-start | bytes 663560 | tf_op jit(solution)/shard_map/ppermute | solution.py:32
  42.1 19.5 %collective-permute-start.15 = (bf16[4,2,768]{2,1,0:T(2,128)(2,1)S(1)}, bf16[4,2,768]{2,1,0:T(2,128)(2,1)S(1)}, u32[]{:S(2)}, u32[]{:S(2)}) collective-permute-start(bf16[4,2,768]{2,1,0:T(2,128)(2,1)S(1)} %constant_dynamic-update-slice_fusion), channel_id=1, source_target_pairs={{0,6},{2,4},{4,2},{6,0},{1,7},{3,5},{5,3},{7,1},{8,14},{10,12},{12... | collective-permute-start | bytes 36872 | tf_op jit(solution)/shard_map/ppermute | solution.py:175
  56.4 26.5 %collective-permute-start.11 = (bf16[2,4,64,1536]{3,2,1,0:T(8,128)(2,1)}, bf16[2,4,64,1536]{3,2,1,0:T(8,128)(2,1)}, u32[]{:S(2)}, u32[]{:S(2)}) collective-permute-start(bf16[2,4,64,1536]{3,2,1,0:T(8,128)(2,1)} %pad_maximum_fusion.9.refs_0_), channel_id=1, source_target_pairs={{0,4},{1,3},{2,6},{3,1},{4,0},{5,7},{6,2},{7,5},{8,12},{9,11},{10,... | collective-permute-start | bytes 4718600 | tf_op jit(solution)/shard_map/ppermute | solution.py:91
  61.9 21.0 %collective-permute-start.12 = (bf16[64,3328]{1,0:T(8,128)(2,1)S(1)}, bf16[64,3328]{1,0:T(8,128)(2,1)S(1)}, u32[]{:S(2)}, u32[]{:S(2)}) collective-permute-start(bf16[64,3328]{1,0:T(8,128)(2,1)S(1)} %pad_maximum_fusion.26), channel_id=1, source_target_pairs={{0,16},{8,24},{16,0},{24,8},{1,17},{9,25},{17,1},{25,9},{2,18},{10... | collective-permute-start | bytes 1277960 | tf_op jit(solution)/shard_map/ppermute | solution.py:32
  96.7 22.3 %collective-permute-start.20 = (bf16[256,3328]{1,0:T(8,128)(2,1)S(1)}, bf16[256,3328]{1,0:T(8,128)(2,1)S(1)}, u32[]{:S(2)}, u32[]{:S(2)}) collective-permute-start(bf16[256,3328]{1,0:T(8,128)(2,1)S(1)} %bitcast.372), channel_id=1, source_target_pairs={{0,2},{1,5},{2,0},{3,7},{4,6},{5,1},{6,4},{7,3},{8,10},{9,13},{10,... | collective-permute-start | bytes 5111816 | tf_op jit(solution)/shard_map/ppermute | solution.py:91
  114.9 18.5 %all-to-all-start = ((bf16[8,128,256]{2,1,0:T(8,128)(2,1)}), bf16[8,128,256]{2,1,0:T(8,128)(2,1)}, u32[]{:S(2)}, u32[]{:S(2)}) async-start(bf16[8,128,256]{2,1,0:T(8,128)(2,1)} %bitcast.401), calls=%async_computation | async-start | bytes 1048576 | tf_op jit(solution)/shard_map/all_to_all | solution.py:568
  136.2 58.1 %collective-permute-start.21 = (bf16[2,256,3328]{2,1,0:T(8,128)(2,1)S(1)}, bf16[2,256,3328]{2,1,0:T(8,128)(2,1)}, u32[]{:S(2)}, u32[]{:S(2)}) collective-permute-start(bf16[2,256,3328]{2,1,0:T(8,128)(2,1)S(1)} %pad_maximum_fusion), channel_id=1, source_target_pairs={{0,4},{1,3},{2,6},{3,1},{4,0},{5,7},{6,2},{7,5},{8,12},{9,11},{10,... | collective-permute-start | bytes 10223624 | tf_op jit(solution)/shard_map/ppermute | solution.py:91
  139.8 47.1 %all-to-all-start.1 = ((bf16[8,128,128]{2,1,0:T(8,128)(2,1)}), bf16[8,128,128]{2,1,0:T(8,128)(2,1)}, u32[]{:S(2)}, u32[]{:S(2)}) async-start(bf16[8,128,128]{2,1,0:T(8,128)(2,1)} %state_scan.1), calls=%async_computation.1 | async-start | bytes 524288 | tf_op jit(solution)/shard_map/all_to_all | solution.py:618
  146.3 44.9 %collective-permute-start.24 = (bf16[4,88,1024]{2,1,0:T(8,128)(2,1)}, bf16[4,88,1024]{2,1,0:T(8,128)(2,1)}, u32[]{:S(2)}, u32[]{:S(2)}) collective-permute-start(bf16[4,88,1024]{2,1,0:T(8,128)(2,1)} %pad_maximum_fusion.21), channel_id=1, source_target_pairs={{0,2},{1,5},{2,0},{3,7},{4,6},{5,1},{6,4},{7,3},{8,10},{9,13},{10,... | collective-permute-start | bytes 2162696 | tf_op jit(solution)/shard_map/ppermute | solution.py:91
  192.8 19.1 %collective-permute-start.25 = (bf16[2,4,88,1024]{3,2,0,1:T(8,128)(2,1)S(1)}, bf16[2,4,88,1024]{3,2,0,1:T(8,128)(2,1)S(1)}, u32[]{:S(2)}, u32[]{:S(2)}) collective-permute-start(bf16[2,4,88,1024]{3,2,0,1:T(8,128)(2,1)S(1)} %pad_maximum_fusion.14), channel_id=1, source_target_pairs={{0,4},{1,3},{2,6},{3,1},{4,0},{5,7},{6,2},{7,5},{8,12},{9,11},{10,... | collective-permute-start | bytes 4325384 | tf_op jit(solution)/shard_map/ppermute | solution.py:91
  226.3 51.1 %collective-permute-start.31 = (bf16[4,2,64,1408]{3,2,1,0:T(8,128)(2,1)}, bf16[4,2,64,1408]{3,2,1,0:T(8,128)(2,1)}, u32[]{:S(2)}, u32[]{:S(2)}) collective-permute-start(bf16[4,2,64,1408]{3,2,1,0:T(8,128)(2,1)} %get-tuple-element.439), channel_id=1, source_target_pairs={{0,4},{1,3},{2,6},{3,1},{4,0},{5,7},{6,2},{7,5},{8,12},{9,11},{10,... | collective-permute-start | bytes 4325384 | tf_op jit(solution)/shard_map/ppermute | solution.py:91
  229.6 45.5 %collective-permute-start.29 = (bf16[4,2,88,1024]{3,2,1,0:T(8,128)(2,1)}, bf16[4,2,88,1024]{3,2,1,0:T(8,128)(2,1)}, u32[]{:S(2)}, u32[]{:S(2)}) collective-permute-start(bf16[4,2,88,1024]{3,2,1,0:T(8,128)(2,1)} %get-tuple-element.441), channel_id=1, source_target_pairs={{0,4},{1,3},{2,6},{3,1},{4,0},{5,7},{6,2},{7,5},{8,12},{9,11},{10,... | collective-permute-start | bytes 4325384 | tf_op jit(solution)/shard_map/ppermute | solution.py:91
  257.0 37.7 %collective-permute-start.28 = (bf16[4,2,64,1920]{3,2,1,0:T(8,128)(2,1)}, bf16[4,2,64,1920]{3,2,1,0:T(8,128)(2,1)}, u32[]{:S(2)}, u32[]{:S(2)}) collective-permute-start(bf16[4,2,64,1920]{3,2,1,0:T(8,128)(2,1)} %pad_maximum_fusion.7), channel_id=1, source_target_pairs={{0,4},{1,3},{2,6},{3,1},{4,0},{5,7},{6,2},{7,5},{8,12},{9,11},{10,... | collective-permute-start | bytes 5898248 | tf_op jit(solution)/shard_map/ppermute | solution.py:91
  266.8 31.0 %all-to-all-start.3 = ((bf16[8,128,128]{2,1,0:T(8,128)(2,1)}), bf16[8,128,128]{2,1,0:T(8,128)(2,1)}, u32[]{:S(2)}, u32[]{:S(2)}) async-start(bf16[8,128,128]{2,1,0:T(8,128)(2,1)} %adjoint_scan.1), calls=%async_computation.3 | async-start | bytes 524288 | tf_op jit(solution)/shard_map/all_to_all | solution.py:618
  280.3 34.0 %collective-permute-start.32 = (bf16[4,64,1408]{2,1,0:T(8,128)(2,1)}, bf16[4,64,1408]{2,1,0:T(8,128)(2,1)}, u32[]{:S(2)}, u32[]{:S(2)}) collective-permute-start(bf16[4,64,1408]{2,1,0:T(8,128)(2,1)} %get-tuple-element.469), channel_id=1, source_target_pairs={{0,2},{1,5},{2,0},{3,7},{4,6},{5,1},{6,4},{7,3},{8,10},{9,13},{10,... | collective-permute-start | bytes 2162696 | tf_op jit(solution)/shard_map/ppermute | solution.py:91
  290.4 23.9 %collective-permute-start.36 = (bf16[88,1024]{1,0:T(8,128)(2,1)}, bf16[88,1024]{1,0:T(8,128)(2,1)S(1)}, u32[]{:S(2)}, u32[]{:S(2)}) collective-permute-start(bf16[88,1024]{1,0:T(8,128)(2,1)} %get-tuple-element.491), channel_id=1, source_target_pairs={{0,24},{8,0},{16,8},{24,16},{1,25},{9,1},{17,9},{25,17},{2,26},{10... | collective-permute-start | bytes 540680 | tf_op jit(solution)/shard_map/ppermute | solution.py:32
  293.5 20.8 %collective-permute-start.35 = (bf16[88,1024]{1,0:T(8,128)(2,1)}, bf16[88,1024]{1,0:T(8,128)(2,1)S(1)}, u32[]{:S(2)}, u32[]{:S(2)}) collective-permute-start(bf16[88,1024]{1,0:T(8,128)(2,1)} %get-tuple-element.492), channel_id=1, source_target_pairs={{0,16},{8,24},{16,0},{24,8},{1,17},{9,25},{17,1},{25,9},{2,18},{10... | collective-permute-start | bytes 540680 | tf_op jit(solution)/shard_map/ppermute | solution.py:32
  293.5 20.8 %collective-permute-start.34 = (bf16[88,1024]{1,0:T(8,128)(2,1)}, bf16[88,1024]{1,0:T(8,128)(2,1)}, u32[]{:S(2)}, u32[]{:S(2)}) collective-permute-start(bf16[88,1024]{1,0:T(8,128)(2,1)} %get-tuple-element.493), channel_id=1, source_target_pairs={{0,8},{8,16},{16,24},{24,0},{1,9},{9,17},{17,25},{25,1},{2,10},{10... | collective-permute-start | bytes 540680 | tf_op jit(solution)/shard_map/ppermute | solution.py:32
  328.8 21.6 %collective-permute-start.37 = (bf16[4,2,64,1536]{3,2,1,0:T(8,128)(2,1)}, bf16[4,2,64,1536]{3,2,1,0:T(8,128)(2,1)}, u32[]{:S(2)}, u32[]{:S(2)}) collective-permute-start(bf16[4,2,64,1536]{3,2,1,0:T(8,128)(2,1)} %pad_maximum_fusion.11), channel_id=1, source_target_pairs={{0,4},{1,3},{2,6},{3,1},{4,0},{5,7},{6,2},{7,5},{8,12},{9,11},{10,... | collective-permute-start | bytes 4718600 | tf_op jit(solution)/shard_map/ppermute | solution.py:91
  340.8 31.7 %collective-permute-start.44 = (bf16[64,3328]{1,0:T(8,128)(2,1)}, bf16[64,3328]{1,0:T(8,128)(2,1)}, u32[]{:S(2)}, u32[]{:S(2)}) collective-permute-start(bf16[64,3328]{1,0:T(8,128)(2,1)} %get-tuple-element.451), channel_id=1, source_target_pairs={{0,24},{8,0},{16,8},{24,16},{1,25},{9,1},{17,9},{25,17},{2,26},{10... | collective-permute-start | bytes 1277960 | tf_op jit(solution)/shard_map/ppermute | solution.py:32
  345.2 27.2 %collective-permute-start.42 = (bf16[64,3328]{1,0:T(8,128)(2,1)}, bf16[64,3328]{1,0:T(8,128)(2,1)}, u32[]{:S(2)}, u32[]{:S(2)}) collective-permute-start(bf16[64,3328]{1,0:T(8,128)(2,1)} %get-tuple-element.453), channel_id=1, source_target_pairs={{0,8},{8,16},{16,24},{24,0},{1,9},{9,17},{17,25},{25,1},{2,10},{10... | collective-permute-start | bytes 1277960 | tf_op jit(solution)/shard_map/ppermute | solution.py:32
  345.2 37.7 %collective-permute-start.43 = (bf16[64,3328]{1,0:T(8,128)(2,1)}, bf16[64,3328]{1,0:T(8,128)(2,1)}, u32[]{:S(2)}, u32[]{:S(2)}) collective-permute-start(bf16[64,3328]{1,0:T(8,128)(2,1)} %get-tuple-element.454), channel_id=1, source_target_pairs={{0,16},{8,24},{16,0},{24,8},{1,17},{9,25},{17,1},{25,9},{2,18},{10... | collective-permute-start | bytes 1277960 | tf_op jit(solution)/shard_map/ppermute | solution.py:32
  356.2 26.7 %collective-permute-start.40 = (bf16[4,64,1536]{2,1,0:T(8,128)(2,1)}, bf16[4,64,1536]{2,1,0:T(8,128)(2,1)}, u32[]{:S(2)}, u32[]{:S(2)}) collective-permute-start(bf16[4,64,1536]{2,1,0:T(8,128)(2,1)} %get-tuple-element.345), channel_id=1, source_target_pairs={{0,2},{1,5},{2,0},{3,7},{4,6},{5,1},{6,4},{7,3},{8,10},{9,13},{10,... | collective-permute-start | bytes 2359304 | tf_op jit(solution)/shard_map/ppermute | solution.py:91
  (89 other events, 643.4 us)
